TPU v7x, 512 devices: a whole 4x4x16 slice. The times are simulated.
512 devices in a mesh: row: 32 (over z, y_lo), col: 16 (over x, y_hi, core).
Axes of the slice: x: 4, y: 4 (y_hi: 2, y_lo: 2; y = y_hi * 2 + y_lo), z: 16, core: 2. Of those that a mesh axis runs over, the one named last changes fastest.
Arguments:
- valence: bfloat16 [512, 373248], P(('row', 'col')), may hold values from -6 to 6
- conduction: bfloat16 [512, 373248], P(('row', 'col')), may hold values from -6 to 6
- val_energy: float32 [512], replicated, may hold values from -14 to -2
- cond_energy: float32 [512], P(('row', 'col')), may hold values from 0.5 to 24
- owner: int32 [2], replicated, may hold values from 0 to 511
- g_index: int32 [8192], replicated, may hold values from 0 to 373247, as said below
Outputs:
- chi_zero: float32 [8192, 8192], P('row', 'col')
Inputs may be any that keep to these rules, and one draw needn't show every extreme that they name: `g_index`: distinct flat indices (i * 72 + j) * 72 + k. Taking each of i, j, k into -36 .. 35, each of them lies in -18 .. 17, and they are the 8192 frequency vectors of smallest squared length, listed in non-decreasing squared length; within a shell, and in the partly taken outermost shell, the choice and order come from the seed.
All inputs are finite; a program needn't handle non-finite values.
Results may differ from a plain program's by a relative error of at most 0.0038.
Values may be sent and summed in bfloat16 or wider, within the bound.
No kernel may reach another device: no remote copies, remote signals or barrier semaphores. Data moves between devices by JAX's collectives and lax.ppermute only.
A program may use at most 128 MiB of HBM per device.

v0:
```python
import math

import jax
import jax.numpy as jnp
from jax import lax
from jax.sharding import PartitionSpec as P

GRID = 72
VSTEPS = 2


def from_root(shard, axis, root):
    mine = lax.axis_index(axis) == root
    return lax.psum(jnp.where(mine, shard, jnp.zeros_like(shard)), axis)


def make_tables(size, quarter):
    inputs = jnp.arange(size, dtype=jnp.int32)
    wanted = (jnp.arange(2 * quarter, dtype=jnp.int32) - quarter) % size
    phase = inputs[:, None] * wanted[None, :] % size
    angle = phase.astype(jnp.float32) * (2.0 * math.pi / size)
    back_table = jnp.concatenate([jnp.cos(angle), -jnp.sin(angle)], axis=1)
    return (back_table.T, back_table)


def combine(mixed, width):
    real_part = mixed[0, ..., :width, :] - mixed[1, ..., width:, :]
    imag_part = mixed[0, ..., width:, :] + mixed[1, ..., :width, :]
    return jnp.stack([real_part, imag_part])


def spectrum(rho, front_table, back_table, size, width):
    highest = lax.Precision.HIGHEST
    first = jnp.dot(front_table, rho.reshape(size, size * size), precision=highest)
    first = first.reshape(2, width, size, size)
    second = jnp.einsum("wj,pmjk->pmwk", front_table, first, precision=highest)
    second = combine(second, width)
    third = jnp.dot(second.reshape(2 * width * width, size), back_table, precision=highest)
    third = third.reshape(2, width * width, 2 * width)
    real_part = third[0, :, :width] - third[1, :, width:]
    imag_part = third[0, :, width:] + third[1, :, :width]
    return jnp.stack([real_part.reshape(-1), imag_part.reshape(-1)])


def body(valence, conduction, val_energy, cond_energy, owner, g_index):
    size = GRID
    quarter = size // 4
    width = 2 * quarter
    front_table, back_table = make_tables(size, quarter)
    first_pos = (g_index // (size * size) + quarter) % size
    second_pos = (g_index // size % size + quarter) % size
    third_pos = (g_index % size + quarter) % size
    flat_at = (first_pos * width + second_pos) * width + third_pos
    bands_here = conduction.shape[0]
    nrow = lax.axis_size("row")
    ncol = lax.axis_size("col")
    total = jnp.zeros((g_index.shape[0] // nrow, g_index.shape[0] // ncol), jnp.float32)
    for step in range(VSTEPS):
        psi_v = from_root(valence, ("row", "col"), owner[step])[0]
        pair_psi_v = psi_v
        pair_psi_v = pair_psi_v.astype(jnp.float32)
        rows_out = []
        rho = pair_psi_v * conduction[0].astype(jnp.float32)
        parts = spectrum(rho, front_table, back_table, size, width)
        scale = jnp.sqrt(4.0 / (cond_energy[0] - val_energy[owner[step]])) / math.sqrt(size**3)
        picked = jnp.take(parts, flat_at, axis=1) * scale
        rows_out.append(picked[0])
        rows_out.append(picked[1])
        elems = jnp.stack(rows_out).astype(jnp.bfloat16)
        count = elems.shape[0]
        rows_side = lax.all_to_all(elems, "row", split_axis=1, concat_axis=0, tiled=True)
        cols_side = lax.all_to_all(elems, "col", split_axis=1, concat_axis=0, tiled=True)
        rows_side = rows_side.reshape(1, nrow, count, rows_side.shape[1])
        cols_side = cols_side.reshape(1, ncol, count, cols_side.shape[1])
        whole = lax.all_gather(cols_side, "row", axis=0, tiled=True)
        total = total + jnp.einsum(
            "crlg,rclh->gh",
            lax.all_gather(rows_side, "col", axis=0, tiled=True),
            whole,
            preferred_element_type=jnp.float32,
        )
    bands_all = VSTEPS * bands_here * nrow * ncol
    return -total / math.sqrt(bands_all)


def solution(mesh):
    return jax.shard_map(
        body,
        mesh=mesh,
        in_specs=(
            P(("row", "col"), None),
            P(("row", "col"), None),
            P(),
            P(("row", "col")),
            P(),
            P(),
        ),
        out_specs=P("row", "col"),
        check_vma=False,
    )
```

profile of v0, /device:TPU:2, one launch (start us, length us, event | category | flops | bytes accessed | tf_op | source)
XLA Modules:
  0.0 953.5 jit_solution(11324306015892466669)
XLA Ops:
  9.1 5.1 broadcast_select_fusion
  21.3 482.6 %all-reduce.3.cloned.1.call-done = (bf16[1,373248]{1,0:T(2,128)(2,1)}, bf16[1,373248]{1,0:T(2,128)(2,1)}) async-done(((bf16[1,373248]{1,0:T(2,128)(2,1)}, bf16[1,373248]{1,0:T(2,128)(2,1)}), (bf16[1,373248]{1,0:T(2,128)(2,1)}, bf16[1,373248]{1,0:T(2,128)(2,1)})) %all-reduce.3.cloned.1.call-update) | async-done | bytes 1493008 | tf_op jit(solution)/shard_map/psum | solution.py:14
  503.9 21.6 %multiply_reduce_fusion.1 = (f32[373248]{0:T(1024)S(1)}, f32[373248]{0:T(1024)}) fusion(bf16[1,373248]{1,0:T(2,128)(2,1)S(1)} %copy-done.1, bf16[1,373248]{1,0:T(2,128)(2,1)} %get-tuple-element.8, bf16[1,373248]{1,0:T(2,128)(2,1)} %get-tuple-element.9), kind=kLoop, calls=%fused_computation.15 | loop fusion | flops 1866240 | bytes 5225472 | tf_op jit(solution)/shard_map/mul | solution.py:63
  527.1 2.8 copy.29
  529.9 7.1 fusion.25
  537.0 2.9 fusion.6
  549.3 7.1 fusion.23
  556.4 2.9 fusion.9
  564.9 11.8 %copy.48 = f32[2,46656]{0,1:T(8,128)} copy(f32[2,46656]{1,0:T(2,128)S(1)} %pad_maximum_fusion.3) | data formatting | bytes 746496 | tf_op jit(solution)/shard_map/stack | solution.py:42
  577.0 11.9 %copy.35 = f32[2,46656]{0,1:T(8,128)} copy(f32[2,46656]{1,0:T(2,128)S(1)} %pad_maximum_fusion.2) | data formatting | bytes 746496 | tf_op jit(solution)/shard_map/stack | solution.py:42
  588.9 35.5 %gather_fusion.1 = f32[8192,2]{1,0:T(8,128)} fusion(f32[2,46656]{0,1:T(8,128)} %copy.48, s32[8192]{0:T(1024)S(1)} %broadcast_clamp_fusion), kind=kCustom, calls=%fused_computation.1.clone | custom fusion | bytes 163840 | tf_op jit(solution)/shard_map/jit(_take)/gather | solution.py:66
  624.4 35.5 %gather_fusion = f32[8192,2]{1,0:T(8,128)} fusion(f32[2,46656]{0,1:T(8,128)} %copy.35, s32[8192]{0:T(1024)S(1)} %broadcast_clamp_fusion), kind=kCustom, calls=%fused_computation.clone | custom fusion | bytes 163840 | tf_op jit(solution)/shard_map/jit(_take)/gather | solution.py:66
  659.9 7.8 fusion.1
  669.7 12.6 %all_to_all.64 = bf16[2,16,512]{2,0,1:T(2,128)(2,1)S(1)} all-to-all(bf16[2,16,512]{2,0,1:T(2,128)(2,1)S(1)} %copy.51), channel_id=1, replica_groups=mesh['row'=32,'col'=16] {'col'}, dimensions={1} | all-to-all | bytes 65536 | tf_op jit(solution)/shard_map/all_to_all | solution.py:72
  684.0 10.2 %all_to_all.65 = bf16[2,16,512]{2,0,1:T(2,128)(2,1)S(1)} all-to-all(bf16[2,16,512]{2,0,1:T(2,128)(2,1)S(1)} %copy.38), channel_id=1, replica_groups=mesh['row'=32,'col'=16] {'col'}, dimensions={1} | all-to-all | bytes 65536 | tf_op jit(solution)/shard_map/all_to_all | solution.py:72
  697.4 10.5 %all-to-all-start.2 = ((bf16[2,32,256]{2,0,1:T(2,128)(2,1)}), bf16[2,32,256]{2,0,1:T(2,128)(2,1)S(1)}, u32[]{:S(2)}, u32[]{:S(2)}) async-start(bf16[2,32,256]{2,0,1:T(2,128)(2,1)} %copy.49), calls=%async_computation.2 | async-start | bytes 65536 | tf_op jit(solution)/shard_map/all_to_all | solution.py:71
  709.4 11.8 %all-to-all-done.2 = bf16[2,32,256]{2,0,1:T(2,128)(2,1)S(1)} async-done(((bf16[2,32,256]{2,0,1:T(2,128)(2,1)}), bf16[2,32,256]{2,0,1:T(2,128)(2,1)S(1)}, u32[]{:S(2)}, u32[]{:S(2)}) %all-to-all-start.2) | async-done | bytes 32800 | tf_op jit(solution)/shard_map/all_to_all | solution.py:71
  721.2 3.8 all-to-all-start
  725.0 13.5 %all-to-all-done = bf16[2,32,256]{2,0,1:T(2,128)(2,1)S(1)} async-done(((bf16[2,32,256]{2,0,1:T(2,128)(2,1)}), bf16[2,32,256]{2,0,1:T(2,128)(2,1)S(1)}, u32[]{:S(2)}, u32[]{:S(2)}) %all-to-all-start) | async-done | bytes 32800 | tf_op jit(solution)/shard_map/all_to_all | solution.py:71
  738.5 21.6 %all-gather = bf16[512,2,256]{2,0,1:T(8,128)(2,1)S(1)} all-gather(bf16[32,2,256]{2,0,1:T(8,128)(2,1)S(1)} %bitcast.94), channel_id=2, replica_groups=mesh['row'=32,'col'=16] {'col'}, dimensions={0}, use_global_device_ids=true | all-gather | bytes 557056 | tf_op jit(solution)/shard_map/all_gather | solution.py:78
  760.1 22.8 %all-gather.2 = bf16[512,2,256]{2,0,1:T(8,128)(2,1)S(1)} all-gather(bf16[32,2,256]{2,0,1:T(8,128)(2,1)S(1)} %bitcast.93), channel_id=4, replica_groups=mesh['row'=32,'col'=16] {'col'}, dimensions={0}, use_global_device_ids=true | all-gather | bytes 557056 | tf_op jit(solution)/shard_map/all_gather | solution.py:78
  782.9 28.1 %all-gather.9.cloned.1.call-done = bf16[512,2,512]{2,0,1:T(8,128)(2,1)} async-done(((bf16[16,2,512]{2,0,1:T(8,128)(2,1)}), bf16[512,2,512]{2,0,1:T(8,128)(2,1)}) %all-gather.9.cloned.1.call-update) | async-done | bytes 1048592 | tf_op jit(solution)/shard_map/all_gather | solution.py:75
  813.6 129.6 %all-gather.7.cloned.1.call-done = bf16[512,2,512]{2,0,1:T(8,128)(2,1)} async-done(((bf16[16,2,512]{2,0,1:T(8,128)(2,1)}), bf16[512,2,512]{2,0,1:T(8,128)(2,1)}) %all-gather.7.cloned.1.call-update) | async-done | bytes 1048592 | tf_op jit(solution)/shard_map/all_gather | solution.py:75
  943.2 3.4 fusion.18
  (54 shorter events, 30.1 us)
Async XLA Ops:
  6.5 497.3 %all-reduce.3.cloned.1.call-start = ((), (), s32[]{:S(2)}) async-start(), calls=%async_computation.6 | async-start | bytes 5971968 | tf_op jit(solution)/shard_map/psum | solution.py:14
  14.2 4.7 copy-start.3
  14.2 6.9 copy-start.2
  14.2 489.6 %copy-start.1 = (bf16[1,373248]{1,0:T(2,128)(2,1)S(1)}, bf16[1,373248]{1,0:T(2,128)(2,1)}, u32[]{:S(2)}) copy-start(bf16[1,373248]{1,0:T(2,128)(2,1)} %param.9) | copy-start | bytes 2239492
  14.2 796.8 %all-gather.9.cloned.1.call-start = ((), (), s32[]{:S(2)}) async-start(), calls=%async_computation.5 | async-start | bytes 1081344 | tf_op jit(solution)/shard_map/all_gather | solution.py:75
  542.8 2.1 copy-start
  683.0 260.2 %all-gather.7.cloned.1.call-start = ((), (), s32[]{:S(2)}) async-start(), calls=%async_computation.4 | async-start | bytes 1081344 | tf_op jit(solution)/shard_map/all_gather | solution.py:75
  697.4 23.8 %all-to-all-start.2 = ((bf16[2,32,256]{2,0,1:T(2,128)(2,1)}), bf16[2,32,256]{2,0,1:T(2,128)(2,1)S(1)}, u32[]{:S(2)}, u32[]{:S(2)}) async-start(bf16[2,32,256]{2,0,1:T(2,128)(2,1)} %copy.49), calls=%async_computation.2 | async-start | bytes 65536 | tf_op jit(solution)/shard_map/all_to_all | solution.py:71
  721.2 17.3 %all-to-all-start = ((bf16[2,32,256]{2,0,1:T(2,128)(2,1)}), bf16[2,32,256]{2,0,1:T(2,128)(2,1)S(1)}, u32[]{:S(2)}, u32[]{:S(2)}) async-start(bf16[2,32,256]{2,0,1:T(2,128)(2,1)} %copy.36), calls=%async_computation | async-start | bytes 65536 | tf_op jit(solution)/shard_map/all_to_all | solution.py:71
Sparse Core Ops, SparseCore 0:
  14.4 489.4 all-reduce.2
  683.1 127.8 all-gather.8
  813.3 129.8 all-gather.6
where the time goes:
time: 961 us; the launch traced here: 954 us
  waiting for transfers between devices  666 us (69%)
  local copies, waits for them, and re-layouts  120 us (12%)
  blocking collectives  67.2 us (7%)
  other arithmetic  36.5 us (4%)
  matrix products  29.1 us (3%)
  between operations  21.1 us (2%)
  starting transfers between devices  14.3 us (1%)
    psum x1, waiting for transfers between devices, from_root(): return lax.psum(jnp.where(mine, shard, jnp.zeros_like(shard)), axis)  483 us
    all_gather x2, waiting for transfers between devices, body(): whole = lax.all_gather(cols_side, 'row', axis=0, tiled=True)  158 us
    gather x2, local copies, waits for them, and re-layouts, body(): picked = jnp.take(parts, flat_at, axis=1) * scale  71 us
    all_gather x2, blocking collectives, body(): lax.all_gather(rows_side, 'col', axis=0, tiled=True)  44.4 us
    all_to_all x2, waiting for transfers between devices, body(): lax.all_to_all(elems, 'row', split_axis=1, concat_axis=0, tiled=True)  25.3 us
    another operation x2, local copies, waits for them, and re-layouts, spectrum(): return jnp.stack([real_part.reshape(-1), imag_part.reshape(-1)])  23.7 us
    all_to_all x2, blocking collectives, body(): lax.all_to_all(elems, 'col', split_axis=1, concat_axis=0, tiled=True)  22.8 us
    mul x1, other arithmetic, body(): rho = pair_psi_v * conduction[0].astype(jnp.float32)  21.6 us
  transfers between devices with their start and end apart: 5, of which 5 were waited for; matrix products, arithmetic and copies ran while one was open for 1% of the time, Pallas kernels for 0%

commit v1 on v0

--- a/solution.py
+++ b/solution.py
@@ -3,15 +3,43 @@
 import jax
 import jax.numpy as jnp
 from jax import lax
-from jax.sharding import PartitionSpec as P
+from jax.sharding import Mesh, PartitionSpec as P
 
 GRID = 72
 VSTEPS = 2
+AXES = ("z", "yl", "x", "yh", "c")
+SIZES = (16, 2, 4, 2, 2)
+ROW = ("z", "yl")
+COL = ("x", "yh", "c")
+PLANE = ("yl", "x", "yh", "c")
+TILE = ("yl", "x", "yh")
+LANES = 128
+PIECE = 6
+CHUNK = 16 * PIECE
 
 
-def from_root(shard, axis, root):
-    mine = lax.axis_index(axis) == root
-    return lax.psum(jnp.where(mine, shard, jnp.zeros_like(shard)), axis)
+def exchange(x, axis):
+    return lax.all_to_all(x, axis, split_axis=0, concat_axis=0, tiled=True)
+
+
+def from_owners(shard, owner):
+    size = shard.shape[1]
+    steps = owner.shape[0]
+    owner_z, owner_plane = owner // 32, owner % 32
+    flat = jnp.pad(shard.reshape(size // LANES, LANES), ((0, 32 * CHUNK - size // LANES), (0, 0)))
+    parts = exchange(flat.reshape(32, CHUNK, LANES), PLANE)
+    parts = jnp.stack([lax.dynamic_index_in_dim(parts, owner_plane[s], 0, False) for s in range(steps)])
+    parts = parts.reshape(steps, 16, PIECE, LANES).transpose(1, 0, 2, 3)
+    parts = exchange(parts, "z")
+    parts = jnp.stack([lax.dynamic_index_in_dim(parts[:, s], owner_z[s], 0, False) for s in range(steps)])
+    parts = exchange(jnp.broadcast_to(parts[None], (16,) + parts.shape), "z")
+    parts = parts.transpose(1, 0, 2, 3).reshape(steps * CHUNK, LANES)
+    parts = exchange(jnp.broadcast_to(parts[None], (16,) + parts.shape), TILE)
+    other = lax.ppermute(parts, "c", [(0, 1), (1, 0)])
+    first = lax.axis_index("c") == 0
+    both = jnp.stack([jnp.where(first, parts, other), jnp.where(first, other, parts)], axis=1)
+    both = both.reshape(32, steps, CHUNK, LANES).transpose(1, 0, 2, 3)
+    return both.reshape(steps, 32 * CHUNK, LANES)
 
 
 def make_tables(size, quarter):
@@ -52,11 +80,12 @@
     third_pos = (g_index % size + quarter) % size
     flat_at = (first_pos * width + second_pos) * width + third_pos
     bands_here = conduction.shape[0]
-    nrow = lax.axis_size("row")
-    ncol = lax.axis_size("col")
+    nrow = lax.axis_size(ROW)
+    ncol = lax.axis_size(COL)
+    psi = from_owners(valence, owner)[:, : size**3 // LANES]
     total = jnp.zeros((g_index.shape[0] // nrow, g_index.shape[0] // ncol), jnp.float32)
     for step in range(VSTEPS):
-        psi_v = from_root(valence, ("row", "col"), owner[step])[0]
+        psi_v = psi[step].reshape(-1)
         pair_psi_v = psi_v
         pair_psi_v = pair_psi_v.astype(jnp.float32)
         rows_out = []
@@ -68,14 +97,14 @@
         rows_out.append(picked[1])
         elems = jnp.stack(rows_out).astype(jnp.bfloat16)
         count = elems.shape[0]
-        rows_side = lax.all_to_all(elems, "row", split_axis=1, concat_axis=0, tiled=True)
-        cols_side = lax.all_to_all(elems, "col", split_axis=1, concat_axis=0, tiled=True)
+        rows_side = lax.all_to_all(elems, ROW, split_axis=1, concat_axis=0, tiled=True)
+        cols_side = lax.all_to_all(elems, COL, split_axis=1, concat_axis=0, tiled=True)
         rows_side = rows_side.reshape(1, nrow, count, rows_side.shape[1])
         cols_side = cols_side.reshape(1, ncol, count, cols_side.shape[1])
-        whole = lax.all_gather(cols_side, "row", axis=0, tiled=True)
+        whole = lax.all_gather(cols_side, ROW, axis=0, tiled=True)
         total = total + jnp.einsum(
             "crlg,rclh->gh",
-            lax.all_gather(rows_side, "col", axis=0, tiled=True),
+            lax.all_gather(rows_side, COL, axis=0, tiled=True),
             whole,
             preferred_element_type=jnp.float32,
         )
@@ -84,17 +113,11 @@
 
 
 def solution(mesh):
+    every = P(AXES)
     return jax.shard_map(
         body,
-        mesh=mesh,
-        in_specs=(
-            P(("row", "col"), None),
-            P(("row", "col"), None),
-            P(),
-            P(("row", "col")),
-            P(),
-            P(),
-        ),
-        out_specs=P("row", "col"),
+        mesh=Mesh(mesh.devices.reshape(SIZES), AXES),
+        in_specs=(P(AXES, None), P(AXES, None), P(), every, P(), P()),
+        out_specs=P(ROW, COL),
         check_vma=False,
     )

time: 961 us -> 558 us (0.58)
  waiting for transfers between devices: 666 us -> 200 us
  starting transfers between devices: 14.3 us -> 37.9 us
  blocking collectives: 67.2 us -> 83.4 us
    psum x1 -> x0, waiting for transfers between devices: 483 us -> none  [from_root(): return lax.psum(jnp.where(mine, shard, jnp.zeros_like(shard)), axis)]
    mul x1 -> x0, other arithmetic: 21.6 us -> none  [body(): rho = pair_psi_v * conduction[0].astype(jnp.float32)]
    all_to_all x2 -> x5, starting transfers between devices: 14.3 us -> 35.7 us  [the longest x3 28 us: exchange(): return lax.all_to_all(x, axis, split_axis=0, concat_axis=0, tiled=True)]
    all_to_all x2 -> x5, waiting for transfers between devices: 25.3 us -> 43.2 us  [the longest x2 25.2 us: body(): lax.all_to_all(elems, ROW, split_axis=1, concat_axis=0, tiled=True)]
    unnamed x0 -> x1, other arithmetic: none -> 16.5 us
    all_to_all x2 -> x3, blocking collectives: 22.8 us -> 39.2 us  [the longest x2 23.6 us: body(): lax.all_to_all(elems, COL, split_axis=1, concat_axis=0, tiled=True)]
    convert_element_type x0 -> x2, other arithmetic: none -> 14.2 us  [the longest x1 12.4 us: body(): rho = pair_psi_v * conduction[0].astype(jnp.float32)]
  transfers between devices with their start and end apart: 5 -> 8, of which waited for: 5 -> 6; matrix products, arithmetic and copies ran while one was open for 1% -> 4% of each run, Pallas kernels for 0% -> 0%
where the time goes in v1:
time: 558 us; the launch traced here: 548 us
  waiting for transfers between devices  200 us (36%)
  local copies, waits for them, and re-layouts  124 us (22%)
  blocking collectives  83.4 us (15%)
  other arithmetic  45.5 us (8%)
  starting transfers between devices  37.9 us (7%)
  matrix products  29.1 us (5%)
  between operations  27.9 us (5%)
    all_gather x2, waiting for transfers between devices, body(): whole = lax.all_gather(cols_side, ROW, axis=0, tiled=True)  157 us
    gather x2, local copies, waits for them, and re-layouts, body(): picked = jnp.take(parts, flat_at, axis=1) * scale  71 us
    all_gather x2, blocking collectives, body(): lax.all_gather(rows_side, COL, axis=0, tiled=True)  44.1 us
    all_to_all x3, starting transfers between devices, exchange(): return lax.all_to_all(x, axis, split_axis=0, concat_axis=0, tiled=True)  28 us
    all_to_all x2, waiting for transfers between devices, body(): lax.all_to_all(elems, ROW, split_axis=1, concat_axis=0, tiled=True)  25.2 us
    another operation x2, local copies, waits for them, and re-layouts, spectrum(): return jnp.stack([real_part.reshape(-1), imag_part.reshape(-1)])  23.7 us
    all_to_all x2, blocking collectives, body(): lax.all_to_all(elems, COL, split_axis=1, concat_axis=0, tiled=True)  23.6 us
    all_to_all x3, waiting for transfers between devices, exchange(): return lax.all_to_all(x, axis, split_axis=0, concat_axis=0, tiled=True)  17.9 us
  transfers between devices with their start and end apart: 8, of which 6 were waited for; matrix products, arithmetic and copies ran while one was open for 4% of the time, Pallas kernels for 0%

profile of v1, /device:TPU:2, one launch (start us, length us, event | category | flops | bytes accessed | tf_op | source)
XLA Modules:
  0.0 548.1 jit_solution(10057166755807860101)
XLA Ops:
  6.5 16.5 %reduce = bf16[373248]{0:T(1024)(128)(2,1)S(1)} reduce(bf16[1,373248]{1,0:T(2,128)(2,1)} %param.8, bf16[]{:T(256)} %constant.136), dimensions={0}, to_apply=%param.8.reduce_sub_computation | reduce | bytes 1492994 | tf_op args[0]
  24.0 9.5 %all-to-all-start = ((bf16[32,96,128]{2,1,0:T(8,128)(2,1)}), bf16[32,96,128]{2,1,0:T(8,128)(2,1)S(1)}, u32[]{:S(2)}, u32[]{:S(2)}) async-start(bf16[32,96,128]{2,1,0:T(8,128)(2,1)} %bitcast.2), calls=%async_computation | async-start | bytes 1572864 | tf_op jit(solution)/shard_map/all_to_all | solution.py:22
  38.1 9.0 %all-to-all-done = bf16[32,96,128]{2,1,0:T(8,128)(2,1)S(1)} async-done(((bf16[32,96,128]{2,1,0:T(8,128)(2,1)}), bf16[32,96,128]{2,1,0:T(8,128)(2,1)S(1)}, u32[]{:S(2)}, u32[]{:S(2)}) %all-to-all-start) | async-done | bytes 786464 | tf_op jit(solution)/shard_map/all_to_all | solution.py:22
  47.8 13.3 %all-to-all-start.1 = ((bf16[16,2,6,128]{3,1,2,0:T(2,128)(2,1)}), bf16[16,2,6,128]{3,1,2,0:T(2,128)(2,1)S(1)}, u32[]{:S(2)}, u32[]{:S(2)}) async-start(bf16[16,2,6,128]{3,1,2,0:T(2,128)(2,1)} %bitcast.6), calls=%async_computation.1 | async-start | bytes 98304 | tf_op jit(solution)/shard_map/all_to_all | solution.py:22
  64.9 8.9 %all-to-all-done.1 = bf16[16,2,6,128]{3,1,2,0:T(2,128)(2,1)S(1)} async-done(((bf16[16,2,6,128]{3,1,2,0:T(2,128)(2,1)}), bf16[16,2,6,128]{3,1,2,0:T(2,128)(2,1)S(1)}, u32[]{:S(2)}, u32[]{:S(2)}) %all-to-all-start.1) | async-done | bytes 49184 | tf_op jit(solution)/shard_map/all_to_all | solution.py:22
  74.0 15.7 %all_to_all.84 = bf16[16,2,6,128]{3,1,2,0:T(2,128)(2,1)S(1)} all-to-all(bf16[16,2,6,128]{3,1,2,0:T(2,128)(2,1)S(1)} %broadcast_in_dim.24), channel_id=1, replica_groups=mesh['z'=16,'yl'=2,'x'=4,'yh'=2,'c'=2] {'z'}, dimensions={0} | all-to-all | bytes 98304 | tf_op jit(solution)/shard_map/all_to_all | solution.py:22
  90.8 5.2 all-to-all-start.3
  99.2 12.4 %convert_reduce_fusion = f32[373248]{0:T(1024)S(1)} fusion(bf16[1,373248]{1,0:T(2,128)(2,1)S(1)} %copy-done), kind=kLoop, calls=%fused_computation.15 | loop fusion | flops 373248 | bytes 2239488 | tf_op jit(solution)/shard_map/convert_element_type | solution.py:92
  132.6 7.1 %fusion.23 = f32[2,36,72,72]{3,1,2,0:T(8,128)S(1)} fusion(f32[72,72,72,1]{2,1,0,3:T(8,128)S(1)} %bitcast.114, f32[2,36,72,1]{2,1,0,3:T(8,128)S(1)} %reshape.210), kind=kOutput, calls=%fused_computation.54 | convolution fusion | flops 322486272 | bytes 3006720 | tf_op jit(solution)/shard_map/dot_general | solution.py:62
  148.1 11.8 %copy.81 = f32[2,46656]{0,1:T(8,128)} copy(f32[2,46656]{1,0:T(2,128)S(1)} %pad_maximum_fusion.4) | data formatting | bytes 746496 | tf_op jit(solution)/shard_map/stack | solution.py:70
  162.5 7.1 %fusion.25 = f32[2,36,72,72]{3,1,2,0:T(8,128)S(1)} fusion(f32[72,72,72,1]{2,1,0,3:T(8,128)S(1)} %bitcast.113, f32[2,36,72,1]{2,1,0,3:T(8,128)S(1)} %reshape.210), kind=kOutput, calls=%fused_computation.56 | convolution fusion | flops 322486272 | bytes 3006720 | tf_op jit(solution)/shard_map/dot_general | solution.py:62
  178.1 11.9 %copy.68 = f32[2,46656]{0,1:T(8,128)} copy(f32[2,46656]{1,0:T(2,128)S(1)} %pad_maximum_fusion.3) | data formatting | bytes 746496 | tf_op jit(solution)/shard_map/stack | solution.py:70
  190.0 35.5 %gather_fusion.1 = f32[8192,2]{1,0:T(8,128)} fusion(f32[2,46656]{0,1:T(8,128)} %copy.81, s32[8192]{0:T(1024)S(1)} %broadcast_clamp_fusion), kind=kCustom, calls=%fused_computation.1.clone | custom fusion | bytes 163840 | tf_op jit(solution)/shard_map/jit(_take)/gather | solution.py:95
  225.5 35.5 %gather_fusion = f32[8192,2]{1,0:T(8,128)} fusion(f32[2,46656]{0,1:T(8,128)} %copy.68, s32[8192]{0:T(1024)S(1)} %broadcast_clamp_fusion), kind=kCustom, calls=%fused_computation.clone | custom fusion | bytes 163840 | tf_op jit(solution)/shard_map/jit(_take)/gather | solution.py:95
  261.0 7.8 %fusion.1 = (bf16[2,8192]{0,1:T(8,128)(2,1)S(1)}, bf16[2,8192]{0,1:T(8,128)(2,1)}) fusion(f32[8192,2]{1,0:T(8,128)} %gather_fusion, f32[]{:T(128)} %bitcast.26, pred[8192]{0:T(1024)(128)(4,1)S(1)} %get-tuple-element.6, f32[]{:T(128)} %bitcast.43, f32[8192,2]{1,0:T(8,128)} %gather_fusion.1), kind=kLoop, calls=%fused_computation.5 | loop fusion | flops 98304 | bytes 204808 | tf_op jit(solution)/shard_map/convert_element_type | solution.py:98
  270.8 13.4 %all_to_all.85 = bf16[2,16,512]{2,0,1:T(2,128)(2,1)S(1)} all-to-all(bf16[2,16,512]{2,0,1:T(2,128)(2,1)S(1)} %copy.84), channel_id=1, replica_groups=mesh['z'=16,'yl'=2,'x'=4,'yh'=2,'c'=2] {'x','yh','c'}, dimensions={1} | all-to-all | bytes 65536 | tf_op jit(solution)/shard_map/all_to_all | solution.py:101
  285.8 10.2 %all_to_all.86 = bf16[2,16,512]{2,0,1:T(2,128)(2,1)S(1)} all-to-all(bf16[2,16,512]{2,0,1:T(2,128)(2,1)S(1)} %copy.71), channel_id=1, replica_groups=mesh['z'=16,'yl'=2,'x'=4,'yh'=2,'c'=2] {'x','yh','c'}, dimensions={1} | all-to-all | bytes 65536 | tf_op jit(solution)/shard_map/all_to_all | solution.py:101
  299.2 3.9 all-to-all-start.6
  304.6 12.1 %all-to-all-done.6 = bf16[2,32,256]{2,0,1:T(2,128)(2,1)S(1)} async-done(((bf16[2,32,256]{2,0,1:T(2,128)(2,1)}), bf16[2,32,256]{2,0,1:T(2,128)(2,1)S(1)}, u32[]{:S(2)}, u32[]{:S(2)}) %all-to-all-start.6) | async-done | bytes 32800 | tf_op jit(solution)/shard_map/all_to_all | solution.py:100
  320.6 13.1 %all-to-all-done.4 = bf16[2,32,256]{2,0,1:T(2,128)(2,1)S(1)} async-done(((bf16[2,32,256]{2,0,1:T(2,128)(2,1)}), bf16[2,32,256]{2,0,1:T(2,128)(2,1)S(1)}, u32[]{:S(2)}, u32[]{:S(2)}) %all-to-all-start.4) | async-done | bytes 32800 | tf_op jit(solution)/shard_map/all_to_all | solution.py:100
  333.7 21.0 %all-gather.2 = bf16[512,2,256]{2,0,1:T(8,128)(2,1)S(1)} all-gather(bf16[32,2,256]{2,0,1:T(8,128)(2,1)S(1)} %bitcast.123), channel_id=4, replica_groups=mesh['z'=16,'yl'=2,'x'=4,'yh'=2,'c'=2] {'x','yh','c'}, dimensions={0}, use_global_device_ids=true | all-gather | bytes 557056 | tf_op jit(solution)/shard_map/all_gather | solution.py:107
  354.7 23.2 %all-gather = bf16[512,2,256]{2,0,1:T(8,128)(2,1)S(1)} all-gather(bf16[32,2,256]{2,0,1:T(8,128)(2,1)S(1)} %bitcast.124), channel_id=2, replica_groups=mesh['z'=16,'yl'=2,'x'=4,'yh'=2,'c'=2] {'x','yh','c'}, dimensions={0}, use_global_device_ids=true | all-gather | bytes 557056 | tf_op jit(solution)/shard_map/all_gather | solution.py:107
  377.9 28.1 %all-gather.9.cloned.1.call-done = bf16[512,2,512]{2,0,1:T(8,128)(2,1)} async-done(((bf16[16,2,512]{2,0,1:T(8,128)(2,1)}), bf16[512,2,512]{2,0,1:T(8,128)(2,1)}) %all-gather.9.cloned.1.call-update) | async-done | bytes 1048592 | tf_op jit(solution)/shard_map/all_gather | solution.py:104
  408.5 129.0 %all-gather.7.cloned.1.call-done = bf16[512,2,512]{2,0,1:T(8,128)(2,1)} async-done(((bf16[16,2,512]{2,0,1:T(8,128)(2,1)}), bf16[512,2,512]{2,0,1:T(8,128)(2,1)}) %all-gather.7.cloned.1.call-update) | async-done | bytes 1048592 | tf_op jit(solution)/shard_map/all_gather | solution.py:104
  (83 shorter events, 59.1 us)
Async XLA Ops:
  23.0 10.5 %copy-start.2 = (s32[2]{0:T(128)S(1)}, s32[2]{0:T(128)}, u32[]{:S(2)}) copy-start(s32[2]{0:T(128)} %param.12) | copy-start | bytes 28
  24.0 23.1 %all-to-all-start = ((bf16[32,96,128]{2,1,0:T(8,128)(2,1)}), bf16[32,96,128]{2,1,0:T(8,128)(2,1)S(1)}, u32[]{:S(2)}, u32[]{:S(2)}) async-start(bf16[32,96,128]{2,1,0:T(8,128)(2,1)} %bitcast.2), calls=%async_computation | async-start | bytes 1572864 | tf_op jit(solution)/shard_map/all_to_all | solution.py:22
  33.5 65.7 %copy-start = (bf16[1,373248]{1,0:T(2,128)(2,1)S(1)}, bf16[1,373248]{1,0:T(2,128)(2,1)}, u32[]{:S(2)}) copy-start(bf16[1,373248]{1,0:T(2,128)(2,1)} %param.9) | copy-start | bytes 2239492
  47.8 26.0 %all-to-all-start.1 = ((bf16[16,2,6,128]{3,1,2,0:T(2,128)(2,1)}), bf16[16,2,6,128]{3,1,2,0:T(2,128)(2,1)S(1)}, u32[]{:S(2)}, u32[]{:S(2)}) async-start(bf16[16,2,6,128]{3,1,2,0:T(2,128)(2,1)} %bitcast.6), calls=%async_computation.1 | async-start | bytes 98304 | tf_op jit(solution)/shard_map/all_to_all | solution.py:22
  90.8 21.3 %all-to-all-start.3 = ((bf16[16,192,128]{2,1,0:T(8,128)(2,1)}), bf16[16,192,128]{2,1,0:T(8,128)(2,1)}, u32[]{:S(2)}, u32[]{:S(2)}) async-start(bf16[16,192,128]{2,1,0:T(8,128)(2,1)} %broadcast_in_dim.26), calls=%async_computation.3 | async-start | bytes 1572864 | tf_op jit(solution)/shard_map/all_to_all | solution.py:22
  96.0 309.9 %all-gather.9.cloned.1.call-start = ((), (), s32[]{:S(2)}) async-start(), calls=%async_computation.9 | async-start | bytes 1081344 | tf_op jit(solution)/shard_map/all_gather | solution.py:104
  111.6 4.7 copy-start.3
  111.6 6.8 %copy-start.1 = (s32[8192]{0:T(1024)S(1)}, s32[8192]{0:T(1024)}, u32[]{:S(2)}) copy-start(s32[8192]{0:T(1024)} %param.13) | copy-start | bytes 98308
  112.1 6.5 %collective-permute-start = (bf16[16,192,128]{2,1,0:T(8,128)(2,1)}, bf16[16,192,128]{2,1,0:T(8,128)(2,1)S(1)}, u32[]{:S(2)}, u32[]{:S(2)}) collective-permute-start(bf16[16,192,128]{2,1,0:T(8,128)(2,1)} %all-to-all-done.3), channel_id=1, source_target_pairs={{0,1},{1,0},{2,3},{3,2},{4,5},{5,4},{6,7},{7,6},{8,9},{9,8},{10,11... | collective-permute-start | bytes 2359304 | tf_op jit(solution)/shard_map/ppermute | solution.py:38
  284.8 252.6 %all-gather.7.cloned.1.call-start = ((), (), s32[]{:S(2)}) async-start(), calls=%async_computation.8 | async-start | bytes 1081344 | tf_op jit(solution)/shard_map/all_gather | solution.py:104
  299.2 17.5 %all-to-all-start.6 = ((bf16[2,32,256]{2,0,1:T(2,128)(2,1)}), bf16[2,32,256]{2,0,1:T(2,128)(2,1)S(1)}, u32[]{:S(2)}, u32[]{:S(2)}) async-start(bf16[2,32,256]{2,0,1:T(2,128)(2,1)} %copy.82), calls=%async_computation.6 | async-start | bytes 65536 | tf_op jit(solution)/shard_map/all_to_all | solution.py:100
  316.7 17.0 %all-to-all-start.4 = ((bf16[2,32,256]{2,0,1:T(2,128)(2,1)}), bf16[2,32,256]{2,0,1:T(2,128)(2,1)S(1)}, u32[]{:S(2)}, u32[]{:S(2)}) async-start(bf16[2,32,256]{2,0,1:T(2,128)(2,1)} %copy.69), calls=%async_computation.4 | async-start | bytes 65536 | tf_op jit(solution)/shard_map/all_to_all | solution.py:100
Sparse Core Ops, SparseCore 0:
  285.0 120.9 all-gather.8
  408.0 129.4 all-gather.6

commit v2 on v1

v2 whole, which is shorter than its diff:
```python
import math

import jax
import jax.numpy as jnp
import ml_dtypes
import numpy as np
from jax import lax
from jax.experimental import pallas as pl
from jax.experimental.pallas import tpu as pltpu
from jax.sharding import Mesh, PartitionSpec as P

GRID = 72
STEPS = 2
AXES = ("z", "yl", "x", "yh", "c")
SIZES = (16, 2, 4, 2, 2)
ROW = ("z", "yl")
COL = ("x", "yh", "c")
PLANE = ("yl", "x", "yh", "c")
TILE = ("yl", "x", "yh")
QUAD = ("x", "yh")
LANES = 128
PIECE = 6
CHUNK = 16 * PIECE
SWAP = [(0, 1), (1, 0)]
REACH=12
KEPT=2*REACH+1
HALF=GRID//2
PAIR=GRID*GRID*2//LANES
ROWS=GRID**3//LANES
WIDE=16
BACK=32
SLOT=64
PAD_ROWS=40*PAIR


def exchange(x, axis):
    return lax.all_to_all(x, axis, split_axis=0, concat_axis=0, tiled=True)


def from_owners(shard, owner):
    size = shard.shape[1]
    steps = owner.shape[0]
    owner_z, owner_plane = owner // 32, owner % 32
    flat = jnp.pad(shard.reshape(size // LANES, LANES), ((0, 32 * CHUNK - size // LANES), (0, 0)))
    parts = exchange(flat.reshape(32, CHUNK, LANES), PLANE)
    parts = jnp.stack([lax.dynamic_index_in_dim(parts, owner_plane[s], 0, False) for s in range(steps)])
    parts = parts.reshape(steps, 16, PIECE, LANES).transpose(1, 0, 2, 3)
    parts = exchange(parts, "z")
    parts = jnp.stack([lax.dynamic_index_in_dim(parts[:, s], owner_z[s], 0, False) for s in range(steps)])
    parts = exchange(jnp.broadcast_to(parts[None], (16,) + parts.shape), "z")
    parts = parts.transpose(1, 0, 2, 3).reshape(steps * CHUNK, LANES)
    parts = exchange(jnp.broadcast_to(parts[None], (16,) + parts.shape), TILE)
    other = lax.ppermute(parts, "c", SWAP)
    first = lax.axis_index("c") == 0
    both = jnp.stack([jnp.where(first, parts, other), jnp.where(first, other, parts)], axis=1)
    both = both.reshape(32, steps, CHUNK, LANES).transpose(1, 0, 2, 3)
    return both.reshape(steps, 32 * CHUNK, LANES)


def split(x):
    high=x.astype(jnp.bfloat16)
    return high,(x-high.astype(jnp.float32)).astype(jnp.bfloat16)

def split_np(x):
    h=x.astype(ml_dtypes.bfloat16)
    return h,(x-h.astype(np.float64)).astype(ml_dtypes.bfloat16)

def tables():
    point=np.arange(GRID)
    def cs(freq):
        ang=2*math.pi*((freq[:,None]*point[None,:])%GRID)/GRID
        return np.cos(ang),np.sin(ang)
    c,s=cs(np.arange(REACH+1))
    t=np.zeros((2,WIDE,2,40))
    t[0,:REACH+1,0,:HALF]=c[:,0::2]; t[0,:REACH+1,1,:HALF]=c[:,1::2]
    t[1,:REACH+1,0,:HALF]=-s[:,0::2]; t[1,:REACH+1,1,:HALF]=-s[:,1::2]
    t=t.reshape(2*WIDE,80)
    h,l=split_np(t)
    first=np.concatenate([h,h,l],1)
    c,s=cs(np.arange(-REACH,REACH+1))
    w=np.zeros((2,LANES,2,SLOT))
    w[0,:GRID,0,:KEPT]=c.T; w[0,:GRID,1,:KEPT]=-s.T
    w[1,:GRID,0,:KEPT]=s.T; w[1,:GRID,1,:KEPT]=c.T
    w=w.reshape(2*LANES,LANES)
    h,l=split_np(w)
    third=np.concatenate([h,l],1)
    u=np.zeros((2,BACK,GRID))
    u[0,:KEPT]=c; u[1,:KEPT]=s
    u=u.reshape(2*BACK,GRID)
    h,l=split_np(u)
    second=np.concatenate([h,h,l],1)
    return first,second,third

def dft_kernel(scale, psi, cond, first, second, third, place, lane, sign, out, vals, held, mixed, spread):
    f32=jnp.float32; bf=jnp.bfloat16
    tail=PAD_ROWS-ROWS
    for s in range(STEPS):
        vals[s,:ROWS,:]=psi[s,:ROWS,:].astype(f32)*cond[:ROWS,:].astype(f32)
        vals[s,ROWS:,:]=jnp.zeros((tail,LANES),f32)
    left=lax.broadcasted_iota(jnp.int32,(40,LANES),1)<LANES//2
    table=first[...]
    zero=jnp.zeros((40,LANES),f32)
    rolled=[pltpu.roll(vals[s,pl.ds(40,40,stride=PAIR),:],LANES//2,1) for s in range(STEPS)]
    for t in range(41):
        cols=[]
        for s in range(STEPS):
            even=vals[s,pl.ds(t,40,stride=PAIR),:]
            here=rolled[s]
            ahead=pltpu.roll(vals[s,pl.ds(41+t,40,stride=PAIR),:],LANES//2,1) if t<40 else zero
            rolled[s]=ahead
            odd=jnp.where(left,here,ahead)
            x=jnp.concatenate([even,odd],0)
            h=x.astype(bf).astype(f32)
            cols.append(jnp.concatenate([h,x-h,h],0).astype(bf))
        y=jnp.dot(table,jnp.concatenate(cols,1),preferred_element_type=f32)
        for s in range(STEPS):
            held[s,:,t*LANES:(t+1)*LANES]=y[:,s*LANES:(s+1)*LANES]
    w=third[...]
    group=8
    for j0 in range(0,GRID,group):
        parts=[[],[]]
        for j in range(j0,j0+group):
            for s in range(STEPS):
                x=held[s,:,j*GRID:j*GRID+LANES]
                parts[0].append(x[:WIDE]); parts[1].append(x[WIDE:])
        x=jnp.concatenate([jnp.concatenate(parts[0],0),jnp.concatenate(parts[1],0)],1)
        h,l=split(x)
        y=jnp.dot(h,w,preferred_element_type=f32)
        z=jnp.dot(l,w[:,:LANES],preferred_element_type=f32)
        mixed[j0*32:(j0+group)*32,:]=y[:,:LANES]+y[:,LANES:]+z
    table=second[...]
    flip=jnp.where(lax.broadcasted_iota(jnp.int32,(BACK,LANES),1)<SLOT,1.0,-1.0).astype(f32)
    for i in range(REACH+1):
        cols=[]
        for s in range(STEPS):
            x=mixed[pl.ds(s*WIDE+i,GRID,stride=32),:]
            h=x.astype(bf).astype(f32)
            cols.append(jnp.concatenate([h,x-h,h],0).astype(bf))
        y=jnp.dot(table,jnp.concatenate(cols,1),preferred_element_type=f32)
        for s in range(STEPS):
            z=y[:,s*LANES:(s+1)*LANES]
            r=(z[:BACK]+flip*pltpu.roll(z[BACK:],SLOT,1))*scale[s]
            spread[s*LANES:(s+1)*LANES, i*BACK:(i+1)*BACK]=r.T.astype(bf)
    tile=512
    rows=(REACH+1)*BACK
    data=spread[...]
    at=lax.broadcasted_iota(jnp.int32,(rows,tile),0)
    slot=lax.broadcasted_iota(jnp.int32,(SLOT,tile),0)
    def pick(n,_):
        here=pl.ds(pl.multiple_of(n*tile,tile),tile)
        hot=jnp.where(at==place[:,here],1.0,0.0).astype(bf)
        y=jnp.dot(data,hot,preferred_element_type=f32)
        keep=slot==lane[:,here]
        r=[jnp.sum(jnp.where(keep,y[p*SLOT:(p+1)*SLOT],0.0),0,keepdims=True) for p in range(2*STEPS)]
        sg=sign[:,here]
        out[:,here]=jnp.concatenate([r[0],r[1]*sg,r[2],r[3]*sg],0).astype(bf)
        return 0
    lax.fori_loop(0,place.shape[1]//tile,pick,0)

def pairs(psi, cond, scale, g_index):
    third=g_index%GRID; second=g_index//GRID%GRID; first=g_index//(GRID*GRID)
    mid=GRID//2
    i=jnp.where(first<mid,first,first-GRID); j=jnp.where(second<mid,second,second-GRID); k=jnp.where(third<mid,third,third-GRID)
    sg=jnp.where(i<0,-1,1)
    place=i*sg*BACK+(j*sg+REACH)
    lane=k*sg+REACH
    a,b,c=[jnp.asarray(x) for x in tables()]
    ng=g_index.shape[0]
    vm=pl.BlockSpec(memory_space=pltpu.VMEM)
    return pl.pallas_call(dft_kernel,
        out_shape=jax.ShapeDtypeStruct((2*STEPS,ng),jnp.bfloat16),
        in_specs=[pl.BlockSpec(memory_space=pltpu.SMEM)]+[vm]*8,
        out_specs=vm,
        scratch_shapes=[pltpu.VMEM((STEPS,PAD_ROWS,LANES),jnp.float32),
            pltpu.VMEM((STEPS,2*WIDE,41*LANES),jnp.float32),
            pltpu.VMEM((GRID*32,LANES),jnp.float32),
            pltpu.VMEM((STEPS*LANES,(REACH+1)*BACK),jnp.bfloat16)],
        compiler_params=pltpu.CompilerParams(vmem_limit_bytes=48*2**20),
    )(scale,psi,cond,a,b,c,place[None],lane[None],sg.astype(jnp.float32)[None])


def body(valence, conduction, val_energy, cond_energy, owner, g_index):
    bands = STEPS * 512
    psi = from_owners(valence, owner)
    cond = conduction.reshape(ROWS, LANES)
    scale = jnp.sqrt(4.0 / (cond_energy[0] - val_energy[owner])) / math.sqrt(GRID**3)
    elems = pairs(psi, cond, scale, g_index)
    count = elems.shape[0]
    ng = elems.shape[1]
    rows = exchange(elems.reshape(count, 16, ng // 16).transpose(1, 0, 2), "z").transpose(1, 0, 2)
    rows = exchange(jnp.broadcast_to(rows[None], (8,) + rows.shape), QUAD)
    other = lax.ppermute(rows, "c", SWAP)
    first = lax.axis_index("c") == 0
    rows = jnp.stack([jnp.where(first, rows, other), jnp.where(first, other, rows)], axis=1)
    cols = exchange(elems.reshape(count, 16, ng // 16).transpose(1, 0, 2), COL).transpose(1, 0, 2)
    cols = exchange(jnp.broadcast_to(cols[None], (16,) + cols.shape), "z")
    cols = cols.reshape(16, count, 8, 2, ng // 16)
    part = jnp.einsum("mclzg,zlmch->gh", rows, cols, preferred_element_type=jnp.float32)
    part = part.reshape(2, ng // 32, ng // 16)
    mine = lax.axis_index("yl")
    away = lax.dynamic_index_in_dim(part, 1 - mine, 0, False).astype(jnp.bfloat16)
    here = lax.dynamic_index_in_dim(part, mine, 0, False)
    total = here + lax.ppermute(away, "yl", SWAP).astype(jnp.float32)
    return -total / math.sqrt(bands)


def solution(mesh):
    every = P(AXES)
    return jax.shard_map(
        body,
        mesh=Mesh(mesh.devices.reshape(SIZES), AXES),
        in_specs=(P(AXES, None), P(AXES, None), P(), every, P(), P()),
        out_specs=P(ROW, COL),
        check_vma=False,
    )
```

time: 558 us -> 243 us (0.44)
  the two profiles are of different devices: /device:TPU:2 before, /device:TPU:32 now
where the time goes in v2:
time: 243 us; the launch traced here: 242 us
  waiting for transfers between devices  89.1 us (37%)
  blocking collectives  48.5 us (20%)
  starting transfers between devices  40.3 us (17%)
  other arithmetic  34.6 us (14%)
  Pallas kernels  12.9 us (5%)
  between operations  8.53 us (4%)
  local copies, waits for them, and re-layouts  6.97 us (3%)
    all_to_all x5, waiting for transfers between devices, exchange(): return lax.all_to_all(x, axis, split_axis=0, concat_axis=0, tiled=True)  81.7 us
    all_to_all x3, blocking collectives, exchange(): return lax.all_to_all(x, axis, split_axis=0, concat_axis=0, tiled=True)  48.5 us
    all_to_all x5, starting transfers between devices, exchange(): return lax.all_to_all(x, axis, split_axis=0, concat_axis=0, tiled=True)  33.5 us
    unnamed x2, other arithmetic  32 us
    pallas_call x1, Pallas kernels, pairs(): pl.pallas_call(dft_kernel, out_shape=jax.ShapeDtypeStruct((2 * STEPS, ng)...  12.9 us
    ppermute x1, waiting for transfers between devices, body(): total = here + lax.ppermute(away, 'yl', SWAP).astype(jnp.float32)  5.6 us
  transfers between devices with their start and end apart: 8, of which 7 were waited for; matrix products, arithmetic and copies ran while one was open for 7% of the time, Pallas kernels for 0%

profile of v2, /device:TPU:32, one launch (start us, length us, event | category | flops | bytes accessed | tf_op | source)
XLA Modules:
  0.0 241.7 jit_solution(7571255019004461523)
XLA Ops:
  0.0 16.5 %reduce = bf16[373248]{0:T(1024)(128)(2,1)S(1)} reduce(bf16[1,373248]{1,0:T(2,128)(2,1)} %param.9, bf16[]{:T(256)} %constant.127), dimensions={0}, to_apply=%param.9.reduce_sub_computation | reduce | bytes 1492994 | tf_op args[0]
  16.5 0.9 pad.4
  17.5 7.3 %all-to-all-start = ((bf16[32,96,128]{2,1,0:T(8,128)(2,1)}), bf16[32,96,128]{2,1,0:T(8,128)(2,1)S(1)}, u32[]{:S(2)}, u32[]{:S(2)}) async-start(bf16[32,96,128]{2,1,0:T(8,128)(2,1)} %bitcast.1), calls=%async_computation | async-start | bytes 1572864 | tf_op jit(solution)/shard_map/all_to_all | solution.py:37
  29.2 10.2 %all-to-all-done = bf16[32,96,128]{2,1,0:T(8,128)(2,1)S(1)} async-done(((bf16[32,96,128]{2,1,0:T(8,128)(2,1)}), bf16[32,96,128]{2,1,0:T(8,128)(2,1)S(1)}, u32[]{:S(2)}, u32[]{:S(2)}) %all-to-all-start) | async-done | bytes 786464 | tf_op jit(solution)/shard_map/all_to_all | solution.py:37
  40.1 15.3 %all-to-all-start.1 = ((bf16[16,2,6,128]{3,1,2,0:T(2,128)(2,1)}), bf16[16,2,6,128]{3,1,2,0:T(2,128)(2,1)S(1)}, u32[]{:S(2)}, u32[]{:S(2)}) async-start(bf16[16,2,6,128]{3,1,2,0:T(2,128)(2,1)} %bitcast.5), calls=%async_computation.1 | async-start | bytes 98304 | tf_op jit(solution)/shard_map/all_to_all | solution.py:37
  59.2 7.9 %all-to-all-done.1 = bf16[16,2,6,128]{3,1,2,0:T(2,128)(2,1)S(1)} async-done(((bf16[16,2,6,128]{3,1,2,0:T(2,128)(2,1)}), bf16[16,2,6,128]{3,1,2,0:T(2,128)(2,1)S(1)}, u32[]{:S(2)}, u32[]{:S(2)}) %all-to-all-start.1) | async-done | bytes 49184 | tf_op jit(solution)/shard_map/all_to_all | solution.py:37
  67.3 15.5 %all_to_all.40 = bf16[16,2,6,128]{3,1,2,0:T(2,128)(2,1)S(1)} all-to-all(bf16[16,2,6,128]{3,1,2,0:T(2,128)(2,1)S(1)} %broadcast_in_dim.42), channel_id=1, replica_groups=mesh['z'=16,'yl'=2,'x'=4,'yh'=2,'c'=2] {'z'}, dimensions={0} | all-to-all | bytes 98304 | tf_op jit(solution)/shard_map/all_to_all | solution.py:37
  83.0 15.6 %all_to_all.41 = bf16[16,192,128]{2,1,0:T(8,128)(2,1)S(1)} all-to-all(bf16[16,192,128]{2,1,0:T(8,128)(2,1)S(1)} %broadcast_in_dim.44), channel_id=1, replica_groups=mesh['z'=16,'yl'=2,'x'=4,'yh'=2,'c'=2] {'yl','x','yh'}, dimensions={0} | all-to-all | bytes 1572864 | tf_op jit(solution)/shard_map/all_to_all | solution.py:37
  98.5 2.2 collective-permute-start
  101.4 15.5 %reduce.1 = bf16[373248]{0:T(1024)(128)(2,1)S(1)} reduce(bf16[1,373248]{1,0:T(2,128)(2,1)S(1)} %copy-done.4, bf16[]{:T(256)} %constant.127), dimensions={0}, to_apply=%param.10.reduce_sub_computation | reduce | bytes 1492994 | tf_op args[1]
  117.7 1.2 select_bitcast_fusion.1
  120.0 12.9 %shard_map.91 = bf16[4,8192]{1,0:T(4,128)(2,1)} custom-call(f32[2]{0:T(128)S(1)} %sqrt_multiply_fusion.scale, bf16[2,3072,128]{2,1,0:T(8,128)(2,1)S(1)} %bitcast.63, bf16[2916,128]{1,0:T(8,128)(2,1)S(1)} %bitcast.64, bf16[32,240]{1,0:T(8,128)(2,1)S(1)} %copy-done.3, bf16[64,216]{1,0:T(8,128)(2,1)S(1)} %copy-done.2, bf16[256,256]{1,0:T(8,128)(2,1)S(1)} %copy-done.1, ...), custom_call_target="tpu_custom_call" | custom-call | tf_op jit(solution)/shard_map/pallas_call | solution.py:170
  133.0 17.4 %all_to_all.42 = bf16[16,4,512]{2,1,0:T(4,128)(2,1)S(1)} all-to-all(bf16[16,4,512]{2,1,0:T(4,128)(2,1)} %bitcast.19), channel_id=1, replica_groups=mesh['z'=16,'yl'=2,'x'=4,'yh'=2,'c'=2] {'z'}, dimensions={0} | all-to-all | bytes 131072 | tf_op jit(solution)/shard_map/all_to_all | solution.py:37
  150.4 3.5 %all-to-all-start.6 = ((bf16[16,4,512]{2,1,0:T(4,128)(2,1)}), bf16[16,4,512]{2,1,0:T(4,128)(2,1)S(1)}, u32[]{:S(2)}, u32[]{:S(2)}) async-start(bf16[16,4,512]{2,1,0:T(4,128)(2,1)} %bitcast.19), calls=%async_computation.6 | async-start | bytes 131072 | tf_op jit(solution)/shard_map/all_to_all | solution.py:37
  153.9 7.6 %all-to-all-done.6 = bf16[16,4,512]{2,1,0:T(4,128)(2,1)S(1)} async-done(((bf16[16,4,512]{2,1,0:T(4,128)(2,1)}), bf16[16,4,512]{2,1,0:T(4,128)(2,1)S(1)}, u32[]{:S(2)}, u32[]{:S(2)}) %all-to-all-start.6) | async-done | bytes 65568 | tf_op jit(solution)/shard_map/all_to_all | solution.py:37
  162.4 3.5 %all-to-all-start.5 = ((bf16[8,4,16,512]{3,2,1,0:T(8,128)(2,1)}), bf16[8,4,16,512]{3,2,1,0:T(8,128)(2,1)S(1)}, u32[]{:S(2)}, u32[]{:S(2)}) async-start(bf16[8,4,16,512]{3,2,1,0:T(8,128)(2,1)} %broadcast_in_dim.48), calls=%async_computation.5 | async-start | bytes 1048576 | tf_op jit(solution)/shard_map/all_to_all | solution.py:37
  165.9 11.2 %all-to-all-done.5 = bf16[8,4,16,512]{3,2,1,0:T(8,128)(2,1)S(1)} async-done(((bf16[8,4,16,512]{3,2,1,0:T(8,128)(2,1)}), bf16[8,4,16,512]{3,2,1,0:T(8,128)(2,1)S(1)}, u32[]{:S(2)}, u32[]{:S(2)}) %all-to-all-start.5) | async-done | bytes 524320 | tf_op jit(solution)/shard_map/all_to_all | solution.py:37
  177.1 1.1 broadcast_in_dim.49
  178.2 3.8 %all-to-all-start.7 = ((bf16[16,4,16,512]{3,2,1,0:T(8,128)(2,1)}), bf16[16,4,16,512]{3,2,1,0:T(8,128)(2,1)S(1)}, u32[]{:S(2)}, u32[]{:S(2)}) async-start(bf16[16,4,16,512]{3,2,1,0:T(8,128)(2,1)} %broadcast_in_dim.49), calls=%async_computation.7 | async-start | bytes 2097152 | tf_op jit(solution)/shard_map/all_to_all | solution.py:37
  182.0 1.9 collective-permute-start.1
  184.0 1.9 collective-permute-done.1
  186.3 44.9 %all-to-all-done.7 = bf16[16,4,16,512]{3,2,1,0:T(8,128)(2,1)S(1)} async-done(((bf16[16,4,16,512]{3,2,1,0:T(8,128)(2,1)}), bf16[16,4,16,512]{3,2,1,0:T(8,128)(2,1)S(1)}, u32[]{:S(2)}, u32[]{:S(2)}) %all-to-all-start.7) | async-done | bytes 1048608 | tf_op jit(solution)/shard_map/all_to_all | solution.py:37
  232.5 2.7 %collective-permute-start.2 = (bf16[256,512]{1,0:T(8,128)(2,1)S(1)}, bf16[256,512]{1,0:T(8,128)(2,1)S(1)}, u32[]{:S(2)}, u32[]{:S(2)}) collective-permute-start(bf16[256,512]{1,0:T(8,128)(2,1)S(1)} %fusion.5), channel_id=1, source_target_pairs={{0,16},{16,0},{1,17},{17,1},{2,18},{18,2},{3,19},{19,3},{4,20},{20... | collective-permute-start | bytes 786440 | tf_op jit(solution)/shard_map/ppermute | solution.py:203
  235.2 5.6 %collective-permute-done.2 = bf16[256,512]{1,0:T(8,128)(2,1)S(1)} collective-permute-done((bf16[256,512]{1,0:T(8,128)(2,1)S(1)}, bf16[256,512]{1,0:T(8,128)(2,1)S(1)}, u32[]{:S(2)}, u32[]{:S(2)}) %collective-permute-start.2) | collective-permute-done | bytes 262176 | tf_op jit(solution)/shard_map/ppermute | solution.py:203
  (47 shorter events, 7.0 us)
Async XLA Ops:
  0.0 116.9 %copy-start = (f32[512]{0:T(512)S(1)}, f32[512]{0:T(512)}, u32[]{:S(2)}) copy-start(f32[512]{0:T(512)} %param.11) | copy-start | bytes 6148
  16.5 8.3 %copy-start.6 = (s32[2]{0:T(128)S(1)}, s32[2]{0:T(128)}, u32[]{:S(2)}) copy-start(s32[2]{0:T(128)} %param.13) | copy-start | bytes 28
  17.5 21.9 %all-to-all-start = ((bf16[32,96,128]{2,1,0:T(8,128)(2,1)}), bf16[32,96,128]{2,1,0:T(8,128)(2,1)S(1)}, u32[]{:S(2)}, u32[]{:S(2)}) async-start(bf16[32,96,128]{2,1,0:T(8,128)(2,1)} %bitcast.1), calls=%async_computation | async-start | bytes 1572864 | tf_op jit(solution)/shard_map/all_to_all | solution.py:37
  40.1 61.3 %copy-start.4 = (bf16[1,373248]{1,0:T(2,128)(2,1)S(1)}, bf16[1,373248]{1,0:T(2,128)(2,1)}, u32[]{:S(2)}) copy-start(bf16[1,373248]{1,0:T(2,128)(2,1)} %param.10) | copy-start | bytes 2239492
  40.1 27.0 %all-to-all-start.1 = ((bf16[16,2,6,128]{3,1,2,0:T(2,128)(2,1)}), bf16[16,2,6,128]{3,1,2,0:T(2,128)(2,1)S(1)}, u32[]{:S(2)}, u32[]{:S(2)}) async-start(bf16[16,2,6,128]{3,1,2,0:T(2,128)(2,1)} %bitcast.5), calls=%async_computation.1 | async-start | bytes 98304 | tf_op jit(solution)/shard_map/all_to_all | solution.py:37
  98.5 19.1 %copy-start.5 = (s32[8192]{0:T(1024)S(1)}, s32[8192]{0:T(1024)}, u32[]{:S(2)}) copy-start(s32[8192]{0:T(1024)} %param.14) | copy-start | bytes 98308
  98.5 19.2 %collective-permute-start = (bf16[16,192,128]{2,1,0:T(8,128)(2,1)S(1)}, bf16[16,192,128]{2,1,0:T(8,128)(2,1)}, u32[]{:S(2)}, u32[]{:S(2)}) collective-permute-start(bf16[16,192,128]{2,1,0:T(8,128)(2,1)S(1)} %all_to_all.41), channel_id=1, source_target_pairs={{0,1},{1,0},{2,3},{3,2},{4,5},{5,4},{6,7},{7,6},{8,9},{9,8},{10,11... | collective-permute-start | bytes 2359304 | tf_op jit(solution)/shard_map/ppermute | solution.py:53
  119.1 0.9 copy-start.1
  119.1 0.9 copy-start.2
  119.1 0.9 copy-start.3
  150.4 11.1 %all-to-all-start.6 = ((bf16[16,4,512]{2,1,0:T(4,128)(2,1)}), bf16[16,4,512]{2,1,0:T(4,128)(2,1)S(1)}, u32[]{:S(2)}, u32[]{:S(2)}) async-start(bf16[16,4,512]{2,1,0:T(4,128)(2,1)} %bitcast.19), calls=%async_computation.6 | async-start | bytes 131072 | tf_op jit(solution)/shard_map/all_to_all | solution.py:37
  162.4 14.7 %all-to-all-start.5 = ((bf16[8,4,16,512]{3,2,1,0:T(8,128)(2,1)}), bf16[8,4,16,512]{3,2,1,0:T(8,128)(2,1)S(1)}, u32[]{:S(2)}, u32[]{:S(2)}) async-start(bf16[8,4,16,512]{3,2,1,0:T(8,128)(2,1)} %broadcast_in_dim.48), calls=%async_computation.5 | async-start | bytes 1048576 | tf_op jit(solution)/shard_map/all_to_all | solution.py:37
  178.2 52.9 %all-to-all-start.7 = ((bf16[16,4,16,512]{3,2,1,0:T(8,128)(2,1)}), bf16[16,4,16,512]{3,2,1,0:T(8,128)(2,1)S(1)}, u32[]{:S(2)}, u32[]{:S(2)}) async-start(bf16[16,4,16,512]{3,2,1,0:T(8,128)(2,1)} %broadcast_in_dim.49), calls=%async_computation.7 | async-start | bytes 2097152 | tf_op jit(solution)/shard_map/all_to_all | solution.py:37
  182.0 3.8 %collective-permute-start.1 = (bf16[8,4,16,512]{3,2,1,0:T(8,128)(2,1)S(1)}, bf16[8,4,16,512]{3,2,1,0:T(8,128)(2,1)S(1)}, u32[]{:S(2)}, u32[]{:S(2)}) collective-permute-start(bf16[8,4,16,512]{3,2,1,0:T(8,128)(2,1)S(1)} %all-to-all-done.5), channel_id=1, source_target_pairs={{0,1},{1,0},{2,3},{3,2},{4,5},{5,4},{6,7},{7,6},{8,9},{9,8},{10,11... | collective-permute-start | bytes 1572872 | tf_op jit(solution)/shard_map/ppermute | solution.py:192
  232.5 8.3 %collective-permute-start.2 = (bf16[256,512]{1,0:T(8,128)(2,1)S(1)}, bf16[256,512]{1,0:T(8,128)(2,1)S(1)}, u32[]{:S(2)}, u32[]{:S(2)}) collective-permute-start(bf16[256,512]{1,0:T(8,128)(2,1)S(1)} %fusion.5), channel_id=1, source_target_pairs={{0,16},{16,0},{1,17},{17,1},{2,18},{18,2},{3,19},{19,3},{4,20},{20... | collective-permute-start | bytes 786440 | tf_op jit(solution)/shard_map/ppermute | solution.py:203

commit v3 on v2

--- a/solution.py
+++ b/solution.py
@@ -37,12 +37,33 @@
     return lax.all_to_all(x, axis, split_axis=0, concat_axis=0, tiled=True)
 
 
+def rows_kernel(flat, out, rows):
+    done = ROWS // 32 * 32
+    for at in range(0, done, 32):
+        part = flat[:, at * LANES : (at + 32) * LANES].astype(jnp.float32)
+        rows[at : at + 32, :] = part.reshape(32, LANES)
+    part = flat[:, done * LANES :].astype(jnp.float32)
+    rows[done:ROWS, :] = part.reshape(ROWS - done, LANES)
+    rows[ROWS:, :] = jnp.zeros((32 * CHUNK - ROWS, LANES), jnp.float32)
+    out[...] = rows[...].astype(jnp.bfloat16)
+
+
+def in_rows(flat):
+    return pl.pallas_call(
+        rows_kernel,
+        out_shape=jax.ShapeDtypeStruct((32 * CHUNK, LANES), jnp.bfloat16),
+        in_specs=[pl.BlockSpec(memory_space=pltpu.VMEM)],
+        out_specs=pl.BlockSpec(memory_space=pltpu.VMEM),
+        scratch_shapes=[pltpu.VMEM((32 * CHUNK, LANES), jnp.float32)],
+        cost_estimate=pl.CostEstimate(flops=0, bytes_accessed=4 * 2**20, transcendentals=0),
+        compiler_params=pltpu.CompilerParams(vmem_limit_bytes=32 * 2**20),
+    )(flat)
+
+
 def from_owners(shard, owner):
-    size = shard.shape[1]
     steps = owner.shape[0]
     owner_z, owner_plane = owner // 32, owner % 32
-    flat = jnp.pad(shard.reshape(size // LANES, LANES), ((0, 32 * CHUNK - size // LANES), (0, 0)))
-    parts = exchange(flat.reshape(32, CHUNK, LANES), PLANE)
+    parts = exchange(in_rows(shard).reshape(32, CHUNK, LANES), PLANE)
     parts = jnp.stack([lax.dynamic_index_in_dim(parts, owner_plane[s], 0, False) for s in range(steps)])
     parts = parts.reshape(steps, 16, PIECE, LANES).transpose(1, 0, 2, 3)
     parts = exchange(parts, "z")
@@ -182,7 +203,7 @@
 def body(valence, conduction, val_energy, cond_energy, owner, g_index):
     bands = STEPS * 512
     psi = from_owners(valence, owner)
-    cond = conduction.reshape(ROWS, LANES)
+    cond = in_rows(conduction)
     scale = jnp.sqrt(4.0 / (cond_energy[0] - val_energy[owner])) / math.sqrt(GRID**3)
     elems = pairs(psi, cond, scale, g_index)
     count = elems.shape[0]

time: 243 us -> 213 us (0.88)
  other arithmetic: 34.6 us -> 2.58 us
    unnamed x2 -> x0, other arithmetic: 32 us -> none
  transfers between devices with their start and end apart: 8 -> 8, of which waited for: 7 -> 8; matrix products, arithmetic and copies ran while one was open for 7% -> 1% of each run, Pallas kernels for 0% -> 0%
where the time goes in v3:
time: 213 us; the launch traced here: 212 us
  waiting for transfers between devices  89.8 us (42%)
  blocking collectives  48.1 us (23%)
  starting transfers between devices  40.7 us (19%)
  Pallas kernels  14.4 us (7%)
  between operations  8.36 us (4%)
  local copies, waits for them, and re-layouts  7.5 us (4%)
  other arithmetic  2.58 us (1%)
    all_to_all x5, waiting for transfers between devices, exchange(): return lax.all_to_all(x, axis, split_axis=0, concat_axis=0, tiled=True)  81.8 us
    all_to_all x3, blocking collectives, exchange(): return lax.all_to_all(x, axis, split_axis=0, concat_axis=0, tiled=True)  48.1 us
    all_to_all x5, starting transfers between devices, exchange(): return lax.all_to_all(x, axis, split_axis=0, concat_axis=0, tiled=True)  34.1 us
    pallas_call x1, Pallas kernels, pairs(): pl.pallas_call(dft_kernel, out_shape=jax.ShapeDtypeStruct((2 * STEPS, ng)...  12.9 us
    ppermute x1, waiting for transfers between devices, body(): total = here + lax.ppermute(away, 'yl', SWAP).astype(jnp.float32)  5.6 us
  transfers between devices with their start and end apart: 8, of which 8 were waited for; matrix products, arithmetic and copies ran while one was open for 1% of the time, Pallas kernels for 0%

profile of v3, /device:TPU:32, one launch (start us, length us, event | category | flops | bytes accessed | tf_op | source)
XLA Modules:
  0.0 212.3 jit_solution(2122338189125620453)
XLA Ops:
  0.0 1.4 copy-done.1
  1.4 1.2 shard_map.91
  2.6 7.3 %all-to-all-start = ((bf16[32,96,128]{2,1,0:T(8,128)(2,1)}), bf16[32,96,128]{2,1,0:T(8,128)(2,1)S(1)}, u32[]{:S(2)}, u32[]{:S(2)}) async-start(bf16[32,96,128]{2,1,0:T(8,128)(2,1)} %bitcast.1), calls=%async_computation | async-start | bytes 1572864 | tf_op jit(solution)/shard_map/all_to_all | solution.py:37
  14.3 10.3 %all-to-all-done = bf16[32,96,128]{2,1,0:T(8,128)(2,1)S(1)} async-done(((bf16[32,96,128]{2,1,0:T(8,128)(2,1)}), bf16[32,96,128]{2,1,0:T(8,128)(2,1)S(1)}, u32[]{:S(2)}, u32[]{:S(2)}) %all-to-all-start) | async-done | bytes 786464 | tf_op jit(solution)/shard_map/all_to_all | solution.py:37
  25.2 15.3 %all-to-all-start.1 = ((bf16[16,2,6,128]{3,1,2,0:T(2,128)(2,1)}), bf16[16,2,6,128]{3,1,2,0:T(2,128)(2,1)S(1)}, u32[]{:S(2)}, u32[]{:S(2)}) async-start(bf16[16,2,6,128]{3,1,2,0:T(2,128)(2,1)} %bitcast.5), calls=%async_computation.1 | async-start | bytes 98304 | tf_op jit(solution)/shard_map/all_to_all | solution.py:37
  44.3 7.9 %all-to-all-done.1 = bf16[16,2,6,128]{3,1,2,0:T(2,128)(2,1)S(1)} async-done(((bf16[16,2,6,128]{3,1,2,0:T(2,128)(2,1)}), bf16[16,2,6,128]{3,1,2,0:T(2,128)(2,1)S(1)}, u32[]{:S(2)}, u32[]{:S(2)}) %all-to-all-start.1) | async-done | bytes 49184 | tf_op jit(solution)/shard_map/all_to_all | solution.py:37
  52.4 15.5 %all_to_all.40 = bf16[16,2,6,128]{3,1,2,0:T(2,128)(2,1)S(1)} all-to-all(bf16[16,2,6,128]{3,1,2,0:T(2,128)(2,1)S(1)} %broadcast_in_dim.42), channel_id=1, replica_groups=mesh['z'=16,'yl'=2,'x'=4,'yh'=2,'c'=2] {'z'}, dimensions={0} | all-to-all | bytes 98304 | tf_op jit(solution)/shard_map/all_to_all | solution.py:37
  68.1 15.6 %all_to_all.41 = bf16[16,192,128]{2,1,0:T(8,128)(2,1)S(1)} all-to-all(bf16[16,192,128]{2,1,0:T(8,128)(2,1)S(1)} %broadcast_in_dim.44), channel_id=1, replica_groups=mesh['z'=16,'yl'=2,'x'=4,'yh'=2,'c'=2] {'yl','x','yh'}, dimensions={0} | all-to-all | bytes 1572864 | tf_op jit(solution)/shard_map/all_to_all | solution.py:37
  83.7 2.0 collective-permute-start
  88.1 1.2 select_bitcast_fusion.1
  90.4 12.9 %shard_map.93 = bf16[4,8192]{1,0:T(4,128)(2,1)} custom-call(f32[2]{0:T(128)S(1)} %sqrt_multiply_fusion.scale, bf16[2,3072,128]{2,1,0:T(8,128)(2,1)S(1)} %bitcast.61, bf16[3072,128]{1,0:T(8,128)(2,1)S(1)} %shard_map.92.cond, bf16[32,240]{1,0:T(8,128)(2,1)S(1)} %copy-done.5, bf16[64,216]{1,0:T(8,128)(2,1)S(1)} %copy-done.4, bf16[256,256]{1,0:T(8,128)(2,1)S(1)} %copy-done.3, ...), custom_call_target="tpu_custom_call" | custom-call | tf_op jit(solution)/shard_map/pallas_call | solution.py:191
  103.4 17.1 %all_to_all.42 = bf16[16,4,512]{2,1,0:T(4,128)(2,1)S(1)} all-to-all(bf16[16,4,512]{2,1,0:T(4,128)(2,1)} %bitcast.19), channel_id=1, replica_groups=mesh['z'=16,'yl'=2,'x'=4,'yh'=2,'c'=2] {'z'}, dimensions={0} | all-to-all | bytes 131072 | tf_op jit(solution)/shard_map/all_to_all | solution.py:37
  120.4 3.5 %all-to-all-start.6 = ((bf16[16,4,512]{2,1,0:T(4,128)(2,1)}), bf16[16,4,512]{2,1,0:T(4,128)(2,1)S(1)}, u32[]{:S(2)}, u32[]{:S(2)}) async-start(bf16[16,4,512]{2,1,0:T(4,128)(2,1)} %bitcast.19), calls=%async_computation.6 | async-start | bytes 131072 | tf_op jit(solution)/shard_map/all_to_all | solution.py:37
  123.9 7.6 %all-to-all-done.6 = bf16[16,4,512]{2,1,0:T(4,128)(2,1)S(1)} async-done(((bf16[16,4,512]{2,1,0:T(4,128)(2,1)}), bf16[16,4,512]{2,1,0:T(4,128)(2,1)S(1)}, u32[]{:S(2)}, u32[]{:S(2)}) %all-to-all-start.6) | async-done | bytes 65568 | tf_op jit(solution)/shard_map/all_to_all | solution.py:37
  132.4 3.5 %all-to-all-start.5 = ((bf16[8,4,16,512]{3,2,1,0:T(8,128)(2,1)}), bf16[8,4,16,512]{3,2,1,0:T(8,128)(2,1)S(1)}, u32[]{:S(2)}, u32[]{:S(2)}) async-start(bf16[8,4,16,512]{3,2,1,0:T(8,128)(2,1)} %broadcast_in_dim.48), calls=%async_computation.5 | async-start | bytes 1048576 | tf_op jit(solution)/shard_map/all_to_all | solution.py:37
  135.9 11.2 %all-to-all-done.5 = bf16[8,4,16,512]{3,2,1,0:T(8,128)(2,1)S(1)} async-done(((bf16[8,4,16,512]{3,2,1,0:T(8,128)(2,1)}), bf16[8,4,16,512]{3,2,1,0:T(8,128)(2,1)S(1)}, u32[]{:S(2)}, u32[]{:S(2)}) %all-to-all-start.5) | async-done | bytes 524320 | tf_op jit(solution)/shard_map/all_to_all | solution.py:37
  147.1 1.1 broadcast_in_dim.49
  148.2 4.4 %all-to-all-start.7 = ((bf16[16,4,16,512]{3,2,1,0:T(8,128)(2,1)}), bf16[16,4,16,512]{3,2,1,0:T(8,128)(2,1)S(1)}, u32[]{:S(2)}, u32[]{:S(2)}) async-start(bf16[16,4,16,512]{3,2,1,0:T(8,128)(2,1)} %broadcast_in_dim.49), calls=%async_computation.7 | async-start | bytes 2097152 | tf_op jit(solution)/shard_map/all_to_all | solution.py:37
  152.7 1.9 collective-permute-start.1
  154.6 1.9 collective-permute-done.1
  156.9 44.9 %all-to-all-done.7 = bf16[16,4,16,512]{3,2,1,0:T(8,128)(2,1)S(1)} async-done(((bf16[16,4,16,512]{3,2,1,0:T(8,128)(2,1)}), bf16[16,4,16,512]{3,2,1,0:T(8,128)(2,1)S(1)}, u32[]{:S(2)}, u32[]{:S(2)}) %all-to-all-start.7) | async-done | bytes 1048608 | tf_op jit(solution)/shard_map/all_to_all | solution.py:37
  203.2 2.7 %collective-permute-start.2 = (bf16[256,512]{1,0:T(8,128)(2,1)S(1)}, bf16[256,512]{1,0:T(8,128)(2,1)S(1)}, u32[]{:S(2)}, u32[]{:S(2)}) collective-permute-start(bf16[256,512]{1,0:T(8,128)(2,1)S(1)} %fusion.5), channel_id=1, source_target_pairs={{0,16},{16,0},{1,17},{17,1},{2,18},{18,2},{3,19},{19,3},{4,20},{20... | collective-permute-start | bytes 786440 | tf_op jit(solution)/shard_map/ppermute | solution.py:224
  205.8 5.6 %collective-permute-done.2 = bf16[256,512]{1,0:T(8,128)(2,1)S(1)} collective-permute-done((bf16[256,512]{1,0:T(8,128)(2,1)S(1)}, bf16[256,512]{1,0:T(8,128)(2,1)S(1)}, u32[]{:S(2)}, u32[]{:S(2)}) %collective-permute-start.2) | collective-permute-done | bytes 262176 | tf_op jit(solution)/shard_map/ppermute | solution.py:224
  211.4 0.9 fusion.4
  (48 shorter events, 7.1 us)
Async XLA Ops:
  0.0 86.7 %copy-start = (f32[512]{0:T(512)S(1)}, f32[512]{0:T(512)}, u32[]{:S(2)}) copy-start(f32[512]{0:T(512)} %param.11) | copy-start | bytes 6148
  0.0 1.4 copy-start.1
  1.4 8.5 %copy-start.7 = (s32[2]{0:T(128)S(1)}, s32[2]{0:T(128)}, u32[]{:S(2)}) copy-start(s32[2]{0:T(128)} %param.13) | copy-start | bytes 28
  2.6 21.9 %all-to-all-start = ((bf16[32,96,128]{2,1,0:T(8,128)(2,1)}), bf16[32,96,128]{2,1,0:T(8,128)(2,1)S(1)}, u32[]{:S(2)}, u32[]{:S(2)}) async-start(bf16[32,96,128]{2,1,0:T(8,128)(2,1)} %bitcast.1), calls=%async_computation | async-start | bytes 1572864 | tf_op jit(solution)/shard_map/all_to_all | solution.py:37
  25.2 61.2 %copy-start.2 = (bf16[1,373248]{1,0:T(2,128)(2,1)S(1)}, bf16[1,373248]{1,0:T(2,128)(2,1)}, u32[]{:S(2)}) copy-start(bf16[1,373248]{1,0:T(2,128)(2,1)} %flat.3) | copy-start | bytes 2239492
  25.2 27.0 %all-to-all-start.1 = ((bf16[16,2,6,128]{3,1,2,0:T(2,128)(2,1)}), bf16[16,2,6,128]{3,1,2,0:T(2,128)(2,1)S(1)}, u32[]{:S(2)}, u32[]{:S(2)}) async-start(bf16[16,2,6,128]{3,1,2,0:T(2,128)(2,1)} %bitcast.5), calls=%async_computation.1 | async-start | bytes 98304 | tf_op jit(solution)/shard_map/all_to_all | solution.py:37
  83.7 3.7 %copy-start.6 = (s32[8192]{0:T(1024)S(1)}, s32[8192]{0:T(1024)}, u32[]{:S(2)}) copy-start(s32[8192]{0:T(1024)} %param.14) | copy-start | bytes 98308
  83.7 4.4 %collective-permute-start = (bf16[16,192,128]{2,1,0:T(8,128)(2,1)S(1)}, bf16[16,192,128]{2,1,0:T(8,128)(2,1)}, u32[]{:S(2)}, u32[]{:S(2)}) collective-permute-start(bf16[16,192,128]{2,1,0:T(8,128)(2,1)S(1)} %all_to_all.41), channel_id=1, source_target_pairs={{0,1},{1,0},{2,3},{3,2},{4,5},{5,4},{6,7},{7,6},{8,9},{9,8},{10,11... | collective-permute-start | bytes 2359304 | tf_op jit(solution)/shard_map/ppermute | solution.py:74
  89.5 0.9 copy-start.3
  89.5 0.9 copy-start.4
  89.5 0.9 copy-start.5
  120.4 11.1 %all-to-all-start.6 = ((bf16[16,4,512]{2,1,0:T(4,128)(2,1)}), bf16[16,4,512]{2,1,0:T(4,128)(2,1)S(1)}, u32[]{:S(2)}, u32[]{:S(2)}) async-start(bf16[16,4,512]{2,1,0:T(4,128)(2,1)} %bitcast.19), calls=%async_computation.6 | async-start | bytes 131072 | tf_op jit(solution)/shard_map/all_to_all | solution.py:37
  132.4 14.7 %all-to-all-start.5 = ((bf16[8,4,16,512]{3,2,1,0:T(8,128)(2,1)}), bf16[8,4,16,512]{3,2,1,0:T(8,128)(2,1)S(1)}, u32[]{:S(2)}, u32[]{:S(2)}) async-start(bf16[8,4,16,512]{3,2,1,0:T(8,128)(2,1)} %broadcast_in_dim.48), calls=%async_computation.5 | async-start | bytes 1048576 | tf_op jit(solution)/shard_map/all_to_all | solution.py:37
  148.2 53.5 %all-to-all-start.7 = ((bf16[16,4,16,512]{3,2,1,0:T(8,128)(2,1)}), bf16[16,4,16,512]{3,2,1,0:T(8,128)(2,1)S(1)}, u32[]{:S(2)}, u32[]{:S(2)}) async-start(bf16[16,4,16,512]{3,2,1,0:T(8,128)(2,1)} %broadcast_in_dim.49), calls=%async_computation.7 | async-start | bytes 2097152 | tf_op jit(solution)/shard_map/all_to_all | solution.py:37
  152.7 3.8 %collective-permute-start.1 = (bf16[8,4,16,512]{3,2,1,0:T(8,128)(2,1)S(1)}, bf16[8,4,16,512]{3,2,1,0:T(8,128)(2,1)S(1)}, u32[]{:S(2)}, u32[]{:S(2)}) collective-permute-start(bf16[8,4,16,512]{3,2,1,0:T(8,128)(2,1)S(1)} %all-to-all-done.5), channel_id=1, source_target_pairs={{0,1},{1,0},{2,3},{3,2},{4,5},{5,4},{6,7},{7,6},{8,9},{9,8},{10,11... | collective-permute-start | bytes 1572872 | tf_op jit(solution)/shard_map/ppermute | solution.py:213
  203.2 8.3 %collective-permute-start.2 = (bf16[256,512]{1,0:T(8,128)(2,1)S(1)}, bf16[256,512]{1,0:T(8,128)(2,1)S(1)}, u32[]{:S(2)}, u32[]{:S(2)}) collective-permute-start(bf16[256,512]{1,0:T(8,128)(2,1)S(1)} %fusion.5), channel_id=1, source_target_pairs={{0,16},{16,0},{1,17},{17,1},{2,18},{18,2},{3,19},{19,3},{4,20},{20... | collective-permute-start | bytes 786440 | tf_op jit(solution)/shard_map/ppermute | solution.py:224

commit v4 on v3

--- a/solution.py
+++ b/solution.py
@@ -22,6 +22,14 @@
 PIECE = 6
 CHUNK = 16 * PIECE
 SWAP = [(0, 1), (1, 0)]
+NG = 8192
+BLOCKS = 16
+SPAN = NG // BLOCKS
+SLOTS = 320
+WIDTH = 384
+BOTH = 2 * SLOTS // LANES
+ELEMS = 16
+NAMED = 1 << 20
 REACH=12
 KEPT=2*REACH+1
 HALF=GRID//2
@@ -112,7 +120,7 @@
     second=np.concatenate([h,h,l],1)
     return first,second,third
 
-def dft_kernel(scale, psi, cond, first, second, third, place, lane, sign, out, vals, held, mixed, spread):
+def dft_kernel(scale, psi, cond, first, second, third, places, out, vals, held, mixed, spread):
     f32=jnp.float32; bf=jnp.bfloat16
     tail=PAD_ROWS-ROWS
     for s in range(STEPS):
@@ -162,67 +170,186 @@
             z=y[:,s*LANES:(s+1)*LANES]
             r=(z[:BACK]+flip*pltpu.roll(z[BACK:],SLOT,1))*scale[s]
             spread[s*LANES:(s+1)*LANES, i*BACK:(i+1)*BACK]=r.T.astype(bf)
-    tile=512
-    rows=(REACH+1)*BACK
-    data=spread[...]
-    at=lax.broadcasted_iota(jnp.int32,(rows,tile),0)
-    slot=lax.broadcasted_iota(jnp.int32,(SLOT,tile),0)
-    def pick(n,_):
-        here=pl.ds(pl.multiple_of(n*tile,tile),tile)
-        hot=jnp.where(at==place[:,here],1.0,0.0).astype(bf)
-        y=jnp.dot(data,hot,preferred_element_type=f32)
-        keep=slot==lane[:,here]
-        r=[jnp.sum(jnp.where(keep,y[p*SLOT:(p+1)*SLOT],0.0),0,keepdims=True) for p in range(2*STEPS)]
-        sg=sign[:,here]
-        out[:,here]=jnp.concatenate([r[0],r[1]*sg,r[2],r[3]*sg],0).astype(bf)
-        return 0
-    lax.fori_loop(0,place.shape[1]//tile,pick,0)
-
-def pairs(psi, cond, scale, g_index):
-    third=g_index%GRID; second=g_index//GRID%GRID; first=g_index//(GRID*GRID)
-    mid=GRID//2
-    i=jnp.where(first<mid,first,first-GRID); j=jnp.where(second<mid,second,second-GRID); k=jnp.where(third<mid,third,third-GRID)
-    sg=jnp.where(i<0,-1,1)
-    place=i*sg*BACK+(j*sg+REACH)
-    lane=k*sg+REACH
-    a,b,c=[jnp.asarray(x) for x in tables()]
-    ng=g_index.shape[0]
-    vm=pl.BlockSpec(memory_space=pltpu.VMEM)
-    return pl.pallas_call(dft_kernel,
-        out_shape=jax.ShapeDtypeStruct((2*STEPS,ng),jnp.bfloat16),
-        in_specs=[pl.BlockSpec(memory_space=pltpu.SMEM)]+[vm]*8,
+    rows = (REACH + 1) * BACK
+    data = spread[...]
+    at = lax.broadcasted_iota(jnp.int32, (rows, WIDTH), 0)
+    slot = lax.broadcasted_iota(jnp.int32, (SLOT, WIDTH), 0)
+    gap = jnp.zeros((STEPS, 2 * LANES), f32)
+    for b in range(BLOCKS):
+        place = places[b : b + 1, :]
+        hot = jnp.where(at == (place >> 6), 1.0, 0.0).astype(bf)
+        y = jnp.dot(data, hot, preferred_element_type=f32)
+        keep = slot == (place & (SLOT - 1))
+        got = [
+            jnp.sum(jnp.where(keep, y[p * SLOT : (p + 1) * SLOT], 0.0), 0, keepdims=True)
+            for p in range(2 * STEPS)
+        ]
+        real = jnp.concatenate([jnp.concatenate(got[0::2], 0), gap], 1)
+        imag = pltpu.roll(jnp.concatenate(got[1::2], 0), WIDTH - SLOTS, 1)
+        both = real + jnp.concatenate([gap, imag], 1)
+        lines = [both[s : s + 1, n * LANES : (n + 1) * LANES] for s in range(STEPS) for n in range(BOTH)]
+        lines.append(jnp.zeros((ELEMS - len(lines), LANES), f32))
+        out[b] = jnp.concatenate(lines, 0).astype(bf)
+
+
+def layout():
+    axis = np.arange(-REACH, REACH + 1)
+    grid = np.stack(np.meshgrid(axis, axis, axis, indexing="ij"), -1).reshape(-1, 3)
+    length = (grid**2).sum(1)
+    fixed = np.full((BLOCKS, WIDTH), -1)
+    kind = np.zeros((BLOCKS, WIDTH), np.int32)
+    target = np.full((BLOCKS, SPAN), -1)
+    own = np.full((BLOCKS, WIDTH), -5)
+    begin = [0] * BLOCKS
+    shells = [[] for _ in range(BLOCKS)]
+    ends = [0] * BLOCKS
+    at = 0
+    for value in np.unique(length):
+        if at >= NG:
+            break
+        shell = grid[length == value]
+        stop = min(at + len(shell), NG)
+        for b in range(at // SPAN, (stop - 1) // SPAN + 1):
+            low, high = max(at, b * SPAN), min(stop, b * SPAN + SPAN)
+            if high - low == len(shell) or 2 * (high - low) > len(shell):
+                i, j, k = shell.T
+                front = (i > 0) | ((i == 0) & ((j > 0) | ((j == 0) & (k >= 0))))
+                i, j, k = shell[front].T
+                shells[b].append((i * BACK + j + REACH) * SLOT + k + REACH)
+            elif low == b * SPAN:
+                begin[b] = high - low
+            else:
+                assert high == b * SPAN + SPAN
+                ends[b] = high - low
+        at = stop
+    for b in range(BLOCKS):
+        known = np.concatenate(shells[b])
+        assert begin[b] + len(known) + ends[b] <= SLOTS
+        fixed[b, begin[b] : begin[b] + len(known)] = known
+        own[b, begin[b] : begin[b] + len(known)] = known
+        kind[b, : begin[b]] = 1
+        kind[b, SLOTS - ends[b] : SLOTS] = 2
+        target[b, : begin[b]] = NAMED + np.arange(begin[b])
+        target[b, SPAN - ends[b] :] = NAMED + np.arange(SLOTS - ends[b], SLOTS)
+        places = np.arange(WIDTH)
+        own[b] = np.where(kind[b] > 0, NAMED + places, own[b])
+    columns = np.full((2, WIDTH, LANES), -5.0, np.float32)
+    columns[0, :, :BLOCKS] = own.T
+    columns[1, SLOT:, :BLOCKS] = own.T[: WIDTH - SLOT]
+    return fixed.astype(np.int32), kind, target.astype(np.int32), columns
+
+
+def frequencies(g_index):
+    fixed, kind, target, _ = layout()
+    g = g_index.reshape(BLOCKS, SPAN)
+    half = GRID // 2
+    i, j, k = g // (GRID * GRID), g // GRID % GRID, g % GRID
+    i, j, k = [jnp.where(n < half, n, n - GRID) for n in (i, j, k)]
+    front = (i > 0) | ((i == 0) & ((j > 0) | ((j == 0) & (k >= 0))))
+    sign = jnp.where(front, 1, -1)
+    ids = (i * sign * BACK + j * sign + REACH) * SLOT + k * sign + REACH
+    first = ids[:, :WIDTH]
+    last = jnp.pad(ids[:, SPAN - SLOTS :], ((0, 0), (0, WIDTH - SLOTS)))
+    places = jnp.where(kind == 1, first, jnp.where(kind == 2, last, fixed))
+    names = jnp.where(target >= 0, target, ids)
+    return places, names.astype(jnp.float32), sign.astype(jnp.float32)
+
+
+def pairs(psi, cond, scale, places):
+    first, second, third = [jnp.asarray(table) for table in (tables())]
+    vm = pl.BlockSpec(memory_space=pltpu.VMEM)
+    return pl.pallas_call(
+        dft_kernel,
+        out_shape=jax.ShapeDtypeStruct((BLOCKS, ELEMS, LANES), jnp.bfloat16),
+        in_specs=[pl.BlockSpec(memory_space=pltpu.SMEM)] + [vm] * 6,
         out_specs=vm,
-        scratch_shapes=[pltpu.VMEM((STEPS,PAD_ROWS,LANES),jnp.float32),
-            pltpu.VMEM((STEPS,2*WIDE,41*LANES),jnp.float32),
-            pltpu.VMEM((GRID*32,LANES),jnp.float32),
-            pltpu.VMEM((STEPS*LANES,(REACH+1)*BACK),jnp.bfloat16)],
-        compiler_params=pltpu.CompilerParams(vmem_limit_bytes=48*2**20),
-    )(scale,psi,cond,a,b,c,place[None],lane[None],sg.astype(jnp.float32)[None])
+        scratch_shapes=[
+            pltpu.VMEM((STEPS, PAD_ROWS, LANES), jnp.float32),
+            pltpu.VMEM((STEPS, 2 * WIDE, 41 * LANES), jnp.float32),
+            pltpu.VMEM((GRID * 32, LANES), jnp.float32),
+            pltpu.VMEM((STEPS * LANES, (REACH + 1) * BACK), jnp.bfloat16),
+        ],
+        compiler_params=pltpu.CompilerParams(vmem_limit_bytes=48 * 2**20),
+    )(scale, psi, cond, first, second, third, places)
+
+
+def sums_kernel(me, same, other, cols, names, signs, columns, here, away):
+    f32, bf = jnp.float32, jnp.bfloat16
+    z, m, yl, c = [me[n] for n in range(4)]
+    half = SPAN // 2
+
+    def spread(block, swapped):
+        name, sign = names[pl.ds(block, 1), :], signs[pl.ds(block, 1), :]
+        if swapped is not None:
+            turn = lambda x: jnp.where(swapped, jnp.concatenate([x[:, half:], x[:, :half]], 1), x)
+            name, sign = turn(name), turn(sign)
+        chosen = lax.broadcasted_iota(jnp.int32, (WIDTH, LANES), 1) == block
+        place = [jnp.sum(jnp.where(chosen, columns[p], 0.0), 1, keepdims=True) for p in range(2)]
+        real = jnp.where(place[0] == name, 1.0, 0.0).astype(bf)
+        return real, jnp.where(place[1] == name, sign, 0.0).astype(bf)
+
+    def lanes(ref, n):
+        return ref[:, n * 32 : (n + 1) * 32, :].reshape(-1, LANES)
+
+    def widened(tiles, hot):
+        real = jnp.dot(jnp.concatenate(tiles[:3], 1), hot[0], preferred_element_type=f32)
+        imag = jnp.dot(jnp.concatenate(tiles[2:], 1), hot[1], preferred_element_type=f32)
+        return real.astype(bf), imag.astype(bf)
+
+    count = cols.shape[0] * 32
+    to = lax.broadcasted_iota(jnp.int32, (count, count), 0)
+    at = lax.broadcasted_iota(jnp.int32, (count, count), 1)
+    core = jnp.bitwise_xor(at >> 8, c)
+    order = ((at & 15) << 5) | (((at >> 4) & 1) << 4) | (((at >> 5) & 7) << 1) | core
+    order = jnp.where(to == order, 1.0, 0.0).astype(bf)
+    tiles = [jnp.concatenate([lanes(same, n), lanes(other, n)], 0) for n in range(BOTH)]
+    tiles = jnp.dot(order, jnp.concatenate(tiles, 1), preferred_element_type=f32).astype(bf)
+    tiles = [tiles[:, n * LANES : (n + 1) * LANES] for n in range(BOTH)]
+    left = widened(tiles, spread(z, yl == 1))
+    right = widened([lanes(cols, n) for n in range(BOTH)], spread(m, None))
+    over = (((0,), (0,)), ((), ()))
+    total = lax.dot_general(left[0], right[0], over, preferred_element_type=f32)
+    total += lax.dot_general(left[1], right[1], over, preferred_element_type=f32)
+    total *= -1.0 / math.sqrt(STEPS * 512)
+    here[...] = total[:half]
+    away[...] = total[half:].astype(bf)
+
+
+def sums(me, same, other, cols, names, signs):
+    vm = pl.BlockSpec(memory_space=pltpu.VMEM)
+    half = SPAN // 2
+    return pl.pallas_call(
+        sums_kernel,
+        out_shape=[
+            jax.ShapeDtypeStruct((half, SPAN), jnp.float32),
+            jax.ShapeDtypeStruct((half, SPAN), jnp.bfloat16),
+        ],
+        in_specs=[pl.BlockSpec(memory_space=pltpu.SMEM)] + [vm] * 6,
+        out_specs=[vm, vm],
+        compiler_params=pltpu.CompilerParams(vmem_limit_bytes=48 * 2**20),
+    )(me, same, other, cols, names, signs, jnp.asarray(layout()[3]))
 
 
 def body(valence, conduction, val_energy, cond_energy, owner, g_index):
-    bands = STEPS * 512
     psi = from_owners(valence, owner)
     cond = in_rows(conduction)
     scale = jnp.sqrt(4.0 / (cond_energy[0] - val_energy[owner])) / math.sqrt(GRID**3)
-    elems = pairs(psi, cond, scale, g_index)
-    count = elems.shape[0]
-    ng = elems.shape[1]
-    rows = exchange(elems.reshape(count, 16, ng // 16).transpose(1, 0, 2), "z").transpose(1, 0, 2)
+    places, names, signs = frequencies(g_index)
+    elems = pairs(psi, cond, scale, places)
+
+    def by_lanes(x):
+        return x.reshape(16, STEPS, BOTH, LANES).transpose(2, 1, 0, 3).reshape(16 * STEPS * BOTH, LANES)
+
+    used = STEPS * BOTH
+    cols = by_lanes(exchange(elems, COL)[:, :used])
+    cols = jnp.broadcast_to(cols[None], (16,) + cols.shape)
+    cols = exchange(jnp.concatenate([cols, elems], axis=1), "z")
+    rows = by_lanes(cols[:, -ELEMS : used - ELEMS])
     rows = exchange(jnp.broadcast_to(rows[None], (8,) + rows.shape), QUAD)
     other = lax.ppermute(rows, "c", SWAP)
-    first = lax.axis_index("c") == 0
-    rows = jnp.stack([jnp.where(first, rows, other), jnp.where(first, other, rows)], axis=1)
-    cols = exchange(elems.reshape(count, 16, ng // 16).transpose(1, 0, 2), COL).transpose(1, 0, 2)
-    cols = exchange(jnp.broadcast_to(cols[None], (16,) + cols.shape), "z")
-    cols = cols.reshape(16, count, 8, 2, ng // 16)
-    part = jnp.einsum("mclzg,zlmch->gh", rows, cols, preferred_element_type=jnp.float32)
-    part = part.reshape(2, ng // 32, ng // 16)
-    mine = lax.axis_index("yl")
-    away = lax.dynamic_index_in_dim(part, 1 - mine, 0, False).astype(jnp.bfloat16)
-    here = lax.dynamic_index_in_dim(part, mine, 0, False)
-    total = here + lax.ppermute(away, "yl", SWAP).astype(jnp.float32)
-    return -total / math.sqrt(bands)
+    me = jnp.stack([lax.axis_index(a) for a in ("z", COL, "yl", "c")]).astype(jnp.int32)
+    here, away = sums(me, rows, other, cols, names, signs)
+    return here + lax.ppermute(away, "yl", SWAP).astype(jnp.float32)
 
 
 def solution(mesh):

time: 213 us -> 184 us (0.86)
  the two profiles are of different devices: /device:TPU:32 before, /device:TPU:1 now
where the time goes in v4:
time: 184 us; the launch traced here: 183 us
  blocking collectives  74.9 us (41%)
  starting transfers between devices  42.6 us (23%)
  waiting for transfers between devices  36.4 us (20%)
  Pallas kernels  11.8 us (6%)
  between operations  8.67 us (5%)
  local copies, waits for them, and re-layouts  5.82 us (3%)
  other arithmetic  2.64 us (1%)
    all_to_all x4, blocking collectives, exchange(): return lax.all_to_all(x, axis, split_axis=0, concat_axis=0, tiled=True)  74.9 us
    all_to_all x3, waiting for transfers between devices, exchange(): return lax.all_to_all(x, axis, split_axis=0, concat_axis=0, tiled=True)  27.8 us
    all_to_all x3, starting transfers between devices, exchange(): return lax.all_to_all(x, axis, split_axis=0, concat_axis=0, tiled=True)  27.3 us
    pallas_call x1, Pallas kernels, pairs(): pl.pallas_call(dft_kernel, out_shape=jax.ShapeDtypeStruct((BLOCKS, ELEMS,...  7.41 us
    ppermute x1, starting transfers between devices, body(): other = lax.ppermute(rows, 'c', SWAP)  6.64 us
    ppermute x1, waiting for transfers between devices, body(): return here + lax.ppermute(away, 'yl', SWAP).astype(jnp.float32)  6.37 us
    ppermute x1, starting transfers between devices, from_owners(): other = lax.ppermute(parts, 'c', SWAP)  5.67 us
  transfers between devices with their start and end apart: 6, of which 6 were waited for; matrix products, arithmetic and copies ran while one was open for 1% of the time, Pallas kernels for 0%

profile of v4, /device:TPU:1, one launch (start us, length us, event | category | flops | bytes accessed | tf_op | source)
XLA Modules:
  0.0 182.9 jit_solution(7152375341591806654)
XLA Ops:
  0.0 1.4 copy-done.1
  1.4 1.2 shard_map.145
  2.6 10.4 %all-to-all-start = ((bf16[32,96,128]{2,1,0:T(8,128)(2,1)}), bf16[32,96,128]{2,1,0:T(8,128)(2,1)S(1)}, u32[]{:S(2)}, u32[]{:S(2)}) async-start(bf16[32,96,128]{2,1,0:T(8,128)(2,1)} %bitcast.5), calls=%async_computation | async-start | bytes 1572864 | tf_op jit(solution)/shard_map/all_to_all | solution.py:45
  17.4 10.1 %all-to-all-done = bf16[32,96,128]{2,1,0:T(8,128)(2,1)S(1)} async-done(((bf16[32,96,128]{2,1,0:T(8,128)(2,1)}), bf16[32,96,128]{2,1,0:T(8,128)(2,1)S(1)}, u32[]{:S(2)}, u32[]{:S(2)}) %all-to-all-start) | async-done | bytes 786464 | tf_op jit(solution)/shard_map/all_to_all | solution.py:45
  28.2 13.1 %all-to-all-start.1 = ((bf16[16,2,6,128]{3,1,2,0:T(2,128)(2,1)}), bf16[16,2,6,128]{3,1,2,0:T(2,128)(2,1)S(1)}, u32[]{:S(2)}, u32[]{:S(2)}) async-start(bf16[16,2,6,128]{3,1,2,0:T(2,128)(2,1)} %bitcast.9), calls=%async_computation.1 | async-start | bytes 98304 | tf_op jit(solution)/shard_map/all_to_all | solution.py:45
  45.2 7.6 %all-to-all-done.1 = bf16[16,2,6,128]{3,1,2,0:T(2,128)(2,1)S(1)} async-done(((bf16[16,2,6,128]{3,1,2,0:T(2,128)(2,1)}), bf16[16,2,6,128]{3,1,2,0:T(2,128)(2,1)S(1)}, u32[]{:S(2)}, u32[]{:S(2)}) %all-to-all-start.1) | async-done | bytes 49184 | tf_op jit(solution)/shard_map/all_to_all | solution.py:45
  53.0 15.3 %all_to_all.35 = bf16[16,2,6,128]{3,1,2,0:T(2,128)(2,1)S(1)} all-to-all(bf16[16,2,6,128]{3,1,2,0:T(2,128)(2,1)S(1)} %broadcast_in_dim.35), channel_id=1, replica_groups=mesh['z'=16,'yl'=2,'x'=4,'yh'=2,'c'=2] {'z'}, dimensions={0} | all-to-all | bytes 98304 | tf_op jit(solution)/shard_map/all_to_all | solution.py:45
  68.3 1.1 broadcast_in_dim.37
  69.4 3.7 %all-to-all-start.3 = ((bf16[16,192,128]{2,1,0:T(8,128)(2,1)}), bf16[16,192,128]{2,1,0:T(8,128)(2,1)S(1)}, u32[]{:S(2)}, u32[]{:S(2)}) async-start(bf16[16,192,128]{2,1,0:T(8,128)(2,1)} %broadcast_in_dim.37), calls=%async_computation.3 | async-start | bytes 1572864 | tf_op jit(solution)/shard_map/all_to_all | solution.py:45
  74.5 10.1 %all-to-all-done.3 = bf16[16,192,128]{2,1,0:T(8,128)(2,1)S(1)} async-done(((bf16[16,192,128]{2,1,0:T(8,128)(2,1)}), bf16[16,192,128]{2,1,0:T(8,128)(2,1)S(1)}, u32[]{:S(2)}, u32[]{:S(2)}) %all-to-all-start.3) | async-done | bytes 786464 | tf_op jit(solution)/shard_map/all_to_all | solution.py:45
  84.5 5.7 %collective-permute-start = (bf16[16,192,128]{2,1,0:T(8,128)(2,1)S(1)}, bf16[16,192,128]{2,1,0:T(8,128)(2,1)}, u32[]{:S(2)}, u32[]{:S(2)}) collective-permute-start(bf16[16,192,128]{2,1,0:T(8,128)(2,1)S(1)} %all-to-all-done.3), channel_id=1, source_target_pairs={{0,1},{1,0},{2,3},{3,2},{4,5},{5,4},{6,7},{7,6},{8,9},{9,8},{10,11... | collective-permute-start | bytes 2359304 | tf_op jit(solution)/shard_map/ppermute | solution.py:82
  91.1 1.1 collective-permute-done
  92.2 1.2 select_bitcast_fusion.1
  93.8 0.8 copy-done.4
  94.6 7.4 %shard_map.147 = bf16[16,16,128]{2,1,0:T(8,128)(2,1)S(1)} custom-call(f32[2]{0:T(128)S(1)} %sqrt_multiply_fusion.scale, bf16[2,3072,128]{2,1,0:T(8,128)(2,1)S(1)} %bitcast.40, bf16[3072,128]{1,0:T(8,128)(2,1)S(1)} %shard_map.146.cond, bf16[32,240]{1,0:T(8,128)(2,1)S(1)} %copy-done.6, bf16[64,216]{1,0:T(8,128)(2,1)S(1)} %copy-done.5, ...), custom_call_target="tpu_custom_call" | custom-call | tf_op jit(solution)/shard_map/pallas_call | solution.py:261
  102.0 11.3 %all_to_all.36 = bf16[16,16,128]{2,1,0:T(8,128)(2,1)S(1)} all-to-all(bf16[16,16,128]{2,1,0:T(8,128)(2,1)S(1)} %shard_map.147), channel_id=1, replica_groups=mesh['z'=16,'yl'=2,'x'=4,'yh'=2,'c'=2] {'x','yh','c'}, dimensions={0} | all-to-all | bytes 131072 | tf_op jit(solution)/shard_map/all_to_all | solution.py:45
  113.4 38.0 %all_to_all.37.cols = bf16[16,176,128]{2,1,0:T(8,128)(2,1)S(1)} all-to-all(bf16[16,176,128]{2,1,0:T(8,128)(2,1)S(1)} %pad_maximum_fusion.1), channel_id=1, replica_groups=mesh['z'=16,'yl'=2,'x'=4,'yh'=2,'c'=2] {'z'}, dimensions={0} | all-to-all | bytes 1441792 | tf_op jit(solution)/shard_map/all_to_all | solution.py:45
  151.5 10.4 %all_to_all.38.same = bf16[8,160,128]{2,1,0:T(8,128)(2,1)S(1)} all-to-all(bf16[8,160,128]{2,1,0:T(8,128)(2,1)S(1)} %broadcast_in_dim.41), channel_id=1, replica_groups=mesh['z'=16,'yl'=2,'x'=4,'yh'=2,'c'=2] {'x','yh'}, dimensions={0} | all-to-all | bytes 655360 | tf_op jit(solution)/shard_map/all_to_all | solution.py:45
  161.9 6.6 %collective-permute-start.1 = (bf16[8,160,128]{2,1,0:T(8,128)(2,1)S(1)}, bf16[8,160,128]{2,1,0:T(8,128)(2,1)S(1)}, u32[]{:S(2)}, u32[]{:S(2)}) collective-permute-start(bf16[8,160,128]{2,1,0:T(8,128)(2,1)S(1)} %all_to_all.38.same), channel_id=1, source_target_pairs={{0,1},{1,0},{2,3},{3,2},{4,5},{5,4},{6,7},{7,6},{8,9},{9,8},{10,11... | collective-permute-start | bytes 983048 | tf_op jit(solution)/shard_map/ppermute | solution.py:349
  168.7 1.1 collective-permute-done.1.other
  169.8 2.8 %shard_map.148 = (f32[256,512]{1,0:T(8,128)S(1)}, bf16[256,512]{1,0:T(8,128)(2,1)S(1)}) custom-call(s32[4]{0:T(128)S(1)} %pad_add_fusion.me, bf16[8,160,128]{2,1,0:T(8,128)(2,1)S(1)} %all_to_all.38.same, bf16[8,160,128]{2,1,0:T(8,128)(2,1)S(1)} %collective-permute-done.1.other, bf16[16,176,128]{2,1,0:T(8,128)(2,1)S(1)} %all_to_all.37.cols, ...), custom_call_target="tpu_custom_call" | custom-call | tf_op jit(solution)/shard_map/pallas_call | solution.py:321
  172.7 3.0 %collective-permute-start.2 = (bf16[256,512]{1,0:T(8,128)(2,1)S(1)}, bf16[256,512]{1,0:T(8,128)(2,1)S(1)}, u32[]{:S(2)}, u32[]{:S(2)}) collective-permute-start(bf16[256,512]{1,0:T(8,128)(2,1)S(1)} %get-tuple-element.8), channel_id=1, source_target_pairs={{0,16},{16,0},{1,17},{17,1},{2,18},{18,2},{3,19},{19,3},{4,20},{20... | collective-permute-start | bytes 786440 | tf_op jit(solution)/shard_map/ppermute | solution.py:352
  175.7 6.4 %collective-permute-done.2 = bf16[256,512]{1,0:T(8,128)(2,1)S(1)} collective-permute-done((bf16[256,512]{1,0:T(8,128)(2,1)S(1)}, bf16[256,512]{1,0:T(8,128)(2,1)S(1)}, u32[]{:S(2)}, u32[]{:S(2)}) %collective-permute-start.2) | collective-permute-done | bytes 262176 | tf_op jit(solution)/shard_map/ppermute | solution.py:352
  182.1 0.9 convert_add_fusion
  (67 shorter events, 3.5 us)
Async XLA Ops:
  0.0 90.4 %copy-start = (f32[512]{0:T(512)S(1)}, f32[512]{0:T(512)}, u32[]{:S(2)}) copy-start(f32[512]{0:T(512)} %param.17) | copy-start | bytes 6148
  0.0 1.4 copy-start.1
  1.4 11.7 %copy-start.13 = (s32[2]{0:T(128)S(1)}, s32[2]{0:T(128)}, u32[]{:S(2)}) copy-start(s32[2]{0:T(128)} %param.19) | copy-start | bytes 28
  2.6 24.9 %all-to-all-start = ((bf16[32,96,128]{2,1,0:T(8,128)(2,1)}), bf16[32,96,128]{2,1,0:T(8,128)(2,1)S(1)}, u32[]{:S(2)}, u32[]{:S(2)}) async-start(bf16[32,96,128]{2,1,0:T(8,128)(2,1)} %bitcast.5), calls=%async_computation | async-start | bytes 1572864 | tf_op jit(solution)/shard_map/all_to_all | solution.py:45
  28.2 45.7 %copy-start.2 = (bf16[1,373248]{1,0:T(2,128)(2,1)S(1)}, bf16[1,373248]{1,0:T(2,128)(2,1)}, u32[]{:S(2)}) copy-start(bf16[1,373248]{1,0:T(2,128)(2,1)} %flat.3) | copy-start | bytes 2239492
  28.2 24.7 %all-to-all-start.1 = ((bf16[16,2,6,128]{3,1,2,0:T(2,128)(2,1)}), bf16[16,2,6,128]{3,1,2,0:T(2,128)(2,1)S(1)}, u32[]{:S(2)}, u32[]{:S(2)}) async-start(bf16[16,2,6,128]{3,1,2,0:T(2,128)(2,1)} %bitcast.9), calls=%async_computation.1 | async-start | bytes 98304 | tf_op jit(solution)/shard_map/all_to_all | solution.py:45
  69.4 4.8 %copy-start.7 = (s32[8192]{0:T(1024)S(1)}, s32[8192]{0:T(1024)}, u32[]{:S(2)}) copy-start(s32[8192]{0:T(1024)} %param.20) | copy-start | bytes 98308
  69.4 15.1 %all-to-all-start.3 = ((bf16[16,192,128]{2,1,0:T(8,128)(2,1)}), bf16[16,192,128]{2,1,0:T(8,128)(2,1)S(1)}, u32[]{:S(2)}, u32[]{:S(2)}) async-start(bf16[16,192,128]{2,1,0:T(8,128)(2,1)} %broadcast_in_dim.37), calls=%async_computation.3 | async-start | bytes 1572864 | tf_op jit(solution)/shard_map/all_to_all | solution.py:45
  73.2 17.1 %copy-start.8 = (s32[16,512]{1,0:T(8,128)S(1)}, s32[16,512]{1,0:T(8,128)}, u32[]{:S(2)}) copy-start(s32[16,512]{1,0:T(8,128)} %constant.139.clone) | copy-start | bytes 98308
  73.2 17.1 %copy-start.10 = (pred[16,512]{1,0:T(8,128)(4,1)S(1)}, pred[16,512]{1,0:T(8,128)(4,1)}, u32[]{:S(2)}) copy-start(pred[16,512]{1,0:T(8,128)(4,1)} %constant.138.clone) | copy-start | bytes 24580
  73.9 17.2 %copy-start.9 = (s32[16,384]{1,0:T(8,128)S(1)}, s32[16,384]{1,0:T(8,128)}, u32[]{:S(2)}) copy-start(s32[16,384]{1,0:T(8,128)} %constant.136.clone) | copy-start | bytes 73732
  73.9 17.2 %copy-start.11 = (pred[16,384]{1,0:T(8,128)(4,1)S(1)}, pred[16,384]{1,0:T(8,128)(4,1)}, u32[]{:S(2)}) copy-start(pred[16,384]{1,0:T(8,128)(4,1)} %constant.137.clone) | copy-start | bytes 18436
  73.9 17.2 %copy-start.12 = (pred[16,384]{1,0:T(8,128)(4,1)S(1)}, pred[16,384]{1,0:T(8,128)(4,1)}, u32[]{:S(2)}) copy-start(pred[16,384]{1,0:T(8,128)(4,1)} %constant.135.clone) | copy-start | bytes 18436
  84.5 7.7 %collective-permute-start = (bf16[16,192,128]{2,1,0:T(8,128)(2,1)S(1)}, bf16[16,192,128]{2,1,0:T(8,128)(2,1)}, u32[]{:S(2)}, u32[]{:S(2)}) collective-permute-start(bf16[16,192,128]{2,1,0:T(8,128)(2,1)S(1)} %all-to-all-done.3), channel_id=1, source_target_pairs={{0,1},{1,0},{2,3},{3,2},{4,5},{5,4},{6,7},{7,6},{8,9},{9,8},{10,11... | collective-permute-start | bytes 2359304 | tf_op jit(solution)/shard_map/ppermute | solution.py:82
  93.7 0.9 copy-start.4
  93.7 0.9 copy-start.5
  93.7 0.9 copy-start.6
  113.4 56.4 %copy-start.3 = (f32[2,384,128]{2,1,0:T(8,128)S(1)}, f32[2,384,128]{2,1,0:T(8,128)}, u32[]{:S(2)}) copy-start(f32[2,384,128]{2,1,0:T(8,128)} %constant.143.clone.columns) | copy-start | bytes 1179652
  161.9 7.9 %collective-permute-start.1 = (bf16[8,160,128]{2,1,0:T(8,128)(2,1)S(1)}, bf16[8,160,128]{2,1,0:T(8,128)(2,1)S(1)}, u32[]{:S(2)}, u32[]{:S(2)}) collective-permute-start(bf16[8,160,128]{2,1,0:T(8,128)(2,1)S(1)} %all_to_all.38.same), channel_id=1, source_target_pairs={{0,1},{1,0},{2,3},{3,2},{4,5},{5,4},{6,7},{7,6},{8,9},{9,8},{10,11... | collective-permute-start | bytes 983048 | tf_op jit(solution)/shard_map/ppermute | solution.py:349
  172.7 9.4 %collective-permute-start.2 = (bf16[256,512]{1,0:T(8,128)(2,1)S(1)}, bf16[256,512]{1,0:T(8,128)(2,1)S(1)}, u32[]{:S(2)}, u32[]{:S(2)}) collective-permute-start(bf16[256,512]{1,0:T(8,128)(2,1)S(1)} %get-tuple-element.8), channel_id=1, source_target_pairs={{0,16},{16,0},{1,17},{17,1},{2,18},{18,2},{3,19},{19,3},{4,20},{20... | collective-permute-start | bytes 786440 | tf_op jit(solution)/shard_map/ppermute | solution.py:352

commit v5 on v4

--- a/solution.py
+++ b/solution.py
@@ -28,7 +28,8 @@
 SLOTS = 320
 WIDTH = 384
 BOTH = 2 * SLOTS // LANES
-ELEMS = 16
+LINES = STEPS * BOTH
+ELEMS = LINES * BLOCKS
 NAMED = 1 << 20
 REACH=12
 KEPT=2*REACH+1
@@ -79,11 +80,7 @@
     parts = exchange(jnp.broadcast_to(parts[None], (16,) + parts.shape), "z")
     parts = parts.transpose(1, 0, 2, 3).reshape(steps * CHUNK, LANES)
     parts = exchange(jnp.broadcast_to(parts[None], (16,) + parts.shape), TILE)
-    other = lax.ppermute(parts, "c", SWAP)
-    first = lax.axis_index("c") == 0
-    both = jnp.stack([jnp.where(first, parts, other), jnp.where(first, other, parts)], axis=1)
-    both = both.reshape(32, steps, CHUNK, LANES).transpose(1, 0, 2, 3)
-    return both.reshape(steps, 32 * CHUNK, LANES)
+    return parts, lax.ppermute(parts, "c", SWAP)
 
 
 def split(x):
@@ -120,12 +117,15 @@
     second=np.concatenate([h,h,l],1)
     return first,second,third
 
-def dft_kernel(scale, psi, cond, first, second, third, places, out, vals, held, mixed, spread):
+def dft_kernel(core, scale, same, other, cond, first, second, third, places, out, vals, held, mixed, spread, lined):
     f32=jnp.float32; bf=jnp.bfloat16
-    tail=PAD_ROWS-ROWS
     for s in range(STEPS):
-        vals[s,:ROWS,:]=psi[s,:ROWS,:].astype(f32)*cond[:ROWS,:].astype(f32)
-        vals[s,ROWS:,:]=jnp.zeros((tail,LANES),f32)
+        vals[s, 32 * CHUNK :, :] = jnp.zeros((PAD_ROWS - 32 * CHUNK, LANES), f32)
+        for t in range(16):
+            for psi, side in ((same, core[0]), (other, 1 - core[0])):
+                here = pl.ds(pl.multiple_of((2 * t + side) * CHUNK, CHUNK), CHUNK)
+                band = psi[t, s * CHUNK : (s + 1) * CHUNK, :].astype(f32)
+                vals[s, here, :] = band * cond[here, :].astype(f32)
     left=lax.broadcasted_iota(jnp.int32,(40,LANES),1)<LANES//2
     table=first[...]
     zero=jnp.zeros((40,LANES),f32)
@@ -187,9 +187,36 @@
         real = jnp.concatenate([jnp.concatenate(got[0::2], 0), gap], 1)
         imag = pltpu.roll(jnp.concatenate(got[1::2], 0), WIDTH - SLOTS, 1)
         both = real + jnp.concatenate([gap, imag], 1)
-        lines = [both[s : s + 1, n * LANES : (n + 1) * LANES] for s in range(STEPS) for n in range(BOTH)]
-        lines.append(jnp.zeros((ELEMS - len(lines), LANES), f32))
-        out[b] = jnp.concatenate(lines, 0).astype(bf)
+        for s in range(STEPS):
+            for n in range(BOTH):
+                at_line = (s * BOTH + n) * BLOCKS + b
+                lined[at_line : at_line + 1, :] = both[s : s + 1, n * LANES : (n + 1) * LANES]
+    out[...] = lined[...].astype(bf)
+
+
+def turn_kernel(block, gathered, out, rows):
+    rows[...] = gathered[...].astype(jnp.float32)
+    for b in range(BLOCKS):
+        for line in range(LINES):
+            s, n = line // BOTH, line % BOTH
+            got = rows[pl.ds(line * BLOCKS + b, 16, stride=ELEMS), :]
+            to = (n * STEPS + s) * 16
+            out[b, to : to + 16, :] = got.astype(jnp.bfloat16)
+    chosen = out[block[0], :ELEMS, :]
+    for b in range(BLOCKS):
+        out[b, ELEMS:, :] = chosen
+
+
+def turn(block, gathered):
+    vm = pl.BlockSpec(memory_space=pltpu.VMEM)
+    return pl.pallas_call(
+        turn_kernel,
+        out_shape=jax.ShapeDtypeStruct((BLOCKS, 2 * ELEMS, LANES), jnp.bfloat16),
+        in_specs=[pl.BlockSpec(memory_space=pltpu.SMEM), vm],
+        out_specs=vm,
+        scratch_shapes=[pltpu.VMEM((16 * ELEMS, LANES), jnp.float32)],
+        compiler_params=pltpu.CompilerParams(vmem_limit_bytes=32 * 2**20),
+    )(block, gathered)
 
 
 def layout():
@@ -255,27 +282,28 @@
     return places, names.astype(jnp.float32), sign.astype(jnp.float32)
 
 
-def pairs(psi, cond, scale, places):
+def pairs(psi, cond, scale, places, core):
     first, second, third = [jnp.asarray(table) for table in (tables())]
     vm = pl.BlockSpec(memory_space=pltpu.VMEM)
     return pl.pallas_call(
         dft_kernel,
-        out_shape=jax.ShapeDtypeStruct((BLOCKS, ELEMS, LANES), jnp.bfloat16),
-        in_specs=[pl.BlockSpec(memory_space=pltpu.SMEM)] + [vm] * 6,
+        out_shape=jax.ShapeDtypeStruct((ELEMS, LANES), jnp.bfloat16),
+        in_specs=[pl.BlockSpec(memory_space=pltpu.SMEM)] * 2 + [vm] * 7,
         out_specs=vm,
         scratch_shapes=[
             pltpu.VMEM((STEPS, PAD_ROWS, LANES), jnp.float32),
             pltpu.VMEM((STEPS, 2 * WIDE, 41 * LANES), jnp.float32),
             pltpu.VMEM((GRID * 32, LANES), jnp.float32),
             pltpu.VMEM((STEPS * LANES, (REACH + 1) * BACK), jnp.bfloat16),
+            pltpu.VMEM((ELEMS, LANES), jnp.float32),
         ],
         compiler_params=pltpu.CompilerParams(vmem_limit_bytes=48 * 2**20),
-    )(scale, psi, cond, first, second, third, places)
-
-
-def sums_kernel(me, same, other, cols, names, signs, columns, here, away):
+    )(core, scale, *psi, cond, first, second, third, places)
+
+
+def sums_kernel(me, elems, names, signs, columns, here, away):
     f32, bf = jnp.float32, jnp.bfloat16
-    z, m, yl, c = [me[n] for n in range(4)]
+    z, m, yl = [me[n] for n in range(3)]
     half = SPAN // 2
 
     def spread(block, swapped):
@@ -288,25 +316,16 @@
         real = jnp.where(place[0] == name, 1.0, 0.0).astype(bf)
         return real, jnp.where(place[1] == name, sign, 0.0).astype(bf)
 
-    def lanes(ref, n):
-        return ref[:, n * 32 : (n + 1) * 32, :].reshape(-1, LANES)
+    def lanes(n):
+        return elems[:, n * 32 : (n + 1) * 32, :].reshape(-1, LANES)
 
     def widened(tiles, hot):
         real = jnp.dot(jnp.concatenate(tiles[:3], 1), hot[0], preferred_element_type=f32)
         imag = jnp.dot(jnp.concatenate(tiles[2:], 1), hot[1], preferred_element_type=f32)
         return real.astype(bf), imag.astype(bf)
 
-    count = cols.shape[0] * 32
-    to = lax.broadcasted_iota(jnp.int32, (count, count), 0)
-    at = lax.broadcasted_iota(jnp.int32, (count, count), 1)
-    core = jnp.bitwise_xor(at >> 8, c)
-    order = ((at & 15) << 5) | (((at >> 4) & 1) << 4) | (((at >> 5) & 7) << 1) | core
-    order = jnp.where(to == order, 1.0, 0.0).astype(bf)
-    tiles = [jnp.concatenate([lanes(same, n), lanes(other, n)], 0) for n in range(BOTH)]
-    tiles = jnp.dot(order, jnp.concatenate(tiles, 1), preferred_element_type=f32).astype(bf)
-    tiles = [tiles[:, n * LANES : (n + 1) * LANES] for n in range(BOTH)]
-    left = widened(tiles, spread(z, yl == 1))
-    right = widened([lanes(cols, n) for n in range(BOTH)], spread(m, None))
+    left = widened([lanes(BOTH + n) for n in range(BOTH)], spread(z, yl == 1))
+    right = widened([lanes(n) for n in range(BOTH)], spread(m, None))
     over = (((0,), (0,)), ((), ()))
     total = lax.dot_general(left[0], right[0], over, preferred_element_type=f32)
     total += lax.dot_general(left[1], right[1], over, preferred_element_type=f32)
@@ -315,7 +334,7 @@
     away[...] = total[half:].astype(bf)
 
 
-def sums(me, same, other, cols, names, signs):
+def sums(me, elems, names, signs):
     vm = pl.BlockSpec(memory_space=pltpu.VMEM)
     half = SPAN // 2
     return pl.pallas_call(
@@ -324,10 +343,10 @@
             jax.ShapeDtypeStruct((half, SPAN), jnp.float32),
             jax.ShapeDtypeStruct((half, SPAN), jnp.bfloat16),
         ],
-        in_specs=[pl.BlockSpec(memory_space=pltpu.SMEM)] + [vm] * 6,
+        in_specs=[pl.BlockSpec(memory_space=pltpu.SMEM)] + [vm] * 4,
         out_specs=[vm, vm],
         compiler_params=pltpu.CompilerParams(vmem_limit_bytes=48 * 2**20),
-    )(me, same, other, cols, names, signs, jnp.asarray(layout()[3]))
+    )(me, elems, names, signs, jnp.asarray(layout()[3]))
 
 
 def body(valence, conduction, val_energy, cond_energy, owner, g_index):
@@ -335,20 +354,13 @@
     cond = in_rows(conduction)
     scale = jnp.sqrt(4.0 / (cond_energy[0] - val_energy[owner])) / math.sqrt(GRID**3)
     places, names, signs = frequencies(g_index)
-    elems = pairs(psi, cond, scale, places)
-
-    def by_lanes(x):
-        return x.reshape(16, STEPS, BOTH, LANES).transpose(2, 1, 0, 3).reshape(16 * STEPS * BOTH, LANES)
-
-    used = STEPS * BOTH
-    cols = by_lanes(exchange(elems, COL)[:, :used])
-    cols = jnp.broadcast_to(cols[None], (16,) + cols.shape)
-    cols = exchange(jnp.concatenate([cols, elems], axis=1), "z")
-    rows = by_lanes(cols[:, -ELEMS : used - ELEMS])
-    rows = exchange(jnp.broadcast_to(rows[None], (8,) + rows.shape), QUAD)
-    other = lax.ppermute(rows, "c", SWAP)
-    me = jnp.stack([lax.axis_index(a) for a in ("z", COL, "yl", "c")]).astype(jnp.int32)
-    here, away = sums(me, rows, other, cols, names, signs)
+    core = lax.axis_index("c").astype(jnp.int32)
+    elems = pairs(psi, cond, scale, places, core[None])
+
+    elems = lax.all_gather(elems, "z", axis=0, tiled=True)
+    me = jnp.stack([lax.axis_index(a) for a in ("z", COL, "yl")]).astype(jnp.int32)
+    elems = exchange(turn(me, elems), COL)
+    here, away = sums(me, elems, names, signs)
     return here + lax.ppermute(away, "yl", SWAP).astype(jnp.float32)
 
 

time: 184 us -> 170 us (0.924)
  starting transfers between devices: 42.6 us -> 35.7 us
  blocking collectives: 74.9 us -> 70.4 us
    all_to_all x4 -> x2, blocking collectives: 74.9 us -> 46.2 us  [exchange(): return lax.all_to_all(x, axis, split_axis=0, concat_axis=0, tiled=True)]
    all_gather x0 -> x1, blocking collectives: none -> 24.3 us  [body(): elems = lax.all_gather(elems, 'z', axis=0, tiled=True)]
    ppermute x2 -> x1, starting transfers between devices: 12.3 us -> 5.67 us  [from_owners(): return (parts, lax.ppermute(parts, 'c', SWAP))]
    ppermute x2 -> x1, waiting for transfers between devices: 2.28 us -> 0.01 us  [from_owners(): return (parts, lax.ppermute(parts, 'c', SWAP))]
    pallas_call x1 -> x2, Pallas kernels: 7.41 us -> 9.39 us  [the longest x1 7.97 us: pairs(): pl.pallas_call(dft_kernel, out_shape=jax.ShapeDtypeStruct((ELEMS, LANES),...]
  transfers between devices with their start and end apart: 6 -> 5, of which waited for: 6 -> 4; matrix products, arithmetic and copies ran while one was open for 1% -> 1% of each run, Pallas kernels for 0% -> 0%
where the time goes in v5:
time: 170 us; the launch traced here: 169 us
  blocking collectives  70.4 us (41%)
  starting transfers between devices  35.7 us (21%)
  waiting for transfers between devices  35.1 us (21%)
  Pallas kernels  13.4 us (8%)
  between operations  8.86 us (5%)
  local copies, waits for them, and re-layouts  4.77 us (3%)
    all_to_all x2, blocking collectives, exchange(): return lax.all_to_all(x, axis, split_axis=0, concat_axis=0, tiled=True)  46.2 us
    all_to_all x3, waiting for transfers between devices, exchange(): return lax.all_to_all(x, axis, split_axis=0, concat_axis=0, tiled=True)  28.7 us
    all_to_all x3, starting transfers between devices, exchange(): return lax.all_to_all(x, axis, split_axis=0, concat_axis=0, tiled=True)  27 us
    all_gather x1, blocking collectives, body(): elems = lax.all_gather(elems, 'z', axis=0, tiled=True)  24.3 us
    pallas_call x1, Pallas kernels, pairs(): pl.pallas_call(dft_kernel, out_shape=jax.ShapeDtypeStruct((ELEMS, LANES),...  7.97 us
    ppermute x1, waiting for transfers between devices, body(): return here + lax.ppermute(away, 'yl', SWAP).astype(jnp.float32)  6.41 us
    ppermute x1, starting transfers between devices, from_owners(): return (parts, lax.ppermute(parts, 'c', SWAP))  5.67 us
  transfers between devices with their start and end apart: 5, of which 4 were waited for; matrix products, arithmetic and copies ran while one was open for 1% of the time, Pallas kernels for 0%

profile of v5, /device:TPU:1, one launch (start us, length us, event | category | flops | bytes accessed | tf_op | source)
XLA Modules:
  0.0 169.5 jit_solution(9936396647516344760)
XLA Ops:
  0.0 1.4 copy-done.1
  1.4 1.2 shard_map.145
  2.6 10.4 %all-to-all-start = ((bf16[32,96,128]{2,1,0:T(8,128)(2,1)}), bf16[32,96,128]{2,1,0:T(8,128)(2,1)S(1)}, u32[]{:S(2)}, u32[]{:S(2)}) async-start(bf16[32,96,128]{2,1,0:T(8,128)(2,1)} %bitcast.5), calls=%async_computation | async-start | bytes 1572864 | tf_op jit(solution)/shard_map/all_to_all | solution.py:46
  13.1 0.6 fusion.9
  17.5 10.0 %all-to-all-done = bf16[32,96,128]{2,1,0:T(8,128)(2,1)S(1)} async-done(((bf16[32,96,128]{2,1,0:T(8,128)(2,1)}), bf16[32,96,128]{2,1,0:T(8,128)(2,1)S(1)}, u32[]{:S(2)}, u32[]{:S(2)}) %all-to-all-start) | async-done | bytes 786464 | tf_op jit(solution)/shard_map/all_to_all | solution.py:46
  27.5 0.7 copy.18
  28.2 13.0 %all-to-all-start.1 = ((bf16[16,2,6,128]{3,1,2,0:T(2,128)(2,1)}), bf16[16,2,6,128]{3,1,2,0:T(2,128)(2,1)S(1)}, u32[]{:S(2)}, u32[]{:S(2)}) async-start(bf16[16,2,6,128]{3,1,2,0:T(2,128)(2,1)} %bitcast.9), calls=%async_computation.1 | async-start | bytes 98304 | tf_op jit(solution)/shard_map/all_to_all | solution.py:46
  45.1 7.6 %all-to-all-done.1 = bf16[16,2,6,128]{3,1,2,0:T(2,128)(2,1)S(1)} async-done(((bf16[16,2,6,128]{3,1,2,0:T(2,128)(2,1)}), bf16[16,2,6,128]{3,1,2,0:T(2,128)(2,1)S(1)}, u32[]{:S(2)}, u32[]{:S(2)}) %all-to-all-start.1) | async-done | bytes 49184 | tf_op jit(solution)/shard_map/all_to_all | solution.py:46
  52.9 15.3 %all_to_all.25 = bf16[16,2,6,128]{3,1,2,0:T(2,128)(2,1)S(1)} all-to-all(bf16[16,2,6,128]{3,1,2,0:T(2,128)(2,1)S(1)} %broadcast_in_dim.25), channel_id=1, replica_groups=mesh['z'=16,'yl'=2,'x'=4,'yh'=2,'c'=2] {'z'}, dimensions={0} | all-to-all | bytes 98304 | tf_op jit(solution)/shard_map/all_to_all | solution.py:46
  68.3 1.1 broadcast_in_dim.27
  69.4 3.6 %all-to-all-start.3 = ((bf16[16,192,128]{2,1,0:T(8,128)(2,1)}), bf16[16,192,128]{2,1,0:T(8,128)(2,1)S(1)}, u32[]{:S(2)}, u32[]{:S(2)}) async-start(bf16[16,192,128]{2,1,0:T(8,128)(2,1)} %broadcast_in_dim.27), calls=%async_computation.3 | async-start | bytes 1572864 | tf_op jit(solution)/shard_map/all_to_all | solution.py:46
  73.3 11.1 %all-to-all-done.3.same = bf16[16,192,128]{2,1,0:T(8,128)(2,1)S(1)} async-done(((bf16[16,192,128]{2,1,0:T(8,128)(2,1)}), bf16[16,192,128]{2,1,0:T(8,128)(2,1)S(1)}, u32[]{:S(2)}, u32[]{:S(2)}) %all-to-all-start.3) | async-done | bytes 786464 | tf_op jit(solution)/shard_map/all_to_all | solution.py:46
  84.4 5.7 %collective-permute-start = (bf16[16,192,128]{2,1,0:T(8,128)(2,1)S(1)}, bf16[16,192,128]{2,1,0:T(8,128)(2,1)}, u32[]{:S(2)}, u32[]{:S(2)}) collective-permute-start(bf16[16,192,128]{2,1,0:T(8,128)(2,1)S(1)} %all-to-all-done.3.same), channel_id=1, source_target_pairs={{0,1},{1,0},{2,3},{3,2},{4,5},{5,4},{6,7},{7,6},{8,9},{9,8},{10,11... | collective-permute-start | bytes 2359304 | tf_op jit(solution)/shard_map/ppermute | solution.py:83
  90.1 0.1 select_convert_fusion.1
  91.0 0.3 shard_map.146.cond
  91.4 0.6 gather_fusion
  92.2 8.0 %shard_map.147 = bf16[160,128]{1,0:T(8,128)(2,1)S(1)} custom-call(s32[1]{0:T(128)} %bitcast.3.core, f32[2]{0:T(128)S(1)} %sqrt_multiply_fusion.scale, bf16[16,192,128]{2,1,0:T(8,128)(2,1)S(1)} %all-to-all-done.3.same, bf16[16,192,128]{2,1,0:T(8,128)(2,1)} %collective-permute-done.other, bf16[3072,128]{1,0:T(8,128)(2,1)S(1)} %shard_map.146.cond, ...), custom_call_target="tpu_custom_call" | custom-call | tf_op jit(solution)/shard_map/pallas_call | solution.py:288
  100.1 24.3 %all_gather.3.gathered = bf16[2560,128]{1,0:T(8,128)(2,1)S(1)} all-gather(bf16[160,128]{1,0:T(8,128)(2,1)S(1)} %shard_map.147), channel_id=1, replica_groups=mesh['z'=16,'yl'=2,'x'=4,'yh'=2,'c'=2] {'z'}, dimensions={0}, use_global_device_ids=true | all-gather | bytes 696320 | tf_op jit(solution)/shard_map/all_gather | solution.py:360
  124.4 1.4 shard_map.148
  125.8 30.9 %all_to_all.26.elems = bf16[16,320,128]{2,1,0:T(8,128)(2,1)S(1)} all-to-all(bf16[16,320,128]{2,1,0:T(8,128)(2,1)S(1)} %shard_map.148), channel_id=1, replica_groups=mesh['z'=16,'yl'=2,'x'=4,'yh'=2,'c'=2] {'x','yh','c'}, dimensions={0} | all-to-all | bytes 2621440 | tf_op jit(solution)/shard_map/all_to_all | solution.py:46
  156.7 2.5 %shard_map.149 = (f32[256,512]{1,0:T(8,128)S(1)}, bf16[256,512]{1,0:T(8,128)(2,1)S(1)}) custom-call(s32[3]{0:T(128)S(1)} %pad_add_fusion.block.me, bf16[16,320,128]{2,1,0:T(8,128)(2,1)S(1)} %all_to_all.26.elems, f32[16,512]{1,0:T(8,128)S(1)} %get-tuple-element.11.names, f32[16,512]{1,0:T(8,128)S(1)} %get-tuple-element.9.signs, f32[2,384,128]{2,1,0:T(8,128)S(1)} %copy-done.3), custom_call_target="tpu_custom_call" | custom-call | tf_op jit(solution)/shard_map/pallas_call | solution.py:340
  159.2 3.0 %collective-permute-start.1 = (bf16[256,512]{1,0:T(8,128)(2,1)S(1)}, bf16[256,512]{1,0:T(8,128)(2,1)S(1)}, u32[]{:S(2)}, u32[]{:S(2)}) collective-permute-start(bf16[256,512]{1,0:T(8,128)(2,1)S(1)} %get-tuple-element.8), channel_id=1, source_target_pairs={{0,16},{16,0},{1,17},{17,1},{2,18},{18,2},{3,19},{19,3},{4,20},{20... | collective-permute-start | bytes 786440 | tf_op jit(solution)/shard_map/ppermute | solution.py:364
  162.2 6.4 %collective-permute-done.1 = bf16[256,512]{1,0:T(8,128)(2,1)S(1)} collective-permute-done((bf16[256,512]{1,0:T(8,128)(2,1)S(1)}, bf16[256,512]{1,0:T(8,128)(2,1)S(1)}, u32[]{:S(2)}, u32[]{:S(2)}) %collective-permute-start.1) | collective-permute-done | bytes 262176 | tf_op jit(solution)/shard_map/ppermute | solution.py:364
  168.6 0.9 convert_add_fusion
  (54 shorter events, 0.7 us)
Async XLA Ops:
  0.0 91.3 %copy-start = (f32[512]{0:T(512)S(1)}, f32[512]{0:T(512)}, u32[]{:S(2)}) copy-start(f32[512]{0:T(512)} %param.17) | copy-start | bytes 6148
  0.0 1.4 copy-start.1
  1.4 11.7 %copy-start.13 = (s32[2]{0:T(128)S(1)}, s32[2]{0:T(128)}, u32[]{:S(2)}) copy-start(s32[2]{0:T(128)} %param.19) | copy-start | bytes 28
  2.6 24.9 %all-to-all-start = ((bf16[32,96,128]{2,1,0:T(8,128)(2,1)}), bf16[32,96,128]{2,1,0:T(8,128)(2,1)S(1)}, u32[]{:S(2)}, u32[]{:S(2)}) async-start(bf16[32,96,128]{2,1,0:T(8,128)(2,1)} %bitcast.5), calls=%async_computation | async-start | bytes 1572864 | tf_op jit(solution)/shard_map/all_to_all | solution.py:46
  28.2 24.6 %all-to-all-start.1 = ((bf16[16,2,6,128]{3,1,2,0:T(2,128)(2,1)}), bf16[16,2,6,128]{3,1,2,0:T(2,128)(2,1)S(1)}, u32[]{:S(2)}, u32[]{:S(2)}) async-start(bf16[16,2,6,128]{3,1,2,0:T(2,128)(2,1)} %bitcast.9), calls=%async_computation.1 | async-start | bytes 98304 | tf_op jit(solution)/shard_map/all_to_all | solution.py:46
  45.1 27.9 %copy-start.7 = (s32[8192]{0:T(1024)S(1)}, s32[8192]{0:T(1024)}, u32[]{:S(2)}) copy-start(s32[8192]{0:T(1024)} %param.20) | copy-start | bytes 98308
  68.3 21.8 %copy-start.8 = (s32[16,512]{1,0:T(8,128)S(1)}, s32[16,512]{1,0:T(8,128)}, u32[]{:S(2)}) copy-start(s32[16,512]{1,0:T(8,128)} %constant.139.clone) | copy-start | bytes 98308
  68.3 21.8 %copy-start.10 = (pred[16,512]{1,0:T(8,128)(4,1)S(1)}, pred[16,512]{1,0:T(8,128)(4,1)}, u32[]{:S(2)}) copy-start(pred[16,512]{1,0:T(8,128)(4,1)} %constant.138.clone) | copy-start | bytes 24580
  68.3 22.7 %copy-start.2 = (bf16[1,373248]{1,0:T(2,128)(2,1)S(1)}, bf16[1,373248]{1,0:T(2,128)(2,1)}, u32[]{:S(2)}) copy-start(bf16[1,373248]{1,0:T(2,128)(2,1)} %flat.3) | copy-start | bytes 2239492
  69.4 15.0 %all-to-all-start.3 = ((bf16[16,192,128]{2,1,0:T(8,128)(2,1)}), bf16[16,192,128]{2,1,0:T(8,128)(2,1)S(1)}, u32[]{:S(2)}, u32[]{:S(2)}) async-start(bf16[16,192,128]{2,1,0:T(8,128)(2,1)} %broadcast_in_dim.27), calls=%async_computation.3 | async-start | bytes 1572864 | tf_op jit(solution)/shard_map/all_to_all | solution.py:46
  84.4 7.7 %collective-permute-start = (bf16[16,192,128]{2,1,0:T(8,128)(2,1)S(1)}, bf16[16,192,128]{2,1,0:T(8,128)(2,1)}, u32[]{:S(2)}, u32[]{:S(2)}) collective-permute-start(bf16[16,192,128]{2,1,0:T(8,128)(2,1)S(1)} %all-to-all-done.3.same), channel_id=1, source_target_pairs={{0,1},{1,0},{2,3},{3,2},{4,5},{5,4},{6,7},{7,6},{8,9},{9,8},{10,11... | collective-permute-start | bytes 2359304 | tf_op jit(solution)/shard_map/ppermute | solution.py:83
  90.2 1.9 %copy-start.9 = (s32[16,384]{1,0:T(8,128)S(1)}, s32[16,384]{1,0:T(8,128)}, u32[]{:S(2)}) copy-start(s32[16,384]{1,0:T(8,128)} %constant.136.clone) | copy-start | bytes 73732
  90.2 1.9 %copy-start.11 = (pred[16,384]{1,0:T(8,128)(4,1)S(1)}, pred[16,384]{1,0:T(8,128)(4,1)}, u32[]{:S(2)}) copy-start(pred[16,384]{1,0:T(8,128)(4,1)} %constant.137.clone) | copy-start | bytes 18436
  90.2 1.9 %copy-start.12 = (pred[16,384]{1,0:T(8,128)(4,1)S(1)}, pred[16,384]{1,0:T(8,128)(4,1)}, u32[]{:S(2)}) copy-start(pred[16,384]{1,0:T(8,128)(4,1)} %constant.135.clone) | copy-start | bytes 18436
  90.9 1.3 copy-start.4
  90.9 1.3 copy-start.5
  90.9 1.3 copy-start.6
  125.8 30.9 %copy-start.3 = (f32[2,384,128]{2,1,0:T(8,128)S(1)}, f32[2,384,128]{2,1,0:T(8,128)}, u32[]{:S(2)}) copy-start(f32[2,384,128]{2,1,0:T(8,128)} %constant.143.clone.columns) | copy-start | bytes 1179652
  159.2 9.4 %collective-permute-start.1 = (bf16[256,512]{1,0:T(8,128)(2,1)S(1)}, bf16[256,512]{1,0:T(8,128)(2,1)S(1)}, u32[]{:S(2)}, u32[]{:S(2)}) collective-permute-start(bf16[256,512]{1,0:T(8,128)(2,1)S(1)} %get-tuple-element.8), channel_id=1, source_target_pairs={{0,16},{16,0},{1,17},{17,1},{2,18},{18,2},{3,19},{19,3},{4,20},{20... | collective-permute-start | bytes 786440 | tf_op jit(solution)/shard_map/ppermute | solution.py:364

commit v6 on v5

--- a/solution.py
+++ b/solution.py
@@ -37,8 +37,8 @@
 PAIR=GRID*GRID*2//LANES
 ROWS=GRID**3//LANES
 WIDE=16
-BACK=32
-SLOT=64
+BACK=16
+SLOT=32
 PAD_ROWS=40*PAIR
 
 
@@ -70,15 +70,12 @@
 
 
 def from_owners(shard, owner):
-    steps = owner.shape[0]
-    owner_z, owner_plane = owner // 32, owner % 32
     parts = exchange(in_rows(shard).reshape(32, CHUNK, LANES), PLANE)
-    parts = jnp.stack([lax.dynamic_index_in_dim(parts, owner_plane[s], 0, False) for s in range(steps)])
-    parts = parts.reshape(steps, 16, PIECE, LANES).transpose(1, 0, 2, 3)
-    parts = exchange(parts, "z")
-    parts = jnp.stack([lax.dynamic_index_in_dim(parts[:, s], owner_z[s], 0, False) for s in range(steps)])
-    parts = exchange(jnp.broadcast_to(parts[None], (16,) + parts.shape), "z")
-    parts = parts.transpose(1, 0, 2, 3).reshape(steps * CHUNK, LANES)
+    parts = [lax.dynamic_index_in_dim(parts, owner[s] & 31, 0, False) for s in range(STEPS)]
+    parts = lax.all_gather(jnp.concatenate(parts, axis=0), "z", axis=0, tiled=True)
+    parts = parts.reshape(16, STEPS, CHUNK, LANES)
+    parts = [lax.dynamic_index_in_dim(parts[:, s], owner[s] >> 5, 0, False) for s in range(STEPS)]
+    parts = jnp.concatenate(parts, axis=0)
     parts = exchange(jnp.broadcast_to(parts[None], (16,) + parts.shape), TILE)
     return parts, lax.ppermute(parts, "c", SWAP)
 
@@ -104,20 +101,22 @@
     h,l=split_np(t)
     first=np.concatenate([h,h,l],1)
     c,s=cs(np.arange(-REACH,REACH+1))
-    w=np.zeros((2,LANES,2,SLOT))
+    w=np.zeros((2,LANES,4,SLOT))
     w[0,:GRID,0,:KEPT]=c.T; w[0,:GRID,1,:KEPT]=-s.T
     w[1,:GRID,0,:KEPT]=s.T; w[1,:GRID,1,:KEPT]=c.T
+    w[:,:,2]=w[:,:,1]; w[:,:,3]=-w[:,:,0]
     w=w.reshape(2*LANES,LANES)
     h,l=split_np(w)
     third=np.concatenate([h,l],1)
-    u=np.zeros((2,BACK,GRID))
-    u[0,:KEPT]=c; u[1,:KEPT]=s
-    u=u.reshape(2*BACK,GRID)
+    u=np.zeros((2,2,BACK,GRID))
+    u[0,0,:REACH+1]=c[0::2]; u[0,1,:REACH]=c[1::2]
+    u[1,0,:REACH+1]=s[0::2]; u[1,1,:REACH]=s[1::2]
+    u=u.reshape(4*BACK,GRID)
     h,l=split_np(u)
     second=np.concatenate([h,h,l],1)
     return first,second,third
 
-def dft_kernel(core, scale, same, other, cond, first, second, third, places, out, vals, held, mixed, spread, lined):
+def dft_kernel(core, owner, val_energy, cond_energy, same, other, cond, first, second, third, places, out, vals, held, mixed, spread, lined):
     f32=jnp.float32; bf=jnp.bfloat16
     for s in range(STEPS):
         vals[s, 32 * CHUNK :, :] = jnp.zeros((PAD_ROWS - 32 * CHUNK, LANES), f32)
@@ -158,7 +157,11 @@
         z=jnp.dot(l,w[:,:LANES],preferred_element_type=f32)
         mixed[j0*32:(j0+group)*32,:]=y[:,:LANES]+y[:,LANES:]+z
     table=second[...]
-    flip=jnp.where(lax.broadcasted_iota(jnp.int32,(BACK,LANES),1)<SLOT,1.0,-1.0).astype(f32)
+    near = lax.broadcasted_iota(jnp.int32, (BACK, LANES), 1) < LANES // 2
+    factors = []
+    for s in range(STEPS):
+        gap = jnp.full((BACK, LANES), cond_energy[0] - val_energy[owner[s]], f32)
+        factors.append(jnp.sqrt(4.0 / gap) / math.sqrt(GRID**3))
     for i in range(REACH+1):
         cols=[]
         for s in range(STEPS):
@@ -168,22 +171,26 @@
         y=jnp.dot(table,jnp.concatenate(cols,1),preferred_element_type=f32)
         for s in range(STEPS):
             z=y[:,s*LANES:(s+1)*LANES]
-            r=(z[:BACK]+flip*pltpu.roll(z[BACK:],SLOT,1))*scale[s]
-            spread[s*LANES:(s+1)*LANES, i*BACK:(i+1)*BACK]=r.T.astype(bf)
+            r=z[:2*BACK]+pltpu.roll(z[2*BACK:],LANES//2,1)
+            r=jnp.where(near,r[:BACK],pltpu.roll(r[BACK:],LANES//2,1))*factors[s]
+            spread[i*BACK:(i+1)*BACK, s*LANES:(s+1)*LANES]=r
     rows = (REACH + 1) * BACK
-    data = spread[...]
+    data = spread[...].T.astype(bf)
     at = lax.broadcasted_iota(jnp.int32, (rows, WIDTH), 0)
     slot = lax.broadcasted_iota(jnp.int32, (SLOT, WIDTH), 0)
     gap = jnp.zeros((STEPS, 2 * LANES), f32)
     for b in range(BLOCKS):
         place = places[b : b + 1, :]
-        hot = jnp.where(at == (place >> 6), 1.0, 0.0).astype(bf)
+        hot = jnp.where(at == (place >> 7), 1.0, 0.0).astype(bf)
         y = jnp.dot(data, hot, preferred_element_type=f32)
         keep = slot == (place & (SLOT - 1))
-        got = [
-            jnp.sum(jnp.where(keep, y[p * SLOT : (p + 1) * SLOT], 0.0), 0, keepdims=True)
-            for p in range(2 * STEPS)
-        ]
+        even = (place & (LANES // 2)) == 0
+        got = []
+        for s in range(STEPS):
+            half = y[s * LANES : (s + 1) * LANES]
+            half = jnp.where(even, half[: LANES // 2], half[LANES // 2 :])
+            for part in (half[:SLOT], half[SLOT:]):
+                got.append(jnp.sum(jnp.where(keep, part, 0.0), 0, keepdims=True))
         real = jnp.concatenate([jnp.concatenate(got[0::2], 0), gap], 1)
         imag = pltpu.roll(jnp.concatenate(got[1::2], 0), WIDTH - SLOTS, 1)
         both = real + jnp.concatenate([gap, imag], 1)
@@ -217,6 +224,11 @@
         scratch_shapes=[pltpu.VMEM((16 * ELEMS, LANES), jnp.float32)],
         compiler_params=pltpu.CompilerParams(vmem_limit_bytes=32 * 2**20),
     )(block, gathered)
+
+
+def frequency_id(i, j, k):
+    j = j + REACH
+    return (i * BACK + (j >> 1)) * LANES + (j & 1) * (LANES // 2) + k + REACH
 
 
 def layout():
@@ -242,7 +254,7 @@
                 i, j, k = shell.T
                 front = (i > 0) | ((i == 0) & ((j > 0) | ((j == 0) & (k >= 0))))
                 i, j, k = shell[front].T
-                shells[b].append((i * BACK + j + REACH) * SLOT + k + REACH)
+                shells[b].append(frequency_id(i, j, k))
             elif low == b * SPAN:
                 begin[b] = high - low
             else:
@@ -262,7 +274,7 @@
         own[b] = np.where(kind[b] > 0, NAMED + places, own[b])
     columns = np.full((2, WIDTH, LANES), -5.0, np.float32)
     columns[0, :, :BLOCKS] = own.T
-    columns[1, SLOT:, :BLOCKS] = own.T[: WIDTH - SLOT]
+    columns[1, WIDTH - SLOTS :, :BLOCKS] = own.T[:SLOTS]
     return fixed.astype(np.int32), kind, target.astype(np.int32), columns
 
 
@@ -274,7 +286,7 @@
     i, j, k = [jnp.where(n < half, n, n - GRID) for n in (i, j, k)]
     front = (i > 0) | ((i == 0) & ((j > 0) | ((j == 0) & (k >= 0))))
     sign = jnp.where(front, 1, -1)
-    ids = (i * sign * BACK + j * sign + REACH) * SLOT + k * sign + REACH
+    ids = frequency_id(i * sign, j * sign, k * sign)
     first = ids[:, :WIDTH]
     last = jnp.pad(ids[:, SPAN - SLOTS :], ((0, 0), (0, WIDTH - SLOTS)))
     places = jnp.where(kind == 1, first, jnp.where(kind == 2, last, fixed))
@@ -282,35 +294,34 @@
     return places, names.astype(jnp.float32), sign.astype(jnp.float32)
 
 
-def pairs(psi, cond, scale, places, core):
+def pairs(psi, cond, core, owner, val_energy, cond_energy, places):
     first, second, third = [jnp.asarray(table) for table in (tables())]
     vm = pl.BlockSpec(memory_space=pltpu.VMEM)
     return pl.pallas_call(
         dft_kernel,
         out_shape=jax.ShapeDtypeStruct((ELEMS, LANES), jnp.bfloat16),
-        in_specs=[pl.BlockSpec(memory_space=pltpu.SMEM)] * 2 + [vm] * 7,
+        in_specs=[pl.BlockSpec(memory_space=pltpu.SMEM)] * 4 + [vm] * 7,
         out_specs=vm,
         scratch_shapes=[
             pltpu.VMEM((STEPS, PAD_ROWS, LANES), jnp.float32),
             pltpu.VMEM((STEPS, 2 * WIDE, 41 * LANES), jnp.float32),
             pltpu.VMEM((GRID * 32, LANES), jnp.float32),
-            pltpu.VMEM((STEPS * LANES, (REACH + 1) * BACK), jnp.bfloat16),
+            pltpu.VMEM(((REACH + 1) * BACK, STEPS * LANES), jnp.float32),
             pltpu.VMEM((ELEMS, LANES), jnp.float32),
         ],
         compiler_params=pltpu.CompilerParams(vmem_limit_bytes=48 * 2**20),
-    )(core, scale, *psi, cond, first, second, third, places)
-
-
-def sums_kernel(me, elems, names, signs, columns, here, away):
+    )(core, owner, val_energy, cond_energy, *psi, cond, first, second, third, places)
+
+
+def sums_kernel(me, elems, names, signs, columns, out):
     f32, bf = jnp.float32, jnp.bfloat16
     z, m, yl = [me[n] for n in range(3)]
     half = SPAN // 2
 
-    def spread(block, swapped):
+    def spread(block, side):
         name, sign = names[pl.ds(block, 1), :], signs[pl.ds(block, 1), :]
-        if swapped is not None:
-            turn = lambda x: jnp.where(swapped, jnp.concatenate([x[:, half:], x[:, :half]], 1), x)
-            name, sign = turn(name), turn(sign)
+        if side is not None:
+            name, sign = [jnp.where(side == 0, x[:, :half], x[:, half:]) for x in (name, sign)]
         chosen = lax.broadcasted_iota(jnp.int32, (WIDTH, LANES), 1) == block
         place = [jnp.sum(jnp.where(chosen, columns[p], 0.0), 1, keepdims=True) for p in range(2)]
         real = jnp.where(place[0] == name, 1.0, 0.0).astype(bf)
@@ -324,27 +335,22 @@
         imag = jnp.dot(jnp.concatenate(tiles[2:], 1), hot[1], preferred_element_type=f32)
         return real.astype(bf), imag.astype(bf)
 
-    left = widened([lanes(BOTH + n) for n in range(BOTH)], spread(z, yl == 1))
+    left = widened([lanes(BOTH + n) for n in range(BOTH)], spread(z, yl))
     right = widened([lanes(n) for n in range(BOTH)], spread(m, None))
     over = (((0,), (0,)), ((), ()))
     total = lax.dot_general(left[0], right[0], over, preferred_element_type=f32)
     total += lax.dot_general(left[1], right[1], over, preferred_element_type=f32)
-    total *= -1.0 / math.sqrt(STEPS * 512)
-    here[...] = total[:half]
-    away[...] = total[half:].astype(bf)
-
-
-def sums(me, elems, names, signs):
+    out[...] = (total * (-1.0 / math.sqrt(STEPS * 512))).astype(out.dtype)
+
+
+def sums(me, elems, names, signs, dtype):
     vm = pl.BlockSpec(memory_space=pltpu.VMEM)
-    half = SPAN // 2
     return pl.pallas_call(
         sums_kernel,
-        out_shape=[
-            jax.ShapeDtypeStruct((half, SPAN), jnp.float32),
-            jax.ShapeDtypeStruct((half, SPAN), jnp.bfloat16),
-        ],
+        out_shape=jax.ShapeDtypeStruct((SPAN // 2, SPAN), dtype),
         in_specs=[pl.BlockSpec(memory_space=pltpu.SMEM)] + [vm] * 4,
-        out_specs=[vm, vm],
+        out_specs=vm,
+        cost_estimate=pl.CostEstimate(flops=10**9, bytes_accessed=2 * 2**20, transcendentals=0),
         compiler_params=pltpu.CompilerParams(vmem_limit_bytes=48 * 2**20),
     )(me, elems, names, signs, jnp.asarray(layout()[3]))
 
@@ -352,16 +358,18 @@
 def body(valence, conduction, val_energy, cond_energy, owner, g_index):
     psi = from_owners(valence, owner)
     cond = in_rows(conduction)
-    scale = jnp.sqrt(4.0 / (cond_energy[0] - val_energy[owner])) / math.sqrt(GRID**3)
     places, names, signs = frequencies(g_index)
     core = lax.axis_index("c").astype(jnp.int32)
-    elems = pairs(psi, cond, scale, places, core[None])
+    elems = pairs(psi, cond, core[None], owner, val_energy, cond_energy, places)
 
     elems = lax.all_gather(elems, "z", axis=0, tiled=True)
-    me = jnp.stack([lax.axis_index(a) for a in ("z", COL, "yl")]).astype(jnp.int32)
+    place = [lax.axis_index(a) for a in ("z", COL, "yl")]
+    me = jnp.stack(place).astype(jnp.int32)
+    partner = jnp.stack(place[:2] + [1 - place[2]]).astype(jnp.int32)
     elems = exchange(turn(me, elems), COL)
-    here, away = sums(me, elems, names, signs)
-    return here + lax.ppermute(away, "yl", SWAP).astype(jnp.float32)
+    away = sums(partner, elems, names, signs, jnp.bfloat16)
+    away = lax.ppermute(away, "yl", SWAP)
+    return sums(me, elems, names, signs, jnp.float32) + away.astype(jnp.float32)
 
 
 def solution(mesh):

time: 170 us -> 161 us (0.947)
  blocking collectives: 70.4 us -> 54 us
  waiting for transfers between devices: 35.1 us -> 46.4 us
  between operations: 8.86 us -> 3.65 us
  starting transfers between devices: 35.7 us -> 37.9 us
    all_to_all x2 -> x0, blocking collectives: 46.2 us -> none  [exchange(): return lax.all_to_all(x, axis, split_axis=0, concat_axis=0, tiled=True)]
    all_gather x0 -> x1, blocking collectives: none -> 31.1 us  [from_owners(): lax.all_gather(jnp.concatenate(parts, axis=0), 'z', axis=0, tiled=True)]
    all_to_all x3, waiting for transfers between devices: 28.7 us -> 40.3 us  [exchange(): return lax.all_to_all(x, axis, split_axis=0, concat_axis=0, tiled=True)]
    ppermute x1, starting transfers between devices: 5.67 us -> 10.4 us  [from_owners(): return (parts, lax.ppermute(parts, 'c', SWAP))]
    pallas_call x1, Pallas kernels: 7.97 us -> 6.05 us  [pairs(): pl.pallas_call(dft_kernel, out_shape=jax.ShapeDtypeStruct((ELEMS, LANES),...]
    all_to_all x3, starting transfers between devices: 27 us -> 25.3 us  [exchange(): return lax.all_to_all(x, axis, split_axis=0, concat_axis=0, tiled=True)]
    pallas_call x1 -> x2, Pallas kernels: 2.49 us -> 3.98 us  [sums(): pl.pallas_call(sums_kernel, out_shape=jax.ShapeDtypeStruct((SPAN // 2, SP...]
  transfers between devices with their start and end apart: 5 -> 5, of which waited for: 4 -> 5; matrix products, arithmetic and copies ran while one was open for 1% -> 1% of each run, Pallas kernels for 0% -> 1%
where the time goes in v6:
time: 161 us
  blocking collectives  54 us (34%)
  waiting for transfers between devices  46.4 us (29%)
  starting transfers between devices  37.9 us (24%)
  Pallas kernels  14.1 us (9%)
  between operations  3.65 us (2%)
  local copies, waits for them, and re-layouts  3.38 us (2%)
    all_to_all x3, waiting for transfers between devices, exchange(): return lax.all_to_all(x, axis, split_axis=0, concat_axis=0, tiled=True)  40.3 us
    all_gather x1, blocking collectives, from_owners(): lax.all_gather(jnp.concatenate(parts, axis=0), 'z', axis=0, tiled=True)  31.1 us
    all_to_all x3, starting transfers between devices, exchange(): return lax.all_to_all(x, axis, split_axis=0, concat_axis=0, tiled=True)  25.3 us
    all_gather x1, blocking collectives, body(): elems = lax.all_gather(elems, 'z', axis=0, tiled=True)  22.9 us
    ppermute x1, starting transfers between devices, from_owners(): return (parts, lax.ppermute(parts, 'c', SWAP))  10.4 us
    pallas_call x1, Pallas kernels, pairs(): pl.pallas_call(dft_kernel, out_shape=jax.ShapeDtypeStruct((ELEMS, LANES),...  6.05 us
    ppermute x1, waiting for transfers between devices, body(): away = lax.ppermute(away, 'yl', SWAP)  4.72 us
    pallas_call x2, Pallas kernels, sums(): pl.pallas_call(sums_kernel, out_shape=jax.ShapeDtypeStruct((SPAN // 2, SP...  3.98 us
  transfers between devices with their start and end apart: 5, of which 5 were waited for; matrix products, arithmetic and copies ran while one was open for 1% of the time, Pallas kernels for 1%

profile of v6, /device:TPU:1, one launch (start us, length us, event | category | flops | bytes accessed | tf_op | source)
XLA Modules:
  0.0 160.6 jit_solution(3323943082520523994)
XLA Ops:
  0.0 1.4 copy-done
  1.4 1.2 shard_map.154
  2.6 10.4 %all-to-all-start = ((bf16[32,96,128]{2,1,0:T(8,128)(2,1)}), bf16[32,96,128]{2,1,0:T(8,128)(2,1)S(1)}, u32[]{:S(2)}, u32[]{:S(2)}) async-start(bf16[32,96,128]{2,1,0:T(8,128)(2,1)} %bitcast.4), calls=%async_computation | async-start | bytes 1572864 | tf_op jit(solution)/shard_map/all_to_all | solution.py:46
  13.0 0.7 fusion.10
  16.4 11.1 %all-to-all-done = bf16[32,96,128]{2,1,0:T(8,128)(2,1)S(1)} async-done(((bf16[32,96,128]{2,1,0:T(8,128)(2,1)}), bf16[32,96,128]{2,1,0:T(8,128)(2,1)S(1)}, u32[]{:S(2)}, u32[]{:S(2)}) %all-to-all-start) | async-done | bytes 786464 | tf_op jit(solution)/shard_map/all_to_all | solution.py:46
  27.5 31.1 %all_gather.6 = bf16[3072,128]{1,0:T(8,128)(2,1)S(1)} all-gather(bf16[192,128]{1,0:T(8,128)(2,1)S(1)} %pad_maximum_fusion), channel_id=1, replica_groups=mesh['z'=16,'yl'=2,'x'=4,'yh'=2,'c'=2] {'z'}, dimensions={0}, use_global_device_ids=true | all-gather | bytes 835584 | tf_op jit(solution)/shard_map/all_gather | solution.py:75
  58.7 1.0 broadcast_in_dim.14
  59.8 3.6 %all-to-all-start.1 = ((bf16[16,192,128]{2,1,0:T(8,128)(2,1)}), bf16[16,192,128]{2,1,0:T(8,128)(2,1)S(1)}, u32[]{:S(2)}, u32[]{:S(2)}) async-start(bf16[16,192,128]{2,1,0:T(8,128)(2,1)} %broadcast_in_dim.14), calls=%async_computation.1 | async-start | bytes 1572864 | tf_op jit(solution)/shard_map/all_to_all | solution.py:46
  64.3 9.3 %all-to-all-done.1.same = bf16[16,192,128]{2,1,0:T(8,128)(2,1)S(1)} async-done(((bf16[16,192,128]{2,1,0:T(8,128)(2,1)}), bf16[16,192,128]{2,1,0:T(8,128)(2,1)S(1)}, u32[]{:S(2)}, u32[]{:S(2)}) %all-to-all-start.1) | async-done | bytes 786464 | tf_op jit(solution)/shard_map/all_to_all | solution.py:46
  73.7 10.4 %collective-permute-start = (bf16[16,192,128]{2,1,0:T(8,128)(2,1)S(1)}, bf16[16,192,128]{2,1,0:T(8,128)(2,1)}, u32[]{:S(2)}, u32[]{:S(2)}) collective-permute-start(bf16[16,192,128]{2,1,0:T(8,128)(2,1)S(1)} %all-to-all-done.1.same), channel_id=1, source_target_pairs={{0,1},{1,0},{2,3},{3,2},{4,5},{5,4},{6,7},{7,6},{8,9},{9,8},{10,11... | collective-permute-start | bytes 2359304 | tf_op jit(solution)/shard_map/ppermute | solution.py:80
  84.2 0.1 select_convert_fusion.1
  84.4 0.3 shard_map.155.cond
  84.7 0.1 pad_add_fusion.block.me
  84.8 1.3 collective-permute-done.other
  86.2 6.0 %shard_map.156 = bf16[160,128]{1,0:T(8,128)(2,1)S(1)} custom-call(s32[1]{0:T(128)} %bitcast.3.core, s32[2]{0:T(128)S(1)} %copy-done.5, f32[512]{0:T(512)S(1)} %copy-done.6, f32[1]{0:T(128)S(6)} %copy.17.cond_energy, bf16[16,192,128]{2,1,0:T(8,128)(2,1)S(1)} %all-to-all-done.1.same, bf16[16,192,128]{2,1,0:T(8,128)(2,1)} %collective-permute-done.other, ...), custom_call_target="tpu_custom_call" | custom-call | tf_op jit(solution)/shard_map/pallas_call | solution.py:300
  92.2 22.9 %all_gather.7.gathered = bf16[2560,128]{1,0:T(8,128)(2,1)S(1)} all-gather(bf16[160,128]{1,0:T(8,128)(2,1)S(1)} %shard_map.156), channel_id=1, replica_groups=mesh['z'=16,'yl'=2,'x'=4,'yh'=2,'c'=2] {'z'}, dimensions={0}, use_global_device_ids=true | all-gather | bytes 696320 | tf_op jit(solution)/shard_map/all_gather | solution.py:365
  115.1 2.5 %shard_map.157 = bf16[16,320,128]{2,1,0:T(8,128)(2,1)} custom-call(s32[3]{0:T(128)S(1)} %pad_add_fusion.block.me, bf16[2560,128]{1,0:T(8,128)(2,1)S(1)} %all_gather.7.gathered), custom_call_target="tpu_custom_call" | custom-call | tf_op jit(solution)/shard_map/pallas_call | solution.py:219
  117.6 11.3 %all-to-all-start.2 = ((bf16[16,320,128]{2,1,0:T(8,128)(2,1)}), bf16[16,320,128]{2,1,0:T(8,128)(2,1)S(1)}, u32[]{:S(2)}, u32[]{:S(2)}) async-start(bf16[16,320,128]{2,1,0:T(8,128)(2,1)} %shard_map.157), calls=%async_computation.2 | async-start | bytes 2621440 | tf_op jit(solution)/shard_map/all_to_all | solution.py:46
  128.9 19.9 %all-to-all-done.2.elems = bf16[16,320,128]{2,1,0:T(8,128)(2,1)S(1)} async-done(((bf16[16,320,128]{2,1,0:T(8,128)(2,1)}), bf16[16,320,128]{2,1,0:T(8,128)(2,1)S(1)}, u32[]{:S(2)}, u32[]{:S(2)}) %all-to-all-start.2) | async-done | bytes 1310752 | tf_op jit(solution)/shard_map/all_to_all | solution.py:46
  148.9 2.0 %shard_map.159 = bf16[256,512]{1,0:T(8,128)(2,1)S(1)} custom-call(s32[3]{0:T(128)S(1)} %pad_add_fusion.2.me, bf16[16,320,128]{2,1,0:T(8,128)(2,1)S(1)} %all-to-all-done.2.elems, f32[16,512]{1,0:T(8,128)S(1)} %get-tuple-element.7.names, f32[16,512]{1,0:T(8,128)S(1)} %get-tuple-element.5.signs, f32[2,384,128]{2,1,0:T(8,128)S(1)} %copy-done.7), custom_call_target="tpu_custom_call" | custom-call | flops 1000000000 | bytes 2097152 | tf_op jit(solution)/shard_map/pallas_call | solution.py:348
  150.8 2.1 %collective-permute-start.1 = (bf16[256,512]{1,0:T(8,128)(2,1)S(1)}, bf16[256,512]{1,0:T(8,128)(2,1)S(1)}, u32[]{:S(2)}, u32[]{:S(2)}) collective-permute-start(bf16[256,512]{1,0:T(8,128)(2,1)S(1)} %shard_map.159), channel_id=1, source_target_pairs={{0,16},{16,0},{1,17},{17,1},{2,18},{18,2},{3,19},{19,3},{4,20},{20... | collective-permute-start | bytes 786440 | tf_op jit(solution)/shard_map/ppermute | solution.py:371
  153.0 2.0 %shard_map.158 = f32[256,512]{1,0:T(8,128)S(1)} custom-call(s32[3]{0:T(128)S(1)} %pad_add_fusion.block.me, bf16[16,320,128]{2,1,0:T(8,128)(2,1)S(1)} %all-to-all-done.2.elems, f32[16,512]{1,0:T(8,128)S(1)} %get-tuple-element.7.names, f32[16,512]{1,0:T(8,128)S(1)} %get-tuple-element.5.signs, f32[2,384,128]{2,1,0:T(8,128)S(1)} %copy-done.7), custom_call_target="tpu_custom_call" | custom-call | flops 1000000000 | bytes 2097152 | tf_op jit(solution)/shard_map/pallas_call | solution.py:348
  155.0 4.7 %collective-permute-done.1 = bf16[256,512]{1,0:T(8,128)(2,1)S(1)} collective-permute-done((bf16[256,512]{1,0:T(8,128)(2,1)S(1)}, bf16[256,512]{1,0:T(8,128)(2,1)S(1)}, u32[]{:S(2)}, u32[]{:S(2)}) %collective-permute-start.1) | collective-permute-done | bytes 262176 | tf_op jit(solution)/shard_map/ppermute | solution.py:371
  159.7 0.9 convert_add_fusion
  (43 shorter events, 0.5 us)
Async XLA Ops:
  0.0 1.4 copy-start
  1.4 11.7 %copy-start.5 = (s32[2]{0:T(128)S(1)}, s32[2]{0:T(128)}, u32[]{:S(2)}) copy-start(s32[2]{0:T(128)} %owner.1) | copy-start | bytes 28
  2.6 24.9 %all-to-all-start = ((bf16[32,96,128]{2,1,0:T(8,128)(2,1)}), bf16[32,96,128]{2,1,0:T(8,128)(2,1)S(1)}, u32[]{:S(2)}, u32[]{:S(2)}) async-start(bf16[32,96,128]{2,1,0:T(8,128)(2,1)} %bitcast.4), calls=%async_computation | async-start | bytes 1572864 | tf_op jit(solution)/shard_map/all_to_all | solution.py:46
  58.6 5.4 %copy-start.8 = (s32[8192]{0:T(1024)S(1)}, s32[8192]{0:T(1024)}, u32[]{:S(2)}) copy-start(s32[8192]{0:T(1024)} %param.21) | copy-start | bytes 98308
  58.7 25.5 %copy-start.9 = (s32[16,512]{1,0:T(8,128)S(1)}, s32[16,512]{1,0:T(8,128)}, u32[]{:S(2)}) copy-start(s32[16,512]{1,0:T(8,128)} %constant.118.clone) | copy-start | bytes 98308
  58.7 25.5 %copy-start.11 = (pred[16,512]{1,0:T(8,128)(4,1)S(1)}, pred[16,512]{1,0:T(8,128)(4,1)}, u32[]{:S(2)}) copy-start(pred[16,512]{1,0:T(8,128)(4,1)} %constant.117.clone) | copy-start | bytes 24580
  58.7 25.7 %copy-start.1 = (bf16[1,373248]{1,0:T(2,128)(2,1)S(1)}, bf16[1,373248]{1,0:T(2,128)(2,1)}, u32[]{:S(2)}) copy-start(bf16[1,373248]{1,0:T(2,128)(2,1)} %flat.3) | copy-start | bytes 2239492
  59.8 13.9 %all-to-all-start.1 = ((bf16[16,192,128]{2,1,0:T(8,128)(2,1)}), bf16[16,192,128]{2,1,0:T(8,128)(2,1)S(1)}, u32[]{:S(2)}, u32[]{:S(2)}) async-start(bf16[16,192,128]{2,1,0:T(8,128)(2,1)} %broadcast_in_dim.14), calls=%async_computation.1 | async-start | bytes 1572864 | tf_op jit(solution)/shard_map/all_to_all | solution.py:46
  64.2 20.6 %copy-start.10 = (s32[16,384]{1,0:T(8,128)S(1)}, s32[16,384]{1,0:T(8,128)}, u32[]{:S(2)}) copy-start(s32[16,384]{1,0:T(8,128)} %constant.115.clone) | copy-start | bytes 73732
  64.2 20.6 %copy-start.12 = (pred[16,384]{1,0:T(8,128)(4,1)S(1)}, pred[16,384]{1,0:T(8,128)(4,1)}, u32[]{:S(2)}) copy-start(pred[16,384]{1,0:T(8,128)(4,1)} %constant.116.clone) | copy-start | bytes 18436
  64.2 20.6 %copy-start.13 = (pred[16,384]{1,0:T(8,128)(4,1)S(1)}, pred[16,384]{1,0:T(8,128)(4,1)}, u32[]{:S(2)}) copy-start(pred[16,384]{1,0:T(8,128)(4,1)} %constant.114.clone) | copy-start | bytes 18436
  64.2 21.9 %copy-start.2 = (bf16[256,256]{1,0:T(8,128)(2,1)S(1)}, bf16[256,256]{1,0:T(8,128)(2,1)}, u32[]{:S(2)}) copy-start(bf16[256,256]{1,0:T(8,128)(2,1)} %constant.121.clone.third) | copy-start | bytes 393220
  64.3 21.9 %copy-start.3 = (bf16[64,216]{1,0:T(8,128)(2,1)S(1)}, bf16[64,216]{1,0:T(8,128)(2,1)}, u32[]{:S(2)}) copy-start(bf16[64,216]{1,0:T(8,128)(2,1)} %constant.120.clone.second) | copy-start | bytes 82948
  64.3 21.9 %copy-start.4 = (bf16[32,240]{1,0:T(8,128)(2,1)S(1)}, bf16[32,240]{1,0:T(8,128)(2,1)}, u32[]{:S(2)}) copy-start(bf16[32,240]{1,0:T(8,128)(2,1)} %constant.119.clone.first) | copy-start | bytes 46084
  64.3 21.9 %copy-start.6 = (f32[512]{0:T(512)S(1)}, f32[512]{0:T(512)}, u32[]{:S(2)}) copy-start(f32[512]{0:T(512)} %val_energy.1) | copy-start | bytes 6148
  73.7 12.5 %collective-permute-start = (bf16[16,192,128]{2,1,0:T(8,128)(2,1)S(1)}, bf16[16,192,128]{2,1,0:T(8,128)(2,1)}, u32[]{:S(2)}, u32[]{:S(2)}) collective-permute-start(bf16[16,192,128]{2,1,0:T(8,128)(2,1)S(1)} %all-to-all-done.1.same), channel_id=1, source_target_pairs={{0,1},{1,0},{2,3},{3,2},{4,5},{5,4},{6,7},{7,6},{8,9},{9,8},{10,11... | collective-permute-start | bytes 2359304 | tf_op jit(solution)/shard_map/ppermute | solution.py:80
  117.6 31.3 %copy-start.7 = (f32[2,384,128]{2,1,0:T(8,128)S(1)}, f32[2,384,128]{2,1,0:T(8,128)}, u32[]{:S(2)}) copy-start(f32[2,384,128]{2,1,0:T(8,128)} %constant.122.clone.columns) | copy-start | bytes 1179652
  117.6 31.3 %all-to-all-start.2 = ((bf16[16,320,128]{2,1,0:T(8,128)(2,1)}), bf16[16,320,128]{2,1,0:T(8,128)(2,1)S(1)}, u32[]{:S(2)}, u32[]{:S(2)}) async-start(bf16[16,320,128]{2,1,0:T(8,128)(2,1)} %shard_map.157), calls=%async_computation.2 | async-start | bytes 2621440 | tf_op jit(solution)/shard_map/all_to_all | solution.py:46
  150.8 8.8 %collective-permute-start.1 = (bf16[256,512]{1,0:T(8,128)(2,1)S(1)}, bf16[256,512]{1,0:T(8,128)(2,1)S(1)}, u32[]{:S(2)}, u32[]{:S(2)}) collective-permute-start(bf16[256,512]{1,0:T(8,128)(2,1)S(1)} %shard_map.159), channel_id=1, source_target_pairs={{0,16},{16,0},{1,17},{17,1},{2,18},{18,2},{3,19},{19,3},{4,20},{20... | collective-permute-start | bytes 786440 | tf_op jit(solution)/shard_map/ppermute | solution.py:371

commit v7 on v6

--- a/solution.py
+++ b/solution.py
@@ -1,3 +1,4 @@
+import functools
 import math
 
 import jax
@@ -69,7 +70,7 @@
     )(flat)
 
 
-def from_owners(shard, owner):
+def from_owners(shard, owner, late):
     parts = exchange(in_rows(shard).reshape(32, CHUNK, LANES), PLANE)
     parts = [lax.dynamic_index_in_dim(parts, owner[s] & 31, 0, False) for s in range(STEPS)]
     parts = lax.all_gather(jnp.concatenate(parts, axis=0), "z", axis=0, tiled=True)
@@ -77,7 +78,8 @@
     parts = [lax.dynamic_index_in_dim(parts[:, s], owner[s] >> 5, 0, False) for s in range(STEPS)]
     parts = jnp.concatenate(parts, axis=0)
     parts = exchange(jnp.broadcast_to(parts[None], (16,) + parts.shape), TILE)
-    return parts, lax.ppermute(parts, "c", SWAP)
+    parts, late = lax.optimization_barrier((parts, late))
+    return (parts, lax.ppermute(parts, "c", SWAP)), late
 
 
 def split(x):
@@ -116,12 +118,13 @@
     second=np.concatenate([h,h,l],1)
     return first,second,third
 
-def dft_kernel(core, owner, val_energy, cond_energy, same, other, cond, first, second, third, places, out, vals, held, mixed, spread, lined):
+def dft_kernel(owner, val_energy, cond_energy, same, other, cond, first, second, third, places, out, vals, held, mixed, spread, lined):
     f32=jnp.float32; bf=jnp.bfloat16
+    core = lax.axis_index("c")
     for s in range(STEPS):
         vals[s, 32 * CHUNK :, :] = jnp.zeros((PAD_ROWS - 32 * CHUNK, LANES), f32)
         for t in range(16):
-            for psi, side in ((same, core[0]), (other, 1 - core[0])):
+            for psi, side in ((same, core), (other, 1 - core)):
                 here = pl.ds(pl.multiple_of((2 * t + side) * CHUNK, CHUNK), CHUNK)
                 band = psi[t, s * CHUNK : (s + 1) * CHUNK, :].astype(f32)
                 vals[s, here, :] = band * cond[here, :].astype(f32)
@@ -201,7 +204,7 @@
     out[...] = lined[...].astype(bf)
 
 
-def turn_kernel(block, gathered, out, rows):
+def turn_kernel(gathered, out, rows):
     rows[...] = gathered[...].astype(jnp.float32)
     for b in range(BLOCKS):
         for line in range(LINES):
@@ -209,21 +212,21 @@
             got = rows[pl.ds(line * BLOCKS + b, 16, stride=ELEMS), :]
             to = (n * STEPS + s) * 16
             out[b, to : to + 16, :] = got.astype(jnp.bfloat16)
-    chosen = out[block[0], :ELEMS, :]
+    chosen = out[lax.axis_index("z"), :ELEMS, :]
     for b in range(BLOCKS):
         out[b, ELEMS:, :] = chosen
 
 
-def turn(block, gathered):
+def turn(gathered):
     vm = pl.BlockSpec(memory_space=pltpu.VMEM)
     return pl.pallas_call(
         turn_kernel,
         out_shape=jax.ShapeDtypeStruct((BLOCKS, 2 * ELEMS, LANES), jnp.bfloat16),
-        in_specs=[pl.BlockSpec(memory_space=pltpu.SMEM), vm],
+        in_specs=[vm],
         out_specs=vm,
         scratch_shapes=[pltpu.VMEM((16 * ELEMS, LANES), jnp.float32)],
         compiler_params=pltpu.CompilerParams(vmem_limit_bytes=32 * 2**20),
-    )(block, gathered)
+    )(gathered)
 
 
 def frequency_id(i, j, k):
@@ -294,13 +297,13 @@
     return places, names.astype(jnp.float32), sign.astype(jnp.float32)
 
 
-def pairs(psi, cond, core, owner, val_energy, cond_energy, places):
+def pairs(psi, cond, owner, val_energy, cond_energy, places):
     first, second, third = [jnp.asarray(table) for table in (tables())]
     vm = pl.BlockSpec(memory_space=pltpu.VMEM)
     return pl.pallas_call(
         dft_kernel,
         out_shape=jax.ShapeDtypeStruct((ELEMS, LANES), jnp.bfloat16),
-        in_specs=[pl.BlockSpec(memory_space=pltpu.SMEM)] * 4 + [vm] * 7,
+        in_specs=[pl.BlockSpec(memory_space=pltpu.SMEM)] * 3 + [vm] * 7,
         out_specs=vm,
         scratch_shapes=[
             pltpu.VMEM((STEPS, PAD_ROWS, LANES), jnp.float32),
@@ -310,12 +313,14 @@
             pltpu.VMEM((ELEMS, LANES), jnp.float32),
         ],
         compiler_params=pltpu.CompilerParams(vmem_limit_bytes=48 * 2**20),
-    )(core, owner, val_energy, cond_energy, *psi, cond, first, second, third, places)
-
-
-def sums_kernel(me, elems, names, signs, columns, out):
+    )(owner, val_energy, cond_energy, *psi, cond, first, second, third, places)
+
+
+def sums_kernel(partner, elems, names, signs, columns, out):
     f32, bf = jnp.float32, jnp.bfloat16
-    z, m, yl = [me[n] for n in range(3)]
+    z, yl = lax.axis_index("z"), lax.axis_index("yl")
+    m = (lax.axis_index("x") * 2 + lax.axis_index("yh")) * 2 + lax.axis_index("c")
+    yl = 1 - yl if partner else yl
     half = SPAN // 2
 
     def spread(block, side):
@@ -343,33 +348,28 @@
     out[...] = (total * (-1.0 / math.sqrt(STEPS * 512))).astype(out.dtype)
 
 
-def sums(me, elems, names, signs, dtype):
+def sums(elems, names, signs, partner):
     vm = pl.BlockSpec(memory_space=pltpu.VMEM)
     return pl.pallas_call(
-        sums_kernel,
-        out_shape=jax.ShapeDtypeStruct((SPAN // 2, SPAN), dtype),
-        in_specs=[pl.BlockSpec(memory_space=pltpu.SMEM)] + [vm] * 4,
+        functools.partial(sums_kernel, partner),
+        out_shape=jax.ShapeDtypeStruct((SPAN // 2, SPAN), jnp.bfloat16 if partner else jnp.float32),
+        in_specs=[vm] * 4,
         out_specs=vm,
         cost_estimate=pl.CostEstimate(flops=10**9, bytes_accessed=2 * 2**20, transcendentals=0),
         compiler_params=pltpu.CompilerParams(vmem_limit_bytes=48 * 2**20),
-    )(me, elems, names, signs, jnp.asarray(layout()[3]))
+    )(elems, names, signs, jnp.asarray(layout()[3]))
 
 
 def body(valence, conduction, val_energy, cond_energy, owner, g_index):
-    psi = from_owners(valence, owner)
+    psi, g_index = from_owners(valence, owner, g_index)
     cond = in_rows(conduction)
     places, names, signs = frequencies(g_index)
-    core = lax.axis_index("c").astype(jnp.int32)
-    elems = pairs(psi, cond, core[None], owner, val_energy, cond_energy, places)
+    elems = pairs(psi, cond, owner, val_energy, cond_energy, places)
 
     elems = lax.all_gather(elems, "z", axis=0, tiled=True)
-    place = [lax.axis_index(a) for a in ("z", COL, "yl")]
-    me = jnp.stack(place).astype(jnp.int32)
-    partner = jnp.stack(place[:2] + [1 - place[2]]).astype(jnp.int32)
-    elems = exchange(turn(me, elems), COL)
-    away = sums(partner, elems, names, signs, jnp.bfloat16)
-    away = lax.ppermute(away, "yl", SWAP)
-    return sums(me, elems, names, signs, jnp.float32) + away.astype(jnp.float32)
+    elems = exchange(turn(elems), COL)
+    away = lax.ppermute(sums(elems, names, signs, True), "yl", SWAP)
+    return sums(elems, names, signs, False) + away.astype(jnp.float32)
 
 
 def solution(mesh):

time: 161 us -> 159 us (0.988)
  blocking collectives: 54 us -> 85.2 us
  waiting for transfers between devices: 46.4 us -> 27.5 us
  starting transfers between devices: 37.9 us -> 26.6 us
  Pallas kernels: 14.1 us -> 11 us
    all_to_all x0 -> x1, blocking collectives: none -> 31.2 us  [exchange(): return lax.all_to_all(x, axis, split_axis=0, concat_axis=0, tiled=True)]
    all_to_all x3 -> x2, waiting for transfers between devices: 40.3 us -> 20.2 us  [exchange(): return lax.all_to_all(x, axis, split_axis=0, concat_axis=0, tiled=True)]
    all_to_all x3 -> x2, starting transfers between devices: 25.3 us -> 14.1 us  [exchange(): return lax.all_to_all(x, axis, split_axis=0, concat_axis=0, tiled=True)]
    pallas_call x1, Pallas kernels: 2.5 us -> 0.88 us  [turn(): pl.pallas_call(turn_kernel, out_shape=jax.ShapeDtypeStruct((BLOCKS, 2 * E...]
  transfers between devices with their start and end apart: 5 -> 4, of which waited for: 5 -> 4; matrix products, arithmetic and copies ran while one was open for 1% -> 1% of each run, Pallas kernels for 1% -> 1%
where the time goes in v7:
time: 159 us; the launch traced here: 158 us
  blocking collectives  85.2 us (54%)
  waiting for transfers between devices  27.5 us (17%)
  starting transfers between devices  26.6 us (17%)
  Pallas kernels  11 us (7%)
  between operations  3.65 us (2%)
  local copies, waits for them, and re-layouts  3.37 us (2%)
    all_to_all x1, blocking collectives, exchange(): return lax.all_to_all(x, axis, split_axis=0, concat_axis=0, tiled=True)  31.2 us
    all_gather x1, blocking collectives, from_owners(): lax.all_gather(jnp.concatenate(parts, axis=0), 'z', axis=0, tiled=True)  31.1 us
    all_gather x1, blocking collectives, body(): elems = lax.all_gather(elems, 'z', axis=0, tiled=True)  22.9 us
    all_to_all x2, waiting for transfers between devices, exchange(): return lax.all_to_all(x, axis, split_axis=0, concat_axis=0, tiled=True)  20.2 us
    all_to_all x2, starting transfers between devices, exchange(): return lax.all_to_all(x, axis, split_axis=0, concat_axis=0, tiled=True)  14.1 us
    ppermute x1, starting transfers between devices, from_owners(): return ((parts, lax.ppermute(parts, 'c', SWAP)), late)  10.5 us
    ppermute x1, waiting for transfers between devices, body(): away = lax.ppermute(sums(elems, names, signs, True), 'yl', SWAP)  5.79 us
    pallas_call x1, Pallas kernels, pairs(): pl.pallas_call(dft_kernel, out_shape=jax.ShapeDtypeStruct((ELEMS, LANES),...  5.71 us
  transfers between devices with their start and end apart: 4, of which 4 were waited for; matrix products, arithmetic and copies ran while one was open for 1% of the time, Pallas kernels for 1%

profile of v7, /device:TPU:1, one launch (start us, length us, event | category | flops | bytes accessed | tf_op | source)
XLA Modules:
  0.0 158.4 jit_solution(363956891676585629)
XLA Ops:
  0.0 1.4 copy-done
  1.4 1.2 shard_map.154
  2.6 10.4 %all-to-all-start = ((bf16[32,96,128]{2,1,0:T(8,128)(2,1)}), bf16[32,96,128]{2,1,0:T(8,128)(2,1)S(1)}, u32[]{:S(2)}, u32[]{:S(2)}) async-start(bf16[32,96,128]{2,1,0:T(8,128)(2,1)} %bitcast), calls=%async_computation | async-start | bytes 1572864 | tf_op jit(solution)/shard_map/all_to_all | solution.py:47
  13.0 0.7 fusion.10
  16.4 11.1 %all-to-all-done = bf16[32,96,128]{2,1,0:T(8,128)(2,1)S(1)} async-done(((bf16[32,96,128]{2,1,0:T(8,128)(2,1)}), bf16[32,96,128]{2,1,0:T(8,128)(2,1)S(1)}, u32[]{:S(2)}, u32[]{:S(2)}) %all-to-all-start) | async-done | bytes 786464 | tf_op jit(solution)/shard_map/all_to_all | solution.py:47
  27.5 31.1 %all_gather.6 = bf16[3072,128]{1,0:T(8,128)(2,1)S(1)} all-gather(bf16[192,128]{1,0:T(8,128)(2,1)S(1)} %pad_maximum_fusion), channel_id=1, replica_groups=mesh['z'=16,'yl'=2,'x'=4,'yh'=2,'c'=2] {'z'}, dimensions={0}, use_global_device_ids=true | all-gather | bytes 835584 | tf_op jit(solution)/shard_map/all_gather | solution.py:76
  58.7 1.0 broadcast_in_dim.4
  59.7 3.6 %all-to-all-start.1 = ((bf16[16,192,128]{2,1,0:T(8,128)(2,1)}), bf16[16,192,128]{2,1,0:T(8,128)(2,1)S(1)}, u32[]{:S(2)}, u32[]{:S(2)}) async-start(bf16[16,192,128]{2,1,0:T(8,128)(2,1)} %broadcast_in_dim.4), calls=%async_computation.1 | async-start | bytes 1572864 | tf_op jit(solution)/shard_map/all_to_all | solution.py:47
  64.1 0.3 shard_map.155.cond
  64.5 9.1 %all-to-all-done.1.same = bf16[16,192,128]{2,1,0:T(8,128)(2,1)S(1)} async-done(((bf16[16,192,128]{2,1,0:T(8,128)(2,1)}), bf16[16,192,128]{2,1,0:T(8,128)(2,1)S(1)}, u32[]{:S(2)}, u32[]{:S(2)}) %all-to-all-start.1) | async-done | bytes 786464 | tf_op jit(solution)/shard_map/all_to_all | solution.py:47
  73.6 10.5 %collective-permute-start = (bf16[16,192,128]{2,1,0:T(8,128)(2,1)S(1)}, bf16[16,192,128]{2,1,0:T(8,128)(2,1)S(1)}, u32[]{:S(2)}, u32[]{:S(2)}) collective-permute-start(bf16[16,192,128]{2,1,0:T(8,128)(2,1)S(1)} %all-to-all-done.1.same), channel_id=1, source_target_pairs={{0,1},{1,0},{2,3},{3,2},{4,5},{5,4},{6,7},{7,6},{8,9},{9,8},{10,11... | collective-permute-start | bytes 2359304 | tf_op jit(solution)/shard_map/ppermute | solution.py:82
  84.3 0.1 select_convert_fusion
  84.3 0.1 select_convert_fusion.1
  84.4 0.1 slice.29
  84.5 1.5 collective-permute-done.other
  86.0 5.7 %shard_map.156 = bf16[160,128]{1,0:T(8,128)(2,1)S(1)} custom-call(s32[2]{0:T(128)S(1)} %copy-done.5, f32[512]{0:T(512)S(1)} %copy-done.6, f32[1]{0:T(128)S(6)} %copy.17.cond_energy, bf16[16,192,128]{2,1,0:T(8,128)(2,1)S(1)} %all-to-all-done.1.same, bf16[16,192,128]{2,1,0:T(8,128)(2,1)S(1)} %collective-permute-done.other, ...), custom_call_target="tpu_custom_call" | custom-call | tf_op jit(solution)/shard_map/pallas_call | solution.py:303
  91.7 22.9 %all_gather.7.gathered = bf16[2560,128]{1,0:T(8,128)(2,1)S(1)} all-gather(bf16[160,128]{1,0:T(8,128)(2,1)S(1)} %shard_map.156), channel_id=1, replica_groups=mesh['z'=16,'yl'=2,'x'=4,'yh'=2,'c'=2] {'z'}, dimensions={0}, use_global_device_ids=true | all-gather | bytes 696320 | tf_op jit(solution)/shard_map/all_gather | solution.py:369
  114.6 0.9 shard_map.157
  115.5 31.2 %all_to_all.15.elems = bf16[16,320,128]{2,1,0:T(8,128)(2,1)S(1)} all-to-all(bf16[16,320,128]{2,1,0:T(8,128)(2,1)S(1)} %shard_map.157), channel_id=1, replica_groups=mesh['z'=16,'yl'=2,'x'=4,'yh'=2,'c'=2] {'x','yh','c'}, dimensions={0} | all-to-all | bytes 2621440 | tf_op jit(solution)/shard_map/all_to_all | solution.py:47
  146.7 1.5 shard_map.159
  148.1 2.1 %collective-permute-start.1 = (bf16[256,512]{1,0:T(8,128)(2,1)S(1)}, bf16[256,512]{1,0:T(8,128)(2,1)S(1)}, u32[]{:S(2)}, u32[]{:S(2)}) collective-permute-start(bf16[256,512]{1,0:T(8,128)(2,1)S(1)} %shard_map.159), channel_id=1, source_target_pairs={{0,16},{16,0},{1,17},{17,1},{2,18},{18,2},{3,19},{19,3},{4,20},{20... | collective-permute-start | bytes 786440 | tf_op jit(solution)/shard_map/ppermute | solution.py:371
  150.3 1.5 shard_map.158
  151.7 5.8 %collective-permute-done.1 = bf16[256,512]{1,0:T(8,128)(2,1)S(1)} collective-permute-done((bf16[256,512]{1,0:T(8,128)(2,1)S(1)}, bf16[256,512]{1,0:T(8,128)(2,1)S(1)}, u32[]{:S(2)}, u32[]{:S(2)}) %collective-permute-start.1) | collective-permute-done | bytes 262176 | tf_op jit(solution)/shard_map/ppermute | solution.py:371
  157.5 0.9 convert_add_fusion
  (40 shorter events, 0.3 us)
Async XLA Ops:
  0.0 1.4 copy-start
  1.4 11.7 %copy-start.5 = (s32[2]{0:T(128)S(1)}, s32[2]{0:T(128)}, u32[]{:S(2)}) copy-start(s32[2]{0:T(128)} %owner.1) | copy-start | bytes 28
  2.6 24.9 %all-to-all-start = ((bf16[32,96,128]{2,1,0:T(8,128)(2,1)}), bf16[32,96,128]{2,1,0:T(8,128)(2,1)S(1)}, u32[]{:S(2)}, u32[]{:S(2)}) async-start(bf16[32,96,128]{2,1,0:T(8,128)(2,1)} %bitcast), calls=%async_computation | async-start | bytes 1572864 | tf_op jit(solution)/shard_map/all_to_all | solution.py:47
  58.6 5.4 %copy-start.1 = (bf16[1,373248]{1,0:T(2,128)(2,1)S(1)}, bf16[1,373248]{1,0:T(2,128)(2,1)}, u32[]{:S(2)}) copy-start(bf16[1,373248]{1,0:T(2,128)(2,1)} %flat.3) | copy-start | bytes 2239492
  59.7 13.9 %all-to-all-start.1 = ((bf16[16,192,128]{2,1,0:T(8,128)(2,1)}), bf16[16,192,128]{2,1,0:T(8,128)(2,1)S(1)}, u32[]{:S(2)}, u32[]{:S(2)}) async-start(bf16[16,192,128]{2,1,0:T(8,128)(2,1)} %broadcast_in_dim.4), calls=%async_computation.1 | async-start | bytes 1572864 | tf_op jit(solution)/shard_map/all_to_all | solution.py:47
  63.3 10.3 %copy-start.8 = (s32[8192]{0:T(1024)S(1)}, s32[8192]{0:T(1024)}, u32[]{:S(2)}) copy-start(s32[8192]{0:T(1024)} %param.21) | copy-start | bytes 98308
  63.4 21.0 %copy-start.9 = (s32[16,512]{1,0:T(8,128)S(1)}, s32[16,512]{1,0:T(8,128)}, u32[]{:S(2)}) copy-start(s32[16,512]{1,0:T(8,128)} %constant.94.clone) | copy-start | bytes 98308
  63.4 21.0 %copy-start.11 = (pred[16,512]{1,0:T(8,128)(4,1)S(1)}, pred[16,512]{1,0:T(8,128)(4,1)}, u32[]{:S(2)}) copy-start(pred[16,512]{1,0:T(8,128)(4,1)} %constant.93.clone) | copy-start | bytes 24580
  64.1 20.4 %copy-start.10 = (s32[16,384]{1,0:T(8,128)S(1)}, s32[16,384]{1,0:T(8,128)}, u32[]{:S(2)}) copy-start(s32[16,384]{1,0:T(8,128)} %constant.91.clone) | copy-start | bytes 73732
  64.1 20.4 %copy-start.12 = (pred[16,384]{1,0:T(8,128)(4,1)S(1)}, pred[16,384]{1,0:T(8,128)(4,1)}, u32[]{:S(2)}) copy-start(pred[16,384]{1,0:T(8,128)(4,1)} %constant.92.clone) | copy-start | bytes 18436
  64.1 20.4 %copy-start.13 = (pred[16,384]{1,0:T(8,128)(4,1)S(1)}, pred[16,384]{1,0:T(8,128)(4,1)}, u32[]{:S(2)}) copy-start(pred[16,384]{1,0:T(8,128)(4,1)} %constant.90.clone) | copy-start | bytes 18436
  64.1 21.9 %copy-start.2 = (bf16[256,256]{1,0:T(8,128)(2,1)S(1)}, bf16[256,256]{1,0:T(8,128)(2,1)}, u32[]{:S(2)}) copy-start(bf16[256,256]{1,0:T(8,128)(2,1)} %constant.97.clone.third) | copy-start | bytes 393220
  64.1 21.9 %copy-start.3 = (bf16[64,216]{1,0:T(8,128)(2,1)S(1)}, bf16[64,216]{1,0:T(8,128)(2,1)}, u32[]{:S(2)}) copy-start(bf16[64,216]{1,0:T(8,128)(2,1)} %constant.96.clone.second) | copy-start | bytes 82948
  64.1 21.9 %copy-start.4 = (bf16[32,240]{1,0:T(8,128)(2,1)S(1)}, bf16[32,240]{1,0:T(8,128)(2,1)}, u32[]{:S(2)}) copy-start(bf16[32,240]{1,0:T(8,128)(2,1)} %constant.95.clone.first) | copy-start | bytes 46084
  64.1 21.9 %copy-start.6 = (f32[512]{0:T(512)S(1)}, f32[512]{0:T(512)}, u32[]{:S(2)}) copy-start(f32[512]{0:T(512)} %val_energy.1) | copy-start | bytes 6148
  73.6 12.4 %collective-permute-start = (bf16[16,192,128]{2,1,0:T(8,128)(2,1)S(1)}, bf16[16,192,128]{2,1,0:T(8,128)(2,1)S(1)}, u32[]{:S(2)}, u32[]{:S(2)}) collective-permute-start(bf16[16,192,128]{2,1,0:T(8,128)(2,1)S(1)} %all-to-all-done.1.same), channel_id=1, source_target_pairs={{0,1},{1,0},{2,3},{3,2},{4,5},{5,4},{6,7},{7,6},{8,9},{9,8},{10,11... | collective-permute-start | bytes 2359304 | tf_op jit(solution)/shard_map/ppermute | solution.py:82
  115.5 31.2 %copy-start.7 = (f32[2,384,128]{2,1,0:T(8,128)S(1)}, f32[2,384,128]{2,1,0:T(8,128)}, u32[]{:S(2)}) copy-start(f32[2,384,128]{2,1,0:T(8,128)} %constant.98.clone.columns) | copy-start | bytes 1179652
  148.1 9.4 %collective-permute-start.1 = (bf16[256,512]{1,0:T(8,128)(2,1)S(1)}, bf16[256,512]{1,0:T(8,128)(2,1)S(1)}, u32[]{:S(2)}, u32[]{:S(2)}) collective-permute-start(bf16[256,512]{1,0:T(8,128)(2,1)S(1)} %shard_map.159), channel_id=1, source_target_pairs={{0,16},{16,0},{1,17},{17,1},{2,18},{18,2},{3,19},{19,3},{4,20},{20... | collective-permute-start | bytes 786440 | tf_op jit(solution)/shard_map/ppermute | solution.py:371

commit v8 on v7

--- a/solution.py
+++ b/solution.py
@@ -147,7 +147,7 @@
         for s in range(STEPS):
             held[s,:,t*LANES:(t+1)*LANES]=y[:,s*LANES:(s+1)*LANES]
     w=third[...]
-    group=8
+    group=GRID
     for j0 in range(0,GRID,group):
         parts=[[],[]]
         for j in range(j0,j0+group):

time: 159 us -> 158 us (level)
  no operation moved by 1% of the time
where the time goes in v8:
time: 158 us
  blocking collectives  85.2 us (54%)
  waiting for transfers between devices  27.5 us (17%)
  starting transfers between devices  26.6 us (17%)
  Pallas kernels  10.6 us (7%)
  between operations  3.64 us (2%)
  local copies, waits for them, and re-layouts  3.37 us (2%)
    all_to_all x1, blocking collectives, exchange(): return lax.all_to_all(x, axis, split_axis=0, concat_axis=0, tiled=True)  31.2 us
    all_gather x1, blocking collectives, from_owners(): lax.all_gather(jnp.concatenate(parts, axis=0), 'z', axis=0, tiled=True)  31.1 us
    all_gather x1, blocking collectives, body(): elems = lax.all_gather(elems, 'z', axis=0, tiled=True)  22.9 us
    all_to_all x2, waiting for transfers between devices, exchange(): return lax.all_to_all(x, axis, split_axis=0, concat_axis=0, tiled=True)  20.2 us
    all_to_all x2, starting transfers between devices, exchange(): return lax.all_to_all(x, axis, split_axis=0, concat_axis=0, tiled=True)  14.1 us
    ppermute x1, starting transfers between devices, from_owners(): return ((parts, lax.ppermute(parts, 'c', SWAP)), late)  10.5 us
    ppermute x1, waiting for transfers between devices, body(): away = lax.ppermute(sums(elems, names, signs, True), 'yl', SWAP)  5.79 us
    pallas_call x1, Pallas kernels, pairs(): pl.pallas_call(dft_kernel, out_shape=jax.ShapeDtypeStruct((ELEMS, LANES),...  5.26 us
  transfers between devices with their start and end apart: 4, of which 4 were waited for; matrix products, arithmetic and copies ran while one was open for 1% of the time, Pallas kernels for 1%

profile of v8, /device:TPU:1, one launch (start us, length us, event | category | flops | bytes accessed | tf_op | source)
XLA Modules:
  0.0 157.9 jit_solution(11395854457423020723)
XLA Ops:
  0.0 1.4 copy-done
  1.4 1.2 shard_map.154
  2.6 10.4 %all-to-all-start = ((bf16[32,96,128]{2,1,0:T(8,128)(2,1)}), bf16[32,96,128]{2,1,0:T(8,128)(2,1)S(1)}, u32[]{:S(2)}, u32[]{:S(2)}) async-start(bf16[32,96,128]{2,1,0:T(8,128)(2,1)} %bitcast), calls=%async_computation | async-start | bytes 1572864 | tf_op jit(solution)/shard_map/all_to_all | solution.py:47
  13.0 0.7 fusion.10
  16.4 11.1 %all-to-all-done = bf16[32,96,128]{2,1,0:T(8,128)(2,1)S(1)} async-done(((bf16[32,96,128]{2,1,0:T(8,128)(2,1)}), bf16[32,96,128]{2,1,0:T(8,128)(2,1)S(1)}, u32[]{:S(2)}, u32[]{:S(2)}) %all-to-all-start) | async-done | bytes 786464 | tf_op jit(solution)/shard_map/all_to_all | solution.py:47
  27.5 31.1 %all_gather.6 = bf16[3072,128]{1,0:T(8,128)(2,1)S(1)} all-gather(bf16[192,128]{1,0:T(8,128)(2,1)S(1)} %pad_maximum_fusion), channel_id=1, replica_groups=mesh['z'=16,'yl'=2,'x'=4,'yh'=2,'c'=2] {'z'}, dimensions={0}, use_global_device_ids=true | all-gather | bytes 835584 | tf_op jit(solution)/shard_map/all_gather | solution.py:76
  58.7 1.0 broadcast_in_dim.4
  59.7 3.6 %all-to-all-start.1 = ((bf16[16,192,128]{2,1,0:T(8,128)(2,1)}), bf16[16,192,128]{2,1,0:T(8,128)(2,1)S(1)}, u32[]{:S(2)}, u32[]{:S(2)}) async-start(bf16[16,192,128]{2,1,0:T(8,128)(2,1)} %broadcast_in_dim.4), calls=%async_computation.1 | async-start | bytes 1572864 | tf_op jit(solution)/shard_map/all_to_all | solution.py:47
  64.1 0.3 shard_map.155.cond
  64.5 9.1 %all-to-all-done.1.same = bf16[16,192,128]{2,1,0:T(8,128)(2,1)S(1)} async-done(((bf16[16,192,128]{2,1,0:T(8,128)(2,1)}), bf16[16,192,128]{2,1,0:T(8,128)(2,1)S(1)}, u32[]{:S(2)}, u32[]{:S(2)}) %all-to-all-start.1) | async-done | bytes 786464 | tf_op jit(solution)/shard_map/all_to_all | solution.py:47
  73.6 10.5 %collective-permute-start = (bf16[16,192,128]{2,1,0:T(8,128)(2,1)S(1)}, bf16[16,192,128]{2,1,0:T(8,128)(2,1)S(1)}, u32[]{:S(2)}, u32[]{:S(2)}) collective-permute-start(bf16[16,192,128]{2,1,0:T(8,128)(2,1)S(1)} %all-to-all-done.1.same), channel_id=1, source_target_pairs={{0,1},{1,0},{2,3},{3,2},{4,5},{5,4},{6,7},{7,6},{8,9},{9,8},{10,11... | collective-permute-start | bytes 2359304 | tf_op jit(solution)/shard_map/ppermute | solution.py:82
  84.3 0.1 select_convert_fusion
  84.3 0.1 select_convert_fusion.1
  84.4 0.1 slice.29
  84.5 1.5 collective-permute-done.other
  86.0 5.3 %shard_map.156 = bf16[160,128]{1,0:T(8,128)(2,1)S(1)} custom-call(s32[2]{0:T(128)S(1)} %copy-done.5, f32[512]{0:T(512)S(1)} %copy-done.6, f32[1]{0:T(128)S(6)} %copy.17.cond_energy, bf16[16,192,128]{2,1,0:T(8,128)(2,1)S(1)} %all-to-all-done.1.same, bf16[16,192,128]{2,1,0:T(8,128)(2,1)S(1)} %collective-permute-done.other, ...), custom_call_target="tpu_custom_call" | custom-call | tf_op jit(solution)/shard_map/pallas_call | solution.py:303
  91.3 22.9 %all_gather.7.gathered = bf16[2560,128]{1,0:T(8,128)(2,1)S(1)} all-gather(bf16[160,128]{1,0:T(8,128)(2,1)S(1)} %shard_map.156), channel_id=1, replica_groups=mesh['z'=16,'yl'=2,'x'=4,'yh'=2,'c'=2] {'z'}, dimensions={0}, use_global_device_ids=true | all-gather | bytes 696320 | tf_op jit(solution)/shard_map/all_gather | solution.py:369
  114.2 0.9 shard_map.157
  115.1 31.2 %all_to_all.15.elems = bf16[16,320,128]{2,1,0:T(8,128)(2,1)S(1)} all-to-all(bf16[16,320,128]{2,1,0:T(8,128)(2,1)S(1)} %shard_map.157), channel_id=1, replica_groups=mesh['z'=16,'yl'=2,'x'=4,'yh'=2,'c'=2] {'x','yh','c'}, dimensions={0} | all-to-all | bytes 2621440 | tf_op jit(solution)/shard_map/all_to_all | solution.py:47
  146.2 1.5 shard_map.159
  147.7 2.1 %collective-permute-start.1 = (bf16[256,512]{1,0:T(8,128)(2,1)S(1)}, bf16[256,512]{1,0:T(8,128)(2,1)S(1)}, u32[]{:S(2)}, u32[]{:S(2)}) collective-permute-start(bf16[256,512]{1,0:T(8,128)(2,1)S(1)} %shard_map.159), channel_id=1, source_target_pairs={{0,16},{16,0},{1,17},{17,1},{2,18},{18,2},{3,19},{19,3},{4,20},{20... | collective-permute-start | bytes 786440 | tf_op jit(solution)/shard_map/ppermute | solution.py:371
  149.8 1.5 shard_map.158
  151.3 5.8 %collective-permute-done.1 = bf16[256,512]{1,0:T(8,128)(2,1)S(1)} collective-permute-done((bf16[256,512]{1,0:T(8,128)(2,1)S(1)}, bf16[256,512]{1,0:T(8,128)(2,1)S(1)}, u32[]{:S(2)}, u32[]{:S(2)}) %collective-permute-start.1) | collective-permute-done | bytes 262176 | tf_op jit(solution)/shard_map/ppermute | solution.py:371
  157.1 0.9 convert_add_fusion
  (40 shorter events, 0.3 us)
Async XLA Ops:
  0.0 1.4 copy-start
  1.4 11.7 %copy-start.5 = (s32[2]{0:T(128)S(1)}, s32[2]{0:T(128)}, u32[]{:S(2)}) copy-start(s32[2]{0:T(128)} %owner.1) | copy-start | bytes 28
  2.6 24.9 %all-to-all-start = ((bf16[32,96,128]{2,1,0:T(8,128)(2,1)}), bf16[32,96,128]{2,1,0:T(8,128)(2,1)S(1)}, u32[]{:S(2)}, u32[]{:S(2)}) async-start(bf16[32,96,128]{2,1,0:T(8,128)(2,1)} %bitcast), calls=%async_computation | async-start | bytes 1572864 | tf_op jit(solution)/shard_map/all_to_all | solution.py:47
  58.6 5.4 %copy-start.1 = (bf16[1,373248]{1,0:T(2,128)(2,1)S(1)}, bf16[1,373248]{1,0:T(2,128)(2,1)}, u32[]{:S(2)}) copy-start(bf16[1,373248]{1,0:T(2,128)(2,1)} %flat.3) | copy-start | bytes 2239492
  59.7 13.9 %all-to-all-start.1 = ((bf16[16,192,128]{2,1,0:T(8,128)(2,1)}), bf16[16,192,128]{2,1,0:T(8,128)(2,1)S(1)}, u32[]{:S(2)}, u32[]{:S(2)}) async-start(bf16[16,192,128]{2,1,0:T(8,128)(2,1)} %broadcast_in_dim.4), calls=%async_computation.1 | async-start | bytes 1572864 | tf_op jit(solution)/shard_map/all_to_all | solution.py:47
  63.3 10.3 %copy-start.8 = (s32[8192]{0:T(1024)S(1)}, s32[8192]{0:T(1024)}, u32[]{:S(2)}) copy-start(s32[8192]{0:T(1024)} %param.21) | copy-start | bytes 98308
  63.4 21.0 %copy-start.9 = (s32[16,512]{1,0:T(8,128)S(1)}, s32[16,512]{1,0:T(8,128)}, u32[]{:S(2)}) copy-start(s32[16,512]{1,0:T(8,128)} %constant.94.clone) | copy-start | bytes 98308
  63.4 21.0 %copy-start.11 = (pred[16,512]{1,0:T(8,128)(4,1)S(1)}, pred[16,512]{1,0:T(8,128)(4,1)}, u32[]{:S(2)}) copy-start(pred[16,512]{1,0:T(8,128)(4,1)} %constant.93.clone) | copy-start | bytes 24580
  64.1 20.4 %copy-start.10 = (s32[16,384]{1,0:T(8,128)S(1)}, s32[16,384]{1,0:T(8,128)}, u32[]{:S(2)}) copy-start(s32[16,384]{1,0:T(8,128)} %constant.91.clone) | copy-start | bytes 73732
  64.1 20.4 %copy-start.12 = (pred[16,384]{1,0:T(8,128)(4,1)S(1)}, pred[16,384]{1,0:T(8,128)(4,1)}, u32[]{:S(2)}) copy-start(pred[16,384]{1,0:T(8,128)(4,1)} %constant.92.clone) | copy-start | bytes 18436
  64.1 20.4 %copy-start.13 = (pred[16,384]{1,0:T(8,128)(4,1)S(1)}, pred[16,384]{1,0:T(8,128)(4,1)}, u32[]{:S(2)}) copy-start(pred[16,384]{1,0:T(8,128)(4,1)} %constant.90.clone) | copy-start | bytes 18436
  64.1 21.9 %copy-start.2 = (bf16[256,256]{1,0:T(8,128)(2,1)S(1)}, bf16[256,256]{1,0:T(8,128)(2,1)}, u32[]{:S(2)}) copy-start(bf16[256,256]{1,0:T(8,128)(2,1)} %constant.97.clone.third) | copy-start | bytes 393220
  64.1 21.9 %copy-start.3 = (bf16[64,216]{1,0:T(8,128)(2,1)S(1)}, bf16[64,216]{1,0:T(8,128)(2,1)}, u32[]{:S(2)}) copy-start(bf16[64,216]{1,0:T(8,128)(2,1)} %constant.96.clone.second) | copy-start | bytes 82948
  64.1 21.9 %copy-start.4 = (bf16[32,240]{1,0:T(8,128)(2,1)S(1)}, bf16[32,240]{1,0:T(8,128)(2,1)}, u32[]{:S(2)}) copy-start(bf16[32,240]{1,0:T(8,128)(2,1)} %constant.95.clone.first) | copy-start | bytes 46084
  64.1 21.9 %copy-start.6 = (f32[512]{0:T(512)S(1)}, f32[512]{0:T(512)}, u32[]{:S(2)}) copy-start(f32[512]{0:T(512)} %val_energy.1) | copy-start | bytes 6148
  73.6 12.4 %collective-permute-start = (bf16[16,192,128]{2,1,0:T(8,128)(2,1)S(1)}, bf16[16,192,128]{2,1,0:T(8,128)(2,1)S(1)}, u32[]{:S(2)}, u32[]{:S(2)}) collective-permute-start(bf16[16,192,128]{2,1,0:T(8,128)(2,1)S(1)} %all-to-all-done.1.same), channel_id=1, source_target_pairs={{0,1},{1,0},{2,3},{3,2},{4,5},{5,4},{6,7},{7,6},{8,9},{9,8},{10,11... | collective-permute-start | bytes 2359304 | tf_op jit(solution)/shard_map/ppermute | solution.py:82
  115.0 31.2 %copy-start.7 = (f32[2,384,128]{2,1,0:T(8,128)S(1)}, f32[2,384,128]{2,1,0:T(8,128)}, u32[]{:S(2)}) copy-start(f32[2,384,128]{2,1,0:T(8,128)} %constant.98.clone.columns) | copy-start | bytes 1179652
  147.7 9.4 %collective-permute-start.1 = (bf16[256,512]{1,0:T(8,128)(2,1)S(1)}, bf16[256,512]{1,0:T(8,128)(2,1)S(1)}, u32[]{:S(2)}, u32[]{:S(2)}) collective-permute-start(bf16[256,512]{1,0:T(8,128)(2,1)S(1)} %shard_map.159), channel_id=1, source_target_pairs={{0,16},{16,0},{1,17},{17,1},{2,18},{18,2},{3,19},{19,3},{4,20},{20... | collective-permute-start | bytes 786440 | tf_op jit(solution)/shard_map/ppermute | solution.py:371

commit v9 on v8

--- a/solution.py
+++ b/solution.py
@@ -1,4 +1,3 @@
-import functools
 import math
 
 import jax
@@ -78,7 +77,7 @@
     parts = [lax.dynamic_index_in_dim(parts[:, s], owner[s] >> 5, 0, False) for s in range(STEPS)]
     parts = jnp.concatenate(parts, axis=0)
     parts = exchange(jnp.broadcast_to(parts[None], (16,) + parts.shape), TILE)
-    parts, late = lax.optimization_barrier((parts, late))
+    parts, *late = lax.optimization_barrier((parts, *late))
     return (parts, lax.ppermute(parts, "c", SWAP)), late
 
 
@@ -316,11 +315,10 @@
     )(owner, val_energy, cond_energy, *psi, cond, first, second, third, places)
 
 
-def sums_kernel(partner, elems, names, signs, columns, out):
-    f32, bf = jnp.float32, jnp.bfloat16
+def spreads_kernel(names, signs, columns, *outs):
+    bf = jnp.bfloat16
     z, yl = lax.axis_index("z"), lax.axis_index("yl")
     m = (lax.axis_index("x") * 2 + lax.axis_index("yh")) * 2 + lax.axis_index("c")
-    yl = 1 - yl if partner else yl
     half = SPAN // 2
 
     def spread(block, side):
@@ -332,44 +330,64 @@
         real = jnp.where(place[0] == name, 1.0, 0.0).astype(bf)
         return real, jnp.where(place[1] == name, sign, 0.0).astype(bf)
 
+    made = spread(m, None) + spread(z, 1 - yl) + spread(z, yl)
+    for out, hot in zip(outs, made):
+        out[...] = hot
+
+
+def spreads(names, signs):
+    vm = pl.BlockSpec(memory_space=pltpu.VMEM)
+    widths = [SPAN] * 2 + [SPAN // 2] * 4
+    return pl.pallas_call(
+        spreads_kernel,
+        out_shape=[jax.ShapeDtypeStruct((WIDTH, n), jnp.bfloat16) for n in widths],
+        in_specs=[vm] * 3,
+        out_specs=[vm] * 6,
+        compiler_params=pltpu.CompilerParams(vmem_limit_bytes=32 * 2**20),
+    )(names, signs, jnp.asarray(layout()[3]))
+
+
+def sums_kernel(elems, col_re, col_im, row_re, row_im, out):
+    f32, bf = jnp.float32, jnp.bfloat16
+
     def lanes(n):
         return elems[:, n * 32 : (n + 1) * 32, :].reshape(-1, LANES)
 
     def widened(tiles, hot):
-        real = jnp.dot(jnp.concatenate(tiles[:3], 1), hot[0], preferred_element_type=f32)
-        imag = jnp.dot(jnp.concatenate(tiles[2:], 1), hot[1], preferred_element_type=f32)
+        real = jnp.dot(jnp.concatenate(tiles[:3], 1), hot[0][...], preferred_element_type=f32)
+        imag = jnp.dot(jnp.concatenate(tiles[2:], 1), hot[1][...], preferred_element_type=f32)
         return real.astype(bf), imag.astype(bf)
 
-    left = widened([lanes(BOTH + n) for n in range(BOTH)], spread(z, yl))
-    right = widened([lanes(n) for n in range(BOTH)], spread(m, None))
+    left = widened([lanes(BOTH + n) for n in range(BOTH)], (row_re, row_im))
+    right = widened([lanes(n) for n in range(BOTH)], (col_re, col_im))
     over = (((0,), (0,)), ((), ()))
     total = lax.dot_general(left[0], right[0], over, preferred_element_type=f32)
     total += lax.dot_general(left[1], right[1], over, preferred_element_type=f32)
     out[...] = (total * (-1.0 / math.sqrt(STEPS * 512))).astype(out.dtype)
 
 
-def sums(elems, names, signs, partner):
+def sums(elems, cols, rows, dtype):
     vm = pl.BlockSpec(memory_space=pltpu.VMEM)
     return pl.pallas_call(
-        functools.partial(sums_kernel, partner),
-        out_shape=jax.ShapeDtypeStruct((SPAN // 2, SPAN), jnp.bfloat16 if partner else jnp.float32),
-        in_specs=[vm] * 4,
+        sums_kernel,
+        out_shape=jax.ShapeDtypeStruct((SPAN // 2, SPAN), dtype),
+        in_specs=[vm] * 5,
         out_specs=vm,
         cost_estimate=pl.CostEstimate(flops=10**9, bytes_accessed=2 * 2**20, transcendentals=0),
         compiler_params=pltpu.CompilerParams(vmem_limit_bytes=48 * 2**20),
-    )(elems, names, signs, jnp.asarray(layout()[3]))
+    )(elems, *cols, *rows)
 
 
 def body(valence, conduction, val_energy, cond_energy, owner, g_index):
-    psi, g_index = from_owners(valence, owner, g_index)
+    places, names, signs = frequencies(g_index)
+    psi, (places, *hot) = from_owners(valence, owner, (places, *spreads(names, signs)))
     cond = in_rows(conduction)
-    places, names, signs = frequencies(g_index)
     elems = pairs(psi, cond, owner, val_energy, cond_energy, places)
 
     elems = lax.all_gather(elems, "z", axis=0, tiled=True)
     elems = exchange(turn(elems), COL)
-    away = lax.ppermute(sums(elems, names, signs, True), "yl", SWAP)
-    return sums(elems, names, signs, False) + away.astype(jnp.float32)
+    away = lax.ppermute(sums(elems, hot[:2], hot[2:4], jnp.bfloat16), "yl", SWAP)
+    return sums(elems, hot[:2], hot[4:], jnp.float32) + away.astype(jnp.float32)
 
 
 def solution(mesh):

time: 158 us -> 158 us (level)
  local copies, waits for them, and re-layouts: 3.37 us -> 6.07 us
  waiting for transfers between devices: 27.5 us -> 24.9 us
    unnamed x28 -> x44, local copies, waits for them, and re-layouts: 1.46 us -> 4.27 us
    all_to_all x2, waiting for transfers between devices: 20.2 us -> 18 us  [exchange(): return lax.all_to_all(x, axis, split_axis=0, concat_axis=0, tiled=True)]
where the time goes in v9:
time: 158 us
  blocking collectives  85.1 us (54%)
  starting transfers between devices  26.8 us (17%)
  waiting for transfers between devices  24.9 us (16%)
  Pallas kernels  10.7 us (7%)
  local copies, waits for them, and re-layouts  6.07 us (4%)
  between operations  3.38 us (2%)
    all_to_all x1, blocking collectives, exchange(): return lax.all_to_all(x, axis, split_axis=0, concat_axis=0, tiled=True)  31.1 us
    all_gather x1, blocking collectives, from_owners(): lax.all_gather(jnp.concatenate(parts, axis=0), 'z', axis=0, tiled=True)  31.1 us
    all_gather x1, blocking collectives, body(): elems = lax.all_gather(elems, 'z', axis=0, tiled=True)  22.9 us
    all_to_all x2, waiting for transfers between devices, exchange(): return lax.all_to_all(x, axis, split_axis=0, concat_axis=0, tiled=True)  18 us
    all_to_all x2, starting transfers between devices, exchange(): return lax.all_to_all(x, axis, split_axis=0, concat_axis=0, tiled=True)  14.2 us
    ppermute x1, starting transfers between devices, from_owners(): return ((parts, lax.ppermute(parts, 'c', SWAP)), late)  10.4 us
    ppermute x1, waiting for transfers between devices, body(): lax.ppermute(sums(elems, hot[:2], hot[2:4], jnp.bfloat16), 'yl', SWAP)  5.91 us
    pallas_call x1, Pallas kernels, pairs(): pl.pallas_call(dft_kernel, out_shape=jax.ShapeDtypeStruct((ELEMS, LANES),...  5.28 us
  transfers between devices with their start and end apart: 4, of which 4 were waited for; matrix products, arithmetic and copies ran while one was open for 1% of the time, Pallas kernels for 1%

profile of v9, /device:TPU:1, one launch (start us, length us, event | category | flops | bytes accessed | tf_op | source)
XLA Modules:
  0.0 158.0 jit_solution(770442839380354059)
XLA Ops:
  0.0 1.4 copy-done
  1.4 1.2 shard_map.145
  2.6 10.4 %all-to-all-start = ((bf16[32,96,128]{2,1,0:T(8,128)(2,1)}), bf16[32,96,128]{2,1,0:T(8,128)(2,1)S(1)}, u32[]{:S(2)}, u32[]{:S(2)}) async-start(bf16[32,96,128]{2,1,0:T(8,128)(2,1)} %bitcast), calls=%async_computation | async-start | bytes 1572864 | tf_op jit(solution)/shard_map/all_to_all | solution.py:46
  13.0 0.6 fusion.10
  16.0 11.4 %all-to-all-done = bf16[32,96,128]{2,1,0:T(8,128)(2,1)S(1)} async-done(((bf16[32,96,128]{2,1,0:T(8,128)(2,1)}), bf16[32,96,128]{2,1,0:T(8,128)(2,1)S(1)}, u32[]{:S(2)}, u32[]{:S(2)}) %all-to-all-start) | async-done | bytes 786464 | tf_op jit(solution)/shard_map/all_to_all | solution.py:46
  27.5 31.1 %all_gather.6 = bf16[3072,128]{1,0:T(8,128)(2,1)S(1)} all-gather(bf16[192,128]{1,0:T(8,128)(2,1)S(1)} %pad_maximum_fusion), channel_id=1, replica_groups=mesh['z'=16,'yl'=2,'x'=4,'yh'=2,'c'=2] {'z'}, dimensions={0}, use_global_device_ids=true | all-gather | bytes 835584 | tf_op jit(solution)/shard_map/all_gather | solution.py:75
  58.7 1.0 broadcast_in_dim.6
  59.8 3.8 %all-to-all-start.1 = ((bf16[16,192,128]{2,1,0:T(8,128)(2,1)}), bf16[16,192,128]{2,1,0:T(8,128)(2,1)S(1)}, u32[]{:S(2)}, u32[]{:S(2)}) async-start(bf16[16,192,128]{2,1,0:T(8,128)(2,1)} %broadcast_in_dim.6), calls=%async_computation.1 | async-start | bytes 1572864 | tf_op jit(solution)/shard_map/all_to_all | solution.py:46
  64.4 0.7 copy-done.8
  65.1 0.7 copy-done.10
  65.8 0.7 copy-done.12
  66.5 0.7 copy-done.14
  67.2 6.6 %all-to-all-done.1.same = bf16[16,192,128]{2,1,0:T(8,128)(2,1)S(1)} async-done(((bf16[16,192,128]{2,1,0:T(8,128)(2,1)}), bf16[16,192,128]{2,1,0:T(8,128)(2,1)S(1)}, u32[]{:S(2)}, u32[]{:S(2)}) %all-to-all-start.1) | async-done | bytes 786464 | tf_op jit(solution)/shard_map/all_to_all | solution.py:46
  73.8 10.4 %collective-permute-start = (bf16[16,192,128]{2,1,0:T(8,128)(2,1)S(1)}, bf16[16,192,128]{2,1,0:T(8,128)(2,1)S(1)}, u32[]{:S(2)}, u32[]{:S(2)}) collective-permute-start(bf16[16,192,128]{2,1,0:T(8,128)(2,1)S(1)} %all-to-all-done.1.same), channel_id=1, source_target_pairs={{0,1},{1,0},{2,3},{3,2},{4,5},{5,4},{6,7},{7,6},{8,9},{9,8},{10,11... | collective-permute-start | bytes 2359304 | tf_op jit(solution)/shard_map/ppermute | solution.py:81
  85.2 0.9 collective-permute-done.other
  86.2 5.3 %shard_map.148 = bf16[160,128]{1,0:T(8,128)(2,1)S(1)} custom-call(s32[2]{0:T(128)S(1)} %copy-done.6, f32[512]{0:T(512)S(1)} %copy-done.7, f32[1]{0:T(128)S(6)} %copy.16.cond_energy, bf16[16,192,128]{2,1,0:T(8,128)(2,1)S(1)} %all-to-all-done.1.same, bf16[16,192,128]{2,1,0:T(8,128)(2,1)S(1)} %collective-permute-done.other, ...), custom_call_target="tpu_custom_call" | custom-call | tf_op jit(solution)/shard_map/pallas_call | solution.py:302
  91.5 22.9 %all_gather.7.gathered = bf16[2560,128]{1,0:T(8,128)(2,1)S(1)} all-gather(bf16[160,128]{1,0:T(8,128)(2,1)S(1)} %shard_map.148), channel_id=1, replica_groups=mesh['z'=16,'yl'=2,'x'=4,'yh'=2,'c'=2] {'z'}, dimensions={0}, use_global_device_ids=true | all-gather | bytes 696320 | tf_op jit(solution)/shard_map/all_gather | solution.py:387
  114.3 0.9 shard_map.149
  115.3 31.1 %all_to_all.15.elems = bf16[16,320,128]{2,1,0:T(8,128)(2,1)S(1)} all-to-all(bf16[16,320,128]{2,1,0:T(8,128)(2,1)S(1)} %shard_map.149), channel_id=1, replica_groups=mesh['z'=16,'yl'=2,'x'=4,'yh'=2,'c'=2] {'x','yh','c'}, dimensions={0} | all-to-all | bytes 2621440 | tf_op jit(solution)/shard_map/all_to_all | solution.py:46
  146.4 1.3 shard_map.151
  147.8 2.1 %collective-permute-start.1 = (bf16[256,512]{1,0:T(8,128)(2,1)S(1)}, bf16[256,512]{1,0:T(8,128)(2,1)S(1)}, u32[]{:S(2)}, u32[]{:S(2)}) collective-permute-start(bf16[256,512]{1,0:T(8,128)(2,1)S(1)} %shard_map.151), channel_id=1, source_target_pairs={{0,16},{16,0},{1,17},{17,1},{2,18},{18,2},{3,19},{19,3},{4,20},{20... | collective-permute-start | bytes 786440 | tf_op jit(solution)/shard_map/ppermute | solution.py:389
  149.9 1.3 shard_map.150
  151.2 5.9 %collective-permute-done.1 = bf16[256,512]{1,0:T(8,128)(2,1)S(1)} collective-permute-done((bf16[256,512]{1,0:T(8,128)(2,1)S(1)}, bf16[256,512]{1,0:T(8,128)(2,1)S(1)}, u32[]{:S(2)}, u32[]{:S(2)}) %collective-permute-start.1) | collective-permute-done | bytes 262176 | tf_op jit(solution)/shard_map/ppermute | solution.py:389
  157.1 0.9 convert_add_fusion
  (57 shorter events, 1.2 us)
Async XLA Ops:
  0.0 1.4 copy-start
  1.4 11.7 %copy-start.6 = (s32[2]{0:T(128)S(1)}, s32[2]{0:T(128)}, u32[]{:S(2)}) copy-start(s32[2]{0:T(128)} %owner.1) | copy-start | bytes 28
  1.4 14.6 %copy-start.16 = (s32[8192]{0:T(1024)S(1)}, s32[8192]{0:T(1024)}, u32[]{:S(2)}) copy-start(s32[8192]{0:T(1024)} %param.20) | copy-start | bytes 98308
  2.6 24.9 %all-to-all-start = ((bf16[32,96,128]{2,1,0:T(8,128)(2,1)}), bf16[32,96,128]{2,1,0:T(8,128)(2,1)S(1)}, u32[]{:S(2)}, u32[]{:S(2)}) async-start(bf16[32,96,128]{2,1,0:T(8,128)(2,1)} %bitcast), calls=%async_computation | async-start | bytes 1572864 | tf_op jit(solution)/shard_map/all_to_all | solution.py:46
  58.7 5.1 %copy-start.17 = (s32[16,512]{1,0:T(8,128)S(1)}, s32[16,512]{1,0:T(8,128)}, u32[]{:S(2)}) copy-start(s32[16,512]{1,0:T(8,128)} %constant.94.clone) | copy-start | bytes 98308
  58.7 5.1 %copy-start.19 = (pred[16,512]{1,0:T(8,128)(4,1)S(1)}, pred[16,512]{1,0:T(8,128)(4,1)}, u32[]{:S(2)}) copy-start(pred[16,512]{1,0:T(8,128)(4,1)} %constant.93.clone) | copy-start | bytes 24580
  58.7 5.3 %copy-start.2 = (f32[2,384,128]{2,1,0:T(8,128)S(1)}, f32[2,384,128]{2,1,0:T(8,128)}, u32[]{:S(2)}) copy-start(f32[2,384,128]{2,1,0:T(8,128)} %constant.95.clone.columns) | copy-start | bytes 1179652
  59.8 7.4 %copy-start.18 = (s32[16,384]{1,0:T(8,128)S(1)}, s32[16,384]{1,0:T(8,128)}, u32[]{:S(2)}) copy-start(s32[16,384]{1,0:T(8,128)} %constant.91.clone) | copy-start | bytes 73732
  59.8 7.4 %copy-start.20 = (pred[16,384]{1,0:T(8,128)(4,1)S(1)}, pred[16,384]{1,0:T(8,128)(4,1)}, u32[]{:S(2)}) copy-start(pred[16,384]{1,0:T(8,128)(4,1)} %constant.92.clone) | copy-start | bytes 18436
  59.8 7.4 %copy-start.21 = (pred[16,384]{1,0:T(8,128)(4,1)S(1)}, pred[16,384]{1,0:T(8,128)(4,1)}, u32[]{:S(2)}) copy-start(pred[16,384]{1,0:T(8,128)(4,1)} %constant.90.clone) | copy-start | bytes 18436
  59.8 25.1 %copy-start.1 = (bf16[1,373248]{1,0:T(2,128)(2,1)S(1)}, bf16[1,373248]{1,0:T(2,128)(2,1)}, u32[]{:S(2)}) copy-start(bf16[1,373248]{1,0:T(2,128)(2,1)} %flat.3) | copy-start | bytes 2239492
  59.8 14.0 %all-to-all-start.1 = ((bf16[16,192,128]{2,1,0:T(8,128)(2,1)}), bf16[16,192,128]{2,1,0:T(8,128)(2,1)S(1)}, u32[]{:S(2)}, u32[]{:S(2)}) async-start(bf16[16,192,128]{2,1,0:T(8,128)(2,1)} %broadcast_in_dim.6), calls=%async_computation.1 | async-start | bytes 1572864 | tf_op jit(solution)/shard_map/all_to_all | solution.py:46
  63.9 22.3 %copy-start.3 = (bf16[256,256]{1,0:T(8,128)(2,1)S(1)}, bf16[256,256]{1,0:T(8,128)(2,1)}, u32[]{:S(2)}) copy-start(bf16[256,256]{1,0:T(8,128)(2,1)} %constant.98.clone.third) | copy-start | bytes 393220
  63.9 22.3 %copy-start.4 = (bf16[64,216]{1,0:T(8,128)(2,1)S(1)}, bf16[64,216]{1,0:T(8,128)(2,1)}, u32[]{:S(2)}) copy-start(bf16[64,216]{1,0:T(8,128)(2,1)} %constant.97.clone.second) | copy-start | bytes 82948
  63.9 22.3 %copy-start.5 = (bf16[32,240]{1,0:T(8,128)(2,1)S(1)}, bf16[32,240]{1,0:T(8,128)(2,1)}, u32[]{:S(2)}) copy-start(bf16[32,240]{1,0:T(8,128)(2,1)} %constant.96.clone.first) | copy-start | bytes 46084
  63.9 22.3 %copy-start.7 = (f32[512]{0:T(512)S(1)}, f32[512]{0:T(512)}, u32[]{:S(2)}) copy-start(f32[512]{0:T(512)} %val_energy.1) | copy-start | bytes 6148
  64.4 0.7 copy-start.8
  65.1 0.7 copy-start.10
  73.8 12.3 %collective-permute-start = (bf16[16,192,128]{2,1,0:T(8,128)(2,1)S(1)}, bf16[16,192,128]{2,1,0:T(8,128)(2,1)S(1)}, u32[]{:S(2)}, u32[]{:S(2)}) collective-permute-start(bf16[16,192,128]{2,1,0:T(8,128)(2,1)S(1)} %all-to-all-done.1.same), channel_id=1, source_target_pairs={{0,1},{1,0},{2,3},{3,2},{4,5},{5,4},{6,7},{7,6},{8,9},{9,8},{10,11... | collective-permute-start | bytes 2359304 | tf_op jit(solution)/shard_map/ppermute | solution.py:81
  115.2 31.2 %copy-start.9 = (bf16[384,512]{1,0:T(8,128)(2,1)S(1)}, bf16[384,512]{1,0:T(8,128)(2,1)}, u32[]{:S(2)}) copy-start(bf16[384,512]{1,0:T(8,128)(2,1)} %copy-done.8) | copy-start | bytes 1179652
  115.2 31.2 %copy-start.13 = (bf16[384,256]{1,0:T(8,128)(2,1)S(1)}, bf16[384,256]{1,0:T(8,128)(2,1)}, u32[]{:S(2)}) copy-start(bf16[384,256]{1,0:T(8,128)(2,1)} %copy-done.12) | copy-start | bytes 589828
  115.2 31.2 %copy-start.15 = (bf16[384,256]{1,0:T(8,128)(2,1)S(1)}, bf16[384,256]{1,0:T(8,128)(2,1)}, u32[]{:S(2)}) copy-start(bf16[384,256]{1,0:T(8,128)(2,1)} %copy-done.14) | copy-start | bytes 589828
  146.4 3.5 %copy-start.11 = (bf16[384,256]{1,0:T(8,128)(2,1)S(1)}, bf16[384,256]{1,0:T(8,128)(2,1)}, u32[]{:S(2)}) copy-start(bf16[384,256]{1,0:T(8,128)(2,1)} %copy-done.10) | copy-start | bytes 589828
  147.8 9.4 %collective-permute-start.1 = (bf16[256,512]{1,0:T(8,128)(2,1)S(1)}, bf16[256,512]{1,0:T(8,128)(2,1)S(1)}, u32[]{:S(2)}, u32[]{:S(2)}) collective-permute-start(bf16[256,512]{1,0:T(8,128)(2,1)S(1)} %shard_map.151), channel_id=1, source_target_pairs={{0,16},{16,0},{1,17},{17,1},{2,18},{18,2},{3,19},{19,3},{4,20},{20... | collective-permute-start | bytes 786440 | tf_op jit(solution)/shard_map/ppermute | solution.py:389
  (2 other events, 1.4 us)
